TPU v7x, 32 devices: a whole 2x2x4 slice. The times are simulated.
32 devices in a mesh: ctx: 8 (over z, y), fsdp: 4 (over x, core).
Axes of the slice: x: 2, y: 2, z: 4, core: 2. Of those that a mesh axis runs over, the one named last changes fastest.
Arguments:
- tokens: bfloat16 [4096, 1536], P(('ctx', 'fsdp')), may hold values from -6 to 6
- lengths: int32 [4], replicated, may hold values from 1 to 3840, 4096 in all
- wq: bfloat16 [1536, 1536], P('fsdp'), may hold values from -0.15625 to 0.15625
- wk: bfloat16 [1536, 512], P('fsdp'), may hold values from -0.15625 to 0.15625
- wv: bfloat16 [1536, 512], P('fsdp'), may hold values from -0.15625 to 0.15625
- wo: bfloat16 [1536, 1536], P('fsdp'), may hold values from -1.25 to 1.25
- w_gate: bfloat16 [1536, 6912], P('fsdp'), may hold values from -0.15625 to 0.15625
- w_up: bfloat16 [1536, 6912], P('fsdp'), may hold values from -0.15625 to 0.15625
- w_down: bfloat16 [6912, 1536], P('fsdp'), may hold values from -0.078125 to 0.078125
- attn_gain: bfloat16 [1536], P('fsdp'), may hold values from 0.099609375 to 1.8984375
- ffn_gain: bfloat16 [1536], P('fsdp'), may hold values from 0.099609375 to 1.8984375
- q_gain: bfloat16 [64], P('fsdp'), may hold values from 0.099609375 to 1.8984375
- key_norm_gain: bfloat16 [64], P('fsdp'), may hold values from 0.099609375 to 1.8984375
- cotangent: bfloat16 [4096, 1536], P(('ctx', 'fsdp')), may hold values from -6 to 6
Outputs:
- layer_out: bfloat16 [4096, 1536], P(('ctx', 'fsdp'))
- tokens_grad: bfloat16 [4096, 1536], P(('ctx', 'fsdp'))
- wq_grad: float32 [1536, 1536], P('fsdp')
- wk_grad: float32 [1536, 512], P('fsdp')
- wv_grad: float32 [1536, 512], P('fsdp')
- wo_grad: float32 [1536, 1536], P('fsdp')
- gate_grad: float32 [1536, 6912], P('fsdp')
- up_grad: float32 [1536, 6912], P('fsdp')
- down_grad: float32 [6912, 1536], P('fsdp')
- attn_gain_grad: float32 [1536], P('fsdp')
- ffn_gain_grad: float32 [1536], P('fsdp')
- q_gain_grad: float32 [64], P('fsdp')
- k_gain_grad: float32 [64], P('fsdp')
Inputs may be any that keep to these rules, and one draw needn't show every extreme that they name: The lengths sum to 4096; the largest is exactly min(8192, 3840).
All inputs are finite; a program needn't handle non-finite values.
Results may differ from a plain program's by a relative error of at most 0.024.
Values may be sent and summed in bfloat16 or wider, within the bound.
A program may use at most 704 MiB of HBM per device.

v0:
```python
import jax
import jax.numpy as jnp
from jax import lax
from jax.sharding import PartitionSpec as P

QUERY_HEADS = 24
KEY_VALUE_HEADS = 8
HEAD_SIZE = 64


EPSILON = 1e-05
ROPE_BASE = 1000000.0
MASKED_SCORE = -1e30


def passed_along(block, axis, distance):
    devices = range(lax.axis_size(axis))
    route = [((i - distance) % len(devices), i) for i in devices]
    return lax.ppermute(block, axis, route)


def passed_along_2(array, axis, by):
    size = lax.axis_size(axis)
    pairs = [(i, i + by) for i in range(size) if 0 <= i + by < size]
    return lax.ppermute(array, axis, pairs)


def doc_layout(lengths, token_index):
    doc_ends = jnp.cumsum(lengths)
    passed = token_index[:, None] >= doc_ends[None, :]
    document_index = jnp.sum(passed.astype(jnp.int32), axis=1)
    doc_start = jnp.max(jnp.where(passed, doc_ends[None, :], 0), axis=1)
    return (document_index, token_index - doc_start)


def rotation(places, width):
    half_width = width // 2
    inverse_freq = jnp.power(ROPE_BASE, -(jnp.arange(half_width, dtype=jnp.float32) * 2.0 / width))
    angles = places.astype(jnp.float32)[:, None] * inverse_freq[None, :]
    cosine_values = jnp.cos(angles)
    sine_lookup = jnp.sin(angles)
    return (
        jnp.concatenate([cosine_values, cosine_values], 1),
        jnp.concatenate([sine_lookup, sine_lookup], 1),
    )


def apply_rotary(values_in, cosine_values, sine_lookup, sign):
    half_width = values_in.shape[-1] // 2
    swapped = jnp.concatenate([-values_in[..., half_width:], values_in[..., :half_width]], -1)
    return values_in * cosine_values + swapped * (sine_lookup * sign)


def scaled_input(values_in):
    factor = lax.rsqrt(jnp.mean(values_in * values_in, -1, keepdims=True) + EPSILON)
    return (values_in * factor, factor)


def norm_back(upstream, unit_rows, factor, gain_row):
    lifted = upstream * gain_row
    return factor * (lifted - unit_rows * jnp.mean(lifted * unit_rows, -1, keepdims=True))


def on_device(
    tokens,
    lengths,
    wq,
    wk,
    wv,
    wo,
    w_gate,
    w_up,
    w_down,
    attn_gain,
    ffn_gain,
    q_gain,
    key_norm_gain,
    cotangent,
):
    token_rows = tokens.shape[0]
    cycle_size = lax.axis_size("ctx")
    lane_size = lax.axis_size("fsdp")
    rows_per_block = token_rows * lane_size
    ctx_place = lax.axis_index("ctx")
    row_base = (ctx_place * lane_size + lax.axis_index("fsdp")) * token_rows
    query_index = row_base + jnp.arange(token_rows, dtype=jnp.int32)
    query_doc, query_place = doc_layout(lengths, query_index)
    cosine_values, sine_lookup = rotation(query_place, HEAD_SIZE)
    cosine_values = cosine_values[:, None, :]
    sine_lookup = sine_lookup[:, None, :]
    query_group_width = QUERY_HEADS // KEY_VALUE_HEADS
    score_scale = HEAD_SIZE ** (-0.5)
    key_value_width = KEY_VALUE_HEADS * HEAD_SIZE
    full_q, full_k, full_v, full_o, gain_attn, gain_query, gain_key = (
        lax.all_gather(wq, "fsdp", axis=0, tiled=True),
        lax.all_gather(wk, "fsdp", axis=0, tiled=True),
        lax.all_gather(wv, "fsdp", axis=0, tiled=True),
        lax.all_gather(wo, "fsdp", axis=0, tiled=True),
        lax.all_gather(attn_gain, "fsdp", axis=0, tiled=True),
        lax.all_gather(q_gain, "fsdp", axis=0, tiled=True),
        lax.all_gather(key_norm_gain, "fsdp", axis=0, tiled=True),
    )
    inputs = tokens.astype(jnp.float32)
    unit_attn, factor_attn = scaled_input(inputs)
    normed = (unit_attn * gain_attn.astype(jnp.float32)).astype(jnp.bfloat16)
    q_proj = jnp.dot(normed, full_q, preferred_element_type=jnp.float32)
    key_projected = jnp.dot(normed, full_k, preferred_element_type=jnp.float32)
    value_projected = jnp.dot(normed, full_v, preferred_element_type=jnp.float32)
    q_unit, q_factor = scaled_input(q_proj.reshape(token_rows, QUERY_HEADS, HEAD_SIZE))
    key_normalized, key_norm_factor = scaled_input(
        key_projected.reshape(token_rows, KEY_VALUE_HEADS, HEAD_SIZE)
    )
    query_matrix = (
        apply_rotary(q_unit * gain_query.astype(jnp.float32), cosine_values, sine_lookup, 1.0)
        .astype(jnp.bfloat16)
        .reshape(token_rows, KEY_VALUE_HEADS, query_group_width, HEAD_SIZE)
    )
    own_keys = (
        apply_rotary(key_normalized * gain_key.astype(jnp.float32), cosine_values, sine_lookup, 1.0)
        .astype(jnp.bfloat16)
        .reshape(token_rows, key_value_width)
    )
    own_values = value_projected.astype(jnp.bfloat16)

    def piece_mask(first_row, slice_rows):
        key_index = first_row + jnp.arange(slice_rows, dtype=jnp.int32)
        key_doc, unused_place = doc_layout(lengths, key_index)
        return (key_index[None, :] <= query_index[:, None]) & (
            key_doc[None, :] == query_doc[:, None]
        )

    start_state = (
        jnp.full((KEY_VALUE_HEADS, query_group_width, token_rows), MASKED_SCORE, jnp.float32),
        jnp.zeros((KEY_VALUE_HEADS, query_group_width, token_rows), jnp.float32),
        jnp.zeros((KEY_VALUE_HEADS, query_group_width, token_rows, HEAD_SIZE), jnp.float32),
    )
    cycle_keys, cycle_values = (
        lax.all_gather(own_keys, "fsdp", axis=0, tiled=True),
        lax.all_gather(own_values, "fsdp", axis=0, tiled=True),
    )
    first_row = jnp.int32(0)
    key_block_slice = lax.all_gather(cycle_keys, "ctx", axis=0, tiled=True)
    value_block_slice = lax.all_gather(cycle_values, "ctx", axis=0, tiled=True)
    slice_rows = key_block_slice.shape[0]

    def visit(current):
        running_max, running_sum, running_out = current
        allowed = piece_mask(first_row, slice_rows)
        heads_of_keys = key_block_slice.reshape(slice_rows, KEY_VALUE_HEADS, HEAD_SIZE)
        heads_of_values = value_block_slice.reshape(slice_rows, KEY_VALUE_HEADS, HEAD_SIZE)
        scores = (
            jnp.einsum(
                "tkgd,skd->kgts", query_matrix, heads_of_keys, preferred_element_type=jnp.float32
            )
            * score_scale
        )
        scores = jnp.where(allowed, scores, MASKED_SCORE)
        new_max = jnp.maximum(running_max, jnp.max(scores, -1))
        weights = jnp.where(allowed, jnp.exp(scores - new_max[..., None]), 0.0)
        running_sum = jnp.sum(weights, -1)
        running_out = jnp.einsum(
            "kgts,skd->kgtd",
            weights.astype(jnp.bfloat16),
            heads_of_values,
            preferred_element_type=jnp.float32,
        )
        return (new_max, running_sum, running_out)

    running_max, running_sum, running_out = lax.cond(
        first_row <= query_index[-1], visit, lambda unchanged: unchanged, start_state
    )
    log_total = running_max + jnp.log(running_sum)
    mixed_head_rows = jnp.transpose(running_out / running_sum[..., None], (2, 0, 1, 3)).reshape(
        token_rows, QUERY_HEADS * HEAD_SIZE
    )
    mixed_heads = mixed_head_rows.astype(jnp.bfloat16)
    resid = inputs + jnp.dot(mixed_heads, full_o, preferred_element_type=jnp.float32)
    full_gate, full_up, full_down, gain_ffn = (
        lax.all_gather(w_gate, "fsdp", axis=0, tiled=True),
        lax.all_gather(w_up, "fsdp", axis=0, tiled=True),
        lax.all_gather(w_down, "fsdp", axis=0, tiled=True),
        lax.all_gather(ffn_gain, "fsdp", axis=0, tiled=True),
    )
    unit_ffn, factor_ffn = scaled_input(resid)
    hidden_in = (unit_ffn * gain_ffn.astype(jnp.float32)).astype(jnp.bfloat16)
    gate = jnp.dot(hidden_in, full_gate, preferred_element_type=jnp.float32)
    upper = jnp.dot(hidden_in, full_up, preferred_element_type=jnp.float32)
    sigma = jax.nn.sigmoid(gate)
    silu_gate = gate * sigma
    act_rows = (silu_gate * upper).astype(jnp.bfloat16)
    layer_out = (resid + jnp.dot(act_rows, full_down, preferred_element_type=jnp.float32)).astype(
        jnp.bfloat16
    )
    full_gate, full_up, full_down, gain_ffn = (
        lax.all_gather(w_gate, "fsdp", axis=0, tiled=True),
        lax.all_gather(w_up, "fsdp", axis=0, tiled=True),
        lax.all_gather(w_down, "fsdp", axis=0, tiled=True),
        lax.all_gather(ffn_gain, "fsdp", axis=0, tiled=True),
    )
    full_q, full_k, full_v, full_o, gain_attn, gain_query, gain_key = (
        lax.all_gather(wq, "fsdp", axis=0, tiled=True),
        lax.all_gather(wk, "fsdp", axis=0, tiled=True),
        lax.all_gather(wv, "fsdp", axis=0, tiled=True),
        lax.all_gather(wo, "fsdp", axis=0, tiled=True),
        lax.all_gather(attn_gain, "fsdp", axis=0, tiled=True),
        lax.all_gather(q_gain, "fsdp", axis=0, tiled=True),
        lax.all_gather(key_norm_gain, "fsdp", axis=0, tiled=True),
    )
    grad_out = cotangent.astype(jnp.float32)
    down_term = jnp.einsum("tf,td->fd", act_rows, cotangent, preferred_element_type=jnp.float32)
    grad_act = jnp.einsum("td,fd->tf", cotangent, full_down, preferred_element_type=jnp.float32)
    grad_gate = (grad_act * upper * sigma * (1.0 + gate * (1.0 - sigma))).astype(jnp.bfloat16)
    grad_upper = (grad_act * silu_gate).astype(jnp.bfloat16)
    gate_term = jnp.einsum("td,tf->df", hidden_in, grad_gate, preferred_element_type=jnp.float32)
    up_term = jnp.einsum("td,tf->df", hidden_in, grad_upper, preferred_element_type=jnp.float32)
    grad_hidden = jnp.einsum(
        "tf,df->td", grad_gate, full_gate, preferred_element_type=jnp.float32
    ) + jnp.einsum("tf,df->td", grad_upper, full_up, preferred_element_type=jnp.float32)
    ffn_gain_term = jnp.sum(grad_hidden * unit_ffn, 0)
    gate_part, upper_part, down_part, ffn_gain_part = (
        lax.psum_scatter(
            gate_term.astype(jnp.bfloat16), "fsdp", scatter_dimension=0, tiled=True
        ).astype(jnp.float32),
        lax.psum_scatter(
            up_term.astype(jnp.bfloat16), "fsdp", scatter_dimension=0, tiled=True
        ).astype(jnp.float32),
        lax.psum_scatter(
            down_term.astype(jnp.bfloat16), "fsdp", scatter_dimension=0, tiled=True
        ).astype(jnp.float32),
        lax.psum_scatter(
            ffn_gain_term.astype(jnp.bfloat16), "fsdp", scatter_dimension=0, tiled=True
        ).astype(jnp.float32),
    )
    grad_resid = grad_out + norm_back(
        grad_hidden, unit_ffn, factor_ffn, gain_ffn.astype(jnp.float32)
    )
    grad_attn = grad_resid.astype(jnp.bfloat16)
    wo_term = jnp.einsum("tc,td->cd", mixed_heads, grad_attn, preferred_element_type=jnp.float32)
    mixed_gradient = jnp.einsum(
        "td,cd->tc", grad_attn, full_o, preferred_element_type=jnp.float32
    ).astype(jnp.bfloat16)
    heads_gradient = mixed_gradient.reshape(
        token_rows, KEY_VALUE_HEADS, query_group_width, HEAD_SIZE
    )
    row_delta = jnp.einsum(
        "tkgd,tkgd->kgt",
        heads_gradient.astype(jnp.float32),
        mixed_head_rows.reshape(token_rows, KEY_VALUE_HEADS, query_group_width, HEAD_SIZE),
    )

    def contribute(key_rotation_pair, first_row):
        allowed = piece_mask(first_row, rows_per_block)
        heads_of_keys = key_rotation_pair[0].reshape(rows_per_block, KEY_VALUE_HEADS, HEAD_SIZE)
        heads_of_values = key_rotation_pair[1].reshape(rows_per_block, KEY_VALUE_HEADS, HEAD_SIZE)
        scores = (
            jnp.einsum(
                "tkgd,skd->kgts", query_matrix, heads_of_keys, preferred_element_type=jnp.float32
            )
            * score_scale
        )
        probs = jnp.where(allowed, jnp.exp(scores - log_total[..., None]), 0.0)
        value_grad = jnp.einsum(
            "kgts,tkgd->skd",
            probs.astype(jnp.bfloat16),
            heads_gradient,
            preferred_element_type=jnp.float32,
        )
        prob_grad = jnp.einsum(
            "tkgd,skd->kgts", heads_gradient, heads_of_values, preferred_element_type=jnp.float32
        )
        score_grad = (probs * (prob_grad - row_delta[..., None])).astype(jnp.bfloat16)
        query_grad = (
            jnp.einsum(
                "kgts,skd->tkgd", score_grad, heads_of_keys, preferred_element_type=jnp.float32
            )
            * score_scale
        )
        key_grad = (
            jnp.einsum(
                "kgts,tkgd->skd", score_grad, query_matrix, preferred_element_type=jnp.float32
            )
            * score_scale
        )
        return (
            query_grad,
            jnp.stack(
                [
                    key_grad.reshape(rows_per_block, key_value_width),
                    value_grad.reshape(rows_per_block, key_value_width),
                ]
            ),
        )

    def cycle_step(rounds, carried):
        key_rotation_pair, grad_pair, query_acc = carried
        source = (ctx_place - rounds) % cycle_size

        def accumulate(current):
            query_grad, pair_grad = contribute(key_rotation_pair, source * rows_per_block)
            return (current[0] + pair_grad, current[1] + query_grad)

        grad_pair, query_acc = lax.cond(
            source <= ctx_place, accumulate, lambda unchanged: unchanged, (grad_pair, query_acc)
        )
        grad_pair = passed_along(grad_pair.astype(jnp.bfloat16), "ctx", 1).astype(grad_pair.dtype)
        key_rotation_pair = passed_along_2(key_rotation_pair, "ctx", 1)
        return (key_rotation_pair, grad_pair, query_acc)

    cycle_state = (
        jnp.stack([cycle_keys, cycle_values]),
        jnp.zeros((2, rows_per_block, key_value_width), jnp.float32),
        jnp.zeros((token_rows, KEY_VALUE_HEADS, query_group_width, HEAD_SIZE), jnp.float32),
    )
    unused_pair, grad_pair, query_acc = lax.fori_loop(0, cycle_size, cycle_step, cycle_state)
    local_gradients = lax.psum_scatter(
        grad_pair.astype(jnp.bfloat16), "fsdp", scatter_dimension=1, tiled=True
    ).astype(jnp.float32)
    query_turned = apply_rotary(
        query_acc.reshape(token_rows, QUERY_HEADS, HEAD_SIZE), cosine_values, sine_lookup, -1.0
    )
    key_rotated = apply_rotary(
        local_gradients[0].reshape(token_rows, KEY_VALUE_HEADS, HEAD_SIZE),
        cosine_values,
        sine_lookup,
        -1.0,
    )
    q_gain_term = jnp.sum(query_turned * q_unit, (0, 1))
    k_gain_term = jnp.sum(key_rotated * key_normalized, (0, 1))
    grad_qp = (
        norm_back(query_turned, q_unit, q_factor, gain_query.astype(jnp.float32))
        .reshape(token_rows, QUERY_HEADS * HEAD_SIZE)
        .astype(jnp.bfloat16)
    )
    grad_kp = (
        norm_back(key_rotated, key_normalized, key_norm_factor, gain_key.astype(jnp.float32))
        .reshape(token_rows, key_value_width)
        .astype(jnp.bfloat16)
    )
    grad_vp = local_gradients[1].astype(jnp.bfloat16)
    wq_term = jnp.einsum("tc,tq->cq", normed, grad_qp, preferred_element_type=jnp.float32)
    wk_term = jnp.einsum("tc,tq->cq", normed, grad_kp, preferred_element_type=jnp.float32)
    wv_term = jnp.einsum("tc,tq->cq", normed, grad_vp, preferred_element_type=jnp.float32)
    grad_normed = jnp.einsum("tq,cq->tc", grad_qp, full_q, preferred_element_type=jnp.float32)
    grad_normed = grad_normed + jnp.einsum(
        "tq,cq->tc", grad_kp, full_k, preferred_element_type=jnp.float32
    )
    grad_normed = grad_normed + jnp.einsum(
        "tq,cq->tc", grad_vp, full_v, preferred_element_type=jnp.float32
    )
    attn_gain_term = jnp.sum(grad_normed * unit_attn, 0)
    tokens_grad = (
        grad_resid + norm_back(grad_normed, unit_attn, factor_attn, gain_attn.astype(jnp.float32))
    ).astype(jnp.bfloat16)
    wq_part, wk_part, wv_part, wo_part, attn_gain_part, q_gain_part, k_gain_part = (
        lax.psum_scatter(
            wq_term.astype(jnp.bfloat16), "fsdp", scatter_dimension=0, tiled=True
        ).astype(jnp.float32),
        lax.psum_scatter(
            wk_term.astype(jnp.bfloat16), "fsdp", scatter_dimension=0, tiled=True
        ).astype(jnp.float32),
        lax.psum_scatter(
            wv_term.astype(jnp.bfloat16), "fsdp", scatter_dimension=0, tiled=True
        ).astype(jnp.float32),
        lax.psum_scatter(
            wo_term.astype(jnp.bfloat16), "fsdp", scatter_dimension=0, tiled=True
        ).astype(jnp.float32),
        lax.psum_scatter(
            attn_gain_term.astype(jnp.bfloat16), "fsdp", scatter_dimension=0, tiled=True
        ).astype(jnp.float32),
        lax.psum_scatter(
            q_gain_term.astype(jnp.bfloat16), "fsdp", scatter_dimension=0, tiled=True
        ).astype(jnp.float32),
        lax.psum_scatter(
            k_gain_term.astype(jnp.bfloat16), "fsdp", scatter_dimension=0, tiled=True
        ).astype(jnp.float32),
    )
    summed = (
        lax.psum(wq_part.astype(jnp.bfloat16), "ctx").astype(jnp.float32),
        lax.psum(wk_part.astype(jnp.bfloat16), "ctx").astype(jnp.float32),
        lax.psum(wv_part.astype(jnp.bfloat16), "ctx").astype(jnp.float32),
        lax.psum(wo_part.astype(jnp.bfloat16), "ctx").astype(jnp.float32),
        lax.psum(gate_part.astype(jnp.bfloat16), "ctx").astype(jnp.float32),
        lax.psum(upper_part.astype(jnp.bfloat16), "ctx").astype(jnp.float32),
        lax.psum(down_part.astype(jnp.bfloat16), "ctx").astype(jnp.float32),
        lax.psum(attn_gain_part.astype(jnp.bfloat16), "ctx").astype(jnp.float32),
        lax.psum(ffn_gain_part.astype(jnp.bfloat16), "ctx").astype(jnp.float32),
        lax.psum(q_gain_part.astype(jnp.bfloat16), "ctx").astype(jnp.float32),
        lax.psum(k_gain_part.astype(jnp.bfloat16), "ctx").astype(jnp.float32),
    )
    return (
        layer_out,
        tokens_grad,
        summed[0],
        summed[1],
        summed[2],
        summed[3],
        summed[4],
        summed[5],
        summed[6],
        summed[7],
        summed[8],
        summed[9],
        summed[10],
    )


def solution(mesh):
    return jax.shard_map(
        on_device,
        mesh=mesh,
        in_specs=(
            P(("ctx", "fsdp"), None),
            P(),
            P("fsdp", None),
            P("fsdp", None),
            P("fsdp", None),
            P("fsdp", None),
            P("fsdp", None),
            P("fsdp", None),
            P("fsdp", None),
            P("fsdp"),
            P("fsdp"),
            P("fsdp"),
            P("fsdp"),
            P(("ctx", "fsdp"), None),
        ),
        out_specs=(
            P(("ctx", "fsdp"), None),
            P(("ctx", "fsdp"), None),
            P("fsdp", None),
            P("fsdp", None),
            P("fsdp", None),
            P("fsdp", None),
            P("fsdp", None),
            P("fsdp", None),
            P("fsdp", None),
            P("fsdp"),
            P("fsdp"),
            P("fsdp"),
            P("fsdp"),
        ),
        check_vma=False,
    )
```

profile of v0, /device:TPU:0, one launch (start us, length us, event | category | flops | bytes accessed | tf_op | source)
XLA Modules:
  0.0 2549.3 jit_solution(3156485346100730891)
XLA Ops:
  73.5 19.0 all-gather.16.cloned.1.call-done
  97.3 70.5 %all-gather.14.cloned.1.call-done = bf16[4096,512]{1,0:T(8,128)(2,1)} async-done(((bf16[512,512]{1,0:T(8,128)(2,1)}), bf16[4096,512]{1,0:T(8,128)(2,1)}) %all-gather.14.cloned.1.call-update) | async-done | bytes 4194320 | tf_op jit(solution)/shard_map/all_gather | solution.py:142
  167.9 73.7 %all-gather.20.cloned.1.call-done = bf16[4096,512]{1,0:T(8,128)(2,1)} async-done(((bf16[512,512]{1,0:T(8,128)(2,1)}), bf16[4096,512]{1,0:T(8,128)(2,1)}) %all-gather.20.cloned.1.call-update) | async-done | bytes 4194320 | tf_op jit(solution)/shard_map/all_gather | solution.py:143
  241.6 85.3 %conditional.2 = (f32[8,3,128]{2,1,0:T(4,128)}, f32[8,3,128]{2,1,0:T(4,128)}, f32[8,3,128,64]{2,3,1,0:T(8,128)}, f32[8,3,128]{2,1,0:T(4,128)S(1)}) conditional(s32[]{:T(128)} %bitcast.32, () %tuple.47, (s32[128]{0:T(128)S(1)}, s32[4]{0:T(128)S(1)}, s32[128]{0:T(128)S(1)}, bf16[4096,512]{1,0:T(8,128)(2,1)}, bf16[128,8,3,64]{0,3,2,1:T(8,128)(2,1)}, ...), branch_computations={%region_6.7_spmd, %region_7.12_spmd} | conditional | flops 3386418176 | bytes 179569744 | solution.py:169
  250.4 21.6 fusion.2
  272.6 24.0 fusion.4
  303.9 22.8 fusion.5
  332.4 81.0 %all-gather.24.cloned.1.call-done = bf16[1536,6912]{1,0:T(8,128)(2,1)} async-done(((bf16[384,6912]{1,0:T(8,128)(2,1)}), bf16[1536,6912]{1,0:T(8,128)(2,1)}) %all-gather.24.cloned.1.call-update) | async-done | bytes 21233680 | tf_op jit(solution)/shard_map/all_gather | solution.py:179
  425.5 122.5 %all-gather.26.cloned.1.call-done = bf16[1536,6912]{1,0:T(8,128)(2,1)} async-done(((bf16[384,6912]{1,0:T(8,128)(2,1)}), bf16[1536,6912]{1,0:T(8,128)(2,1)}) %all-gather.26.cloned.1.call-update) | async-done | bytes 21233680 | tf_op jit(solution)/shard_map/all_gather | solution.py:180
  560.2 122.5 %all-gather.28.cloned.1.call-done = bf16[6912,1536]{1,0:T(8,128)(2,1)} async-done(((bf16[1728,1536]{1,0:T(8,128)(2,1)}), bf16[6912,1536]{1,0:T(8,128)(2,1)}) %all-gather.28.cloned.1.call-update) | async-done | bytes 21233680 | tf_op jit(solution)/shard_map/all_gather | solution.py:181
  726.4 521.2 %while.20 = (s32[]{:T(128)}, bf16[2,512,512]{1,2,0:T(8,128)(2,1)S(1)}, f32[2,512,512]{1,2,0:T(8,128)}, f32[128,8,3,64]{0,3,2,1:T(8,128)S(1)}, s32[]{:T(128)}, /*...) while((s32[]{:T(128)}, ...), condition=%wide.region_19.20_spmd.clone, body=%wide.region_14.0_spmd.clone.sunk | while | flops 1025841280 | bytes 89900128 | solution.py:314
  728.1 18.2 conditional.5
  752.3 23.3 collective-permute-done.1
  798.5 20.6 collective-permute-start.1
  823.4 21.4 collective-permute-done.1
  870.2 23.4 collective-permute-start
  893.6 19.6 collective-permute-done.1
  918.8 20.7 collective-permute-start.1
  944.7 36.8 %collective-permute-done.1 = bf16[2,512,512]{1,2,0:T(8,128)(2,1)S(1)} collective-permute-done((bf16[2,512,512]{1,2,0:T(8,128)(2,1)}, bf16[2,512,512]{1,2,0:T(8,128)(2,1)S(1)}, u32[]{:S(2)}, u32[]{:S(2)}) %collective-permute-start.1) | collective-permute-done | bytes 1048608 | tf_op jit(solution)/shard_map/while/body/eval_jaxpr/ppermute | solution.py:19
  989.7 19.8 collective-permute-start
  1009.5 39.5 %collective-permute-done.1 = bf16[2,512,512]{1,2,0:T(8,128)(2,1)S(1)} collective-permute-done((bf16[2,512,512]{1,2,0:T(8,128)(2,1)}, bf16[2,512,512]{1,2,0:T(8,128)(2,1)S(1)}, u32[]{:S(2)}, u32[]{:S(2)}) %collective-permute-start.1) | collective-permute-done | bytes 1048608 | tf_op jit(solution)/shard_map/while/body/eval_jaxpr/ppermute | solution.py:19
  1059.4 56.2 %collective-permute-done.1 = bf16[2,512,512]{1,2,0:T(8,128)(2,1)S(1)} collective-permute-done((bf16[2,512,512]{1,2,0:T(8,128)(2,1)}, bf16[2,512,512]{1,2,0:T(8,128)(2,1)S(1)}, u32[]{:S(2)}, u32[]{:S(2)}) %collective-permute-start.1) | collective-permute-done | bytes 1048608 | tf_op jit(solution)/shard_map/while/body/eval_jaxpr/ppermute | solution.py:19
  1125.3 55.9 %collective-permute-done.1 = bf16[2,512,512]{1,2,0:T(8,128)(2,1)S(1)} collective-permute-done((bf16[2,512,512]{1,2,0:T(8,128)(2,1)}, bf16[2,512,512]{1,2,0:T(8,128)(2,1)S(1)}, u32[]{:S(2)}, u32[]{:S(2)}) %collective-permute-start.1) | collective-permute-done | bytes 1048608 | tf_op jit(solution)/shard_map/while/body/eval_jaxpr/ppermute | solution.py:19
  1188.1 57.8 %collective-permute-done.1 = bf16[2,512,512]{1,2,0:T(8,128)(2,1)S(1)} collective-permute-done((bf16[2,512,512]{1,2,0:T(8,128)(2,1)}, bf16[2,512,512]{1,2,0:T(8,128)(2,1)S(1)}, u32[]{:S(2)}, u32[]{:S(2)}) %collective-permute-start.1) | collective-permute-done | bytes 1048608 | tf_op jit(solution)/shard_map/while/body/eval_jaxpr/ppermute | solution.py:19
  1250.3 43.4 %reduce-scatter.9.cloned.1.call-done = bf16[2,128,512]{2,1,0:T(8,128)(2,1)} async-done(((bf16[2,512,512]{2,1,0:T(8,128)(2,1)}), bf16[2,128,512]{2,1,0:T(8,128)(2,1)}) %reduce-scatter.9.cloned.1.call-update) | async-done | bytes 262160 | tf_op jit(solution)/shard_map/reduce_scatter | solution.py:315
  1357.3 51.2 %reduce-scatter.11.cloned.1.call-done = bf16[384,1536]{1,0:T(8,128)(2,1)} async-done(((bf16[1536,1536]{1,0:T(8,128)(2,1)}), bf16[384,1536]{1,0:T(8,128)(2,1)}) %reduce-scatter.11.cloned.1.call-update) | async-done | bytes 1179664 | tf_op jit(solution)/shard_map/reduce_scatter | solution.py:355
  1408.4 50.8 %reduce-scatter.17.cloned.1.call-done = bf16[384,1536]{1,0:T(8,128)(2,1)} async-done(((bf16[1536,1536]{1,0:T(8,128)(2,1)}), bf16[384,1536]{1,0:T(8,128)(2,1)}) %reduce-scatter.17.cloned.1.call-update) | async-done | bytes 1179664 | tf_op jit(solution)/shard_map/reduce_scatter | solution.py:364
  1459.3 157.5 %reduce-scatter.19.cloned.1.call-done = bf16[384,6912]{1,0:T(8,128)(2,1)} async-done(((bf16[1536,6912]{1,0:T(8,128)(2,1)}), bf16[384,6912]{1,0:T(8,128)(2,1)}) %reduce-scatter.19.cloned.1.call-update) | async-done | bytes 5308432 | tf_op jit(solution)/shard_map/reduce_scatter | solution.py:221
  1616.7 157.3 %reduce-scatter.21.cloned.1.call-done = bf16[384,6912]{1,0:T(8,128)(2,1)} async-done(((bf16[1536,6912]{1,0:T(8,128)(2,1)}), bf16[384,6912]{1,0:T(8,128)(2,1)}) %reduce-scatter.21.cloned.1.call-update) | async-done | bytes 5308432 | tf_op jit(solution)/shard_map/reduce_scatter | solution.py:224
  1774.0 157.5 %reduce-scatter.23.cloned.1.call-done = bf16[1728,1536]{1,0:T(8,128)(2,1)} async-done(((bf16[6912,1536]{1,0:T(8,128)(2,1)}), bf16[1728,1536]{1,0:T(8,128)(2,1)}) %reduce-scatter.23.cloned.1.call-update) | async-done | bytes 5308432 | tf_op jit(solution)/shard_map/reduce_scatter | solution.py:227
  1962.2 22.8 all-reduce.6
  1988.2 530.2 %all-reduce.12.cloned.1.call-done = (bf16[384,1536]{1,0:T(8,128)(2,1)}, bf16[384,512]{1,0:T(8,128)(2,1)}, bf16[384,512]{1,0:T(8,128)(2,1)}, bf16[384,1536]{1,0:T...) async-done(((bf16[384,1536]{1,0:T(8,128)(2,1)}, bf16[384,512]{1,0:T(8,128)(2,1)}, bf16[384,512]{1,0:T(8,128)(2,1)}, ...) | async-done | bytes 19070992 | tf_op jit(solution)/shard_map/psum | solution.py:378
  (417 shorter events, 406.5 us)
Async XLA Ops:
  7.9 45.4 %all-gather.18.cloned.1.call-start = ((), (), s32[]{:S(2)}) async-start(), calls=%async_computation.11 | async-start | bytes 1966080 | tf_op jit(solution)/shard_map/all_gather | solution.py:97
  8.7 83.8 %all-gather.16.cloned.1.call-start = ((), (), s32[]{:S(2)}) async-start(), calls=%async_computation.10 | async-start | bytes 5898240 | tf_op jit(solution)/shard_map/all_gather | solution.py:95
  9.4 158.5 %all-gather.14.cloned.1.call-start = ((), (), s32[]{:S(2)}) async-start(), calls=%async_computation.9 | async-start | bytes 4718592 | tf_op jit(solution)/shard_map/all_gather | solution.py:142
  43.2 198.4 %all-gather.20.cloned.1.call-start = ((), (), s32[]{:S(2)}) async-start(), calls=%async_computation.12 | async-start | bytes 4718592 | tf_op jit(solution)/shard_map/all_gather | solution.py:143
  62.9 266.0 %all-gather.22.cloned.1.call-start = ((), (), s32[]{:S(2)}) async-start(), calls=%async_computation.13 | async-start | bytes 5898240 | tf_op jit(solution)/shard_map/all_gather | solution.py:98
  63.5 349.9 %all-gather.24.cloned.1.call-start = ((), (), s32[]{:S(2)}) async-start(), calls=%async_computation.14 | async-start | bytes 26542080 | tf_op jit(solution)/shard_map/all_gather | solution.py:179
  64.3 483.8 %all-gather.26.cloned.1.call-start = ((), (), s32[]{:S(2)}) async-start(), calls=%async_computation.15 | async-start | bytes 26542080 | tf_op jit(solution)/shard_map/all_gather | solution.py:180
  65.0 617.7 %all-gather.28.cloned.1.call-start = ((), (), s32[]{:S(2)}) async-start(), calls=%async_computation.16 | async-start | bytes 26542080 | tf_op jit(solution)/shard_map/all_gather | solution.py:181
  65.7 1228.0 %reduce-scatter.9.cloned.1.call-start = ((), (), s32[]{:S(2)}) async-start(), calls=%async_computation.17 | async-start | bytes 1310720 | tf_op jit(solution)/shard_map/reduce_scatter | solution.py:315
  748.9 45.6 %collective-permute-start = (bf16[2,512,512]{1,2,0:T(8,128)(2,1)}, bf16[2,512,512]{1,2,0:T(8,128)(2,1)S(1)}, u32[]{:S(2)}, u32[]{:S(2)}) collective-permute-start(bf16[2,512,512]{1,2,0:T(8,128)(2,1)} %copy.172), channel_id=1, source_target_pairs={{0,4},{4,8},{8,12},{12,16},{16,20},{20,24},{24,28},{1,5},{5,9},{9,... | collective-permute-start | bytes 3145736 | tf_op jit(solution)/shard_map/while/body/eval_jaxpr/ppermute | solution.py:25
  798.5 46.3 %collective-permute-start.1 = (bf16[2,512,512]{1,2,0:T(8,128)(2,1)}, bf16[2,512,512]{1,2,0:T(8,128)(2,1)S(1)}, u32[]{:S(2)}, u32[]{:S(2)}) collective-permute-start(bf16[2,512,512]{1,2,0:T(8,128)(2,1)} %convert_element_type.368), channel_id=1, source_target_pairs={{28,0},{0,4},{4,8},{8,12},{12,16},{16,20},{20,24},{24,28},{29,1},{... | collective-permute-start | bytes 3145736 | tf_op jit(solution)/shard_map/while/body/eval_jaxpr/ppermute | solution.py:19
  819.0 44.8 %collective-permute-start = (bf16[2,512,512]{1,2,0:T(8,128)(2,1)}, bf16[2,512,512]{1,2,0:T(8,128)(2,1)S(1)}, u32[]{:S(2)}, u32[]{:S(2)}) collective-permute-start(bf16[2,512,512]{1,2,0:T(8,128)(2,1)} %copy.172), channel_id=1, source_target_pairs={{0,4},{4,8},{8,12},{12,16},{16,20},{20,24},{24,28},{1,5},{5,9},{9,... | collective-permute-start | bytes 3145736 | tf_op jit(solution)/shard_map/while/body/eval_jaxpr/ppermute | solution.py:25
  867.8 45.4 %collective-permute-start.1 = (bf16[2,512,512]{1,2,0:T(8,128)(2,1)}, bf16[2,512,512]{1,2,0:T(8,128)(2,1)S(1)}, u32[]{:S(2)}, u32[]{:S(2)}) collective-permute-start(bf16[2,512,512]{1,2,0:T(8,128)(2,1)} %convert_element_type.368), channel_id=1, source_target_pairs={{28,0},{0,4},{4,8},{8,12},{12,16},{16,20},{20,24},{24,28},{29,1},{... | collective-permute-start | bytes 3145736 | tf_op jit(solution)/shard_map/while/body/eval_jaxpr/ppermute | solution.py:19
  870.2 44.6 %collective-permute-start = (bf16[2,512,512]{1,2,0:T(8,128)(2,1)}, bf16[2,512,512]{1,2,0:T(8,128)(2,1)S(1)}, u32[]{:S(2)}, u32[]{:S(2)}) collective-permute-start(bf16[2,512,512]{1,2,0:T(8,128)(2,1)} %copy.172), channel_id=1, source_target_pairs={{0,4},{4,8},{8,12},{12,16},{16,20},{20,24},{24,28},{1,5},{5,9},{9,... | collective-permute-start | bytes 3145736 | tf_op jit(solution)/shard_map/while/body/eval_jaxpr/ppermute | solution.py:25
  918.8 62.8 %collective-permute-start.1 = (bf16[2,512,512]{1,2,0:T(8,128)(2,1)}, bf16[2,512,512]{1,2,0:T(8,128)(2,1)S(1)}, u32[]{:S(2)}, u32[]{:S(2)}) collective-permute-start(bf16[2,512,512]{1,2,0:T(8,128)(2,1)} %convert_element_type.368), channel_id=1, source_target_pairs={{28,0},{0,4},{4,8},{8,12},{12,16},{16,20},{20,24},{24,28},{29,1},{... | collective-permute-start | bytes 3145736 | tf_op jit(solution)/shard_map/while/body/eval_jaxpr/ppermute | solution.py:19
  939.5 43.7 %collective-permute-start = (bf16[2,512,512]{1,2,0:T(8,128)(2,1)}, bf16[2,512,512]{1,2,0:T(8,128)(2,1)S(1)}, u32[]{:S(2)}, u32[]{:S(2)}) collective-permute-start(bf16[2,512,512]{1,2,0:T(8,128)(2,1)} %copy.172), channel_id=1, source_target_pairs={{0,4},{4,8},{8,12},{12,16},{16,20},{20,24},{24,28},{1,5},{5,9},{9,... | collective-permute-start | bytes 3145736 | tf_op jit(solution)/shard_map/while/body/eval_jaxpr/ppermute | solution.py:25
  987.1 61.9 %collective-permute-start.1 = (bf16[2,512,512]{1,2,0:T(8,128)(2,1)}, bf16[2,512,512]{1,2,0:T(8,128)(2,1)S(1)}, u32[]{:S(2)}, u32[]{:S(2)}) collective-permute-start(bf16[2,512,512]{1,2,0:T(8,128)(2,1)} %convert_element_type.368), channel_id=1, source_target_pairs={{28,0},{0,4},{4,8},{8,12},{12,16},{16,20},{20,24},{24,28},{29,1},{... | collective-permute-start | bytes 3145736 | tf_op jit(solution)/shard_map/while/body/eval_jaxpr/ppermute | solution.py:19
  989.7 61.0 %collective-permute-start = (bf16[2,512,512]{1,2,0:T(8,128)(2,1)}, bf16[2,512,512]{1,2,0:T(8,128)(2,1)S(1)}, u32[]{:S(2)}, u32[]{:S(2)}) collective-permute-start(bf16[2,512,512]{1,2,0:T(8,128)(2,1)} %copy.172), channel_id=1, source_target_pairs={{0,4},{4,8},{8,12},{12,16},{16,20},{20,24},{24,28},{1,5},{5,9},{9,... | collective-permute-start | bytes 3145736 | tf_op jit(solution)/shard_map/while/body/eval_jaxpr/ppermute | solution.py:25
  1054.6 61.0 %collective-permute-start.1 = (bf16[2,512,512]{1,2,0:T(8,128)(2,1)}, bf16[2,512,512]{1,2,0:T(8,128)(2,1)S(1)}, u32[]{:S(2)}, u32[]{:S(2)}) collective-permute-start(bf16[2,512,512]{1,2,0:T(8,128)(2,1)} %convert_element_type.368), channel_id=1, source_target_pairs={{28,0},{0,4},{4,8},{8,12},{12,16},{16,20},{20,24},{24,28},{29,1},{... | collective-permute-start | bytes 3145736 | tf_op jit(solution)/shard_map/while/body/eval_jaxpr/ppermute | solution.py:19
  1054.6 62.6 %collective-permute-start = (bf16[2,512,512]{1,2,0:T(8,128)(2,1)}, bf16[2,512,512]{1,2,0:T(8,128)(2,1)S(1)}, u32[]{:S(2)}, u32[]{:S(2)}) collective-permute-start(bf16[2,512,512]{1,2,0:T(8,128)(2,1)} %copy.172), channel_id=1, source_target_pairs={{0,4},{4,8},{8,12},{12,16},{16,20},{20,24},{24,28},{1,5},{5,9},{9,... | collective-permute-start | bytes 3145736 | tf_op jit(solution)/shard_map/while/body/eval_jaxpr/ppermute | solution.py:25
  1121.1 60.1 %collective-permute-start.1 = (bf16[2,512,512]{1,2,0:T(8,128)(2,1)}, bf16[2,512,512]{1,2,0:T(8,128)(2,1)S(1)}, u32[]{:S(2)}, u32[]{:S(2)}) collective-permute-start(bf16[2,512,512]{1,2,0:T(8,128)(2,1)} %convert_element_type.368), channel_id=1, source_target_pairs={{28,0},{0,4},{4,8},{8,12},{12,16},{16,20},{20,24},{24,28},{29,1},{... | collective-permute-start | bytes 3145736 | tf_op jit(solution)/shard_map/while/body/eval_jaxpr/ppermute | solution.py:19
  1121.1 61.7 %collective-permute-start = (bf16[2,512,512]{1,2,0:T(8,128)(2,1)}, bf16[2,512,512]{1,2,0:T(8,128)(2,1)S(1)}, u32[]{:S(2)}, u32[]{:S(2)}) collective-permute-start(bf16[2,512,512]{1,2,0:T(8,128)(2,1)} %copy.172), channel_id=1, source_target_pairs={{0,4},{4,8},{8,12},{12,16},{16,20},{20,24},{24,28},{1,5},{5,9},{9,... | collective-permute-start | bytes 3145736 | tf_op jit(solution)/shard_map/while/body/eval_jaxpr/ppermute | solution.py:25
  1186.8 59.1 %collective-permute-start.1 = (bf16[2,512,512]{1,2,0:T(8,128)(2,1)}, bf16[2,512,512]{1,2,0:T(8,128)(2,1)S(1)}, u32[]{:S(2)}, u32[]{:S(2)}) collective-permute-start(bf16[2,512,512]{1,2,0:T(8,128)(2,1)} %convert_element_type.368), channel_id=1, source_target_pairs={{28,0},{0,4},{4,8},{8,12},{12,16},{16,20},{20,24},{24,28},{29,1},{... | collective-permute-start | bytes 3145736 | tf_op jit(solution)/shard_map/while/body/eval_jaxpr/ppermute | solution.py:19
  1186.8 60.8 %collective-permute-start = (bf16[2,512,512]{1,2,0:T(8,128)(2,1)}, bf16[2,512,512]{1,2,0:T(8,128)(2,1)S(1)}, u32[]{:S(2)}, u32[]{:S(2)}) collective-permute-start(bf16[2,512,512]{1,2,0:T(8,128)(2,1)} %copy.172), channel_id=1, source_target_pairs={{0,4},{4,8},{8,12},{12,16},{16,20},{20,24},{24,28},{1,5},{5,9},{9,... | collective-permute-start | bytes 3145736 | tf_op jit(solution)/shard_map/while/body/eval_jaxpr/ppermute | solution.py:25
  1250.3 105.4 %reduce-scatter.13.cloned.1.call-start = ((), (), s32[]{:S(2)}) async-start(), calls=%async_computation.19 | async-start | bytes 1966080 | tf_op jit(solution)/shard_map/reduce_scatter | solution.py:358
  1298.4 58.9 %reduce-scatter.15.cloned.1.call-start = ((), (), s32[]{:S(2)}) async-start(), calls=%async_computation.20 | async-start | bytes 1966080 | tf_op jit(solution)/shard_map/reduce_scatter | solution.py:361
  1300.3 108.1 %reduce-scatter.11.cloned.1.call-start = ((), (), s32[]{:S(2)}) async-start(), calls=%async_computation.18 | async-start | bytes 5898240 | tf_op jit(solution)/shard_map/reduce_scatter | solution.py:355
  1317.4 141.9 %reduce-scatter.17.cloned.1.call-start = ((), (), s32[]{:S(2)}) async-start(), calls=%async_computation.21 | async-start | bytes 5898240 | tf_op jit(solution)/shard_map/reduce_scatter | solution.py:364
  1322.2 294.6 %reduce-scatter.19.cloned.1.call-start = ((), (), s32[]{:S(2)}) async-start(), calls=%async_computation.22 | async-start | bytes 26542080 | tf_op jit(solution)/shard_map/reduce_scatter | solution.py:221
  1332.3 441.7 %reduce-scatter.21.cloned.1.call-start = ((), (), s32[]{:S(2)}) async-start(), calls=%async_computation.23 | async-start | bytes 26542080 | tf_op jit(solution)/shard_map/reduce_scatter | solution.py:224
  1343.9 587.6 %reduce-scatter.23.cloned.1.call-start = ((), (), s32[]{:S(2)}) async-start(), calls=%async_computation.24 | async-start | bytes 26542080 | tf_op jit(solution)/shard_map/reduce_scatter | solution.py:227
  1355.6 1162.8 %all-reduce.12.cloned.1.call-start = ((), (), s32[]{:S(2)}) async-start(), calls=%async_computation.25 | async-start | bytes 38141952 | tf_op jit(solution)/shard_map/psum | solution.py:378
  (80 other events, 3263.1 us)
Sparse Core Ops, SparseCore 0:
  9.6 22.4 all-gather.11
  33.6 19.6 all-gather.17
  54.9 37.4 all-gather.15
  94.4 73.3 all-gather.13
  169.8 71.6 all-gather.19
  242.9 35.7 all-gather.21
  280.3 133.0 all-gather.23
  414.9 133.0 all-gather.25
  549.6 133.0 all-gather.27
  1250.4 43.2 reduce-scatter.8
  1298.5 28.1 reduce-scatter.12
  1329.1 28.1 reduce-scatter.14
  1360.5 47.8 reduce-scatter.10
  1411.4 47.8 reduce-scatter.16
  1461.9 154.7 reduce-scatter.18
  1619.2 154.7 reduce-scatter.20
  1776.7 154.7 reduce-scatter.22
  1937.1 581.2 all-reduce.11
where the time goes:
time: 2560 us; the launch traced here: 2550 us
  waiting for transfers between devices  2000 us (78%)
  matrix products  198 us (8%)
  starting transfers between devices  115 us (4%)
  other arithmetic  107 us (4%)
  blocking collectives  63.4 us (2%)
  local copies, waits for them, and re-layouts  47.3 us (2%)
    psum x1, waiting for transfers between devices, on_device(): lax.psum(wq_part.astype(jnp.bfloat16), 'ctx').astype(jnp.float32)  530 us
    ppermute x8, waiting for transfers between devices, passed_along(): return lax.ppermute(block, axis, route)  311 us
    reduce_scatter x1, waiting for transfers between devices, on_device(): lax.psum_scatter(gate_term.astype(jnp.bfloat16), 'fsdp', scatter_dimensio...  157 us
    reduce_scatter x1, waiting for transfers between devices, on_device(): lax.psum_scatter(down_term.astype(jnp.bfloat16), 'fsdp', scatter_dimensio...  157 us
    reduce_scatter x1, waiting for transfers between devices, on_device(): lax.psum_scatter(up_term.astype(jnp.bfloat16), 'fsdp', scatter_dimension=...  157 us
    all_gather x1, waiting for transfers between devices, on_device(): lax.all_gather(w_down, 'fsdp', axis=0, tiled=True)  122 us
    all_gather x1, waiting for transfers between devices, on_device(): lax.all_gather(w_up, 'fsdp', axis=0, tiled=True)  122 us
    all_gather x1, waiting for transfers between devices, on_device(): lax.all_gather(w_gate, 'fsdp', axis=0, tiled=True)  81 us
  transfers between devices with their start and end apart: 34, of which 25 were waited for; matrix products, arithmetic and copies ran while one was open for 9% of the time, Pallas kernels for 0%

commit v1 on v0

v1 whole, which is shorter than its diff:
```python
import functools

import jax
import jax.numpy as jnp
from jax import lax
from jax.experimental import pallas as pl
from jax.experimental.pallas import tpu as pltpu
from jax.sharding import PartitionSpec as P

QUERY_HEADS = 24
KEY_VALUE_HEADS = 8
HEAD_SIZE = 64
GROUP = QUERY_HEADS // KEY_VALUE_HEADS
QW = GROUP * HEAD_SIZE
LANES = 128

EPSILON = 1e-05
ROPE_BASE = 1000000.0
APART = 16384.0

MESH = pl.DeviceIdType.MESH
F32 = jnp.float32
BF16 = jnp.bfloat16
ANY = pl.BlockSpec(memory_space=pl.ANY)
VMEM = pl.BlockSpec(memory_space=pltpu.VMEM)
VMEM_LIMIT = 56 * 1024 * 1024


class Team:
    def __init__(self, B, F, T):
        self.B, self.F, self.T = B, F, T
        ctx, self.f = lax.axis_index("ctx"), lax.axis_index("fsdp")
        self.t, self.y = lax.div(ctx, B), lax.rem(ctx, B)
        self.p = self.y * F + self.f

    def member(self, p):
        return (self.t * self.B + lax.div(p, self.F), lax.rem(p, self.F))

    def same_row(self, f):
        return (self.t * self.B + self.y, f)

    def other_team(self, t):
        return (t * self.B + self.y, self.f)


def flip(p, bit):
    return p + bit * (1 - 2 * lax.rem(lax.div(p, bit), 2))


def bit_of(p, bit):
    return lax.rem(lax.div(p, bit), 2)


class Sems:
    def __init__(self, send, recv):
        self.send, self.recv, self.used = send, recv, 0

    def copy(self, src, dst, device):
        i = self.used
        self.used += 1
        return pltpu.make_async_remote_copy(
            src_ref=src,
            dst_ref=dst,
            send_sem=self.send.at[i],
            recv_sem=self.recv.at[i],
            device_id=device,
            device_id_type=MESH,
        )


def greet(devices):
    barrier = pltpu.get_barrier_semaphore()
    for device in devices:
        pl.semaphore_signal(barrier, inc=1, device_id=device, device_id_type=MESH)
    pl.semaphore_wait(barrier, len(devices))


def team_peers(team):
    n = team.B * team.F
    return [team.member(lax.rem(team.p + d, n)) for d in range(1, n)]


def line_peers(team):
    return [team.other_team(lax.rem(team.t + d, team.T)) for d in range(1, team.T)]


def row_peers(team):
    return [team.same_row(lax.rem(team.f + d, team.F)) for d in range(1, team.F)]


class Gather:
    def __init__(self, sems, me, count, device, own, block, half):
        self.sems, self.me, self.count, self.device = sems, me, count, device
        self.own, self.block, self.half = own, block, half
        self.pending = []

    def send(self, src, dst, to):
        copy = self.sems.copy(src, dst, self.device(to))
        copy.start()
        self.pending.append(copy)
        return copy

    def begin(self):
        me = self.me
        self.first = [
            self.send(self.own, self.block(me), flip(me, 1 << k))
            for k in range(self.count.bit_length() - 1)
        ]

    def relay(self):
        me = self.me
        one = flip(me, 1)
        two = flip(me, 2)
        self.first[1].wait_recv()
        self.late = [self.send(self.block(two), self.block(two), one)]
        if self.count == 8:
            four = flip(me, 4)
            low = self.send(self.half(two, 0), self.half(two, 0), four)
            self.first[2].wait_recv()
            self.late.append(self.send(self.block(four), self.block(four), one))
            high = self.send(self.half(four, 1), self.half(four, 1), two)
            far = flip(two, 4)
            self.corner = [(low, far, 0), (high, far, 1)]

    def end(self):
        one = flip(self.me, 1)
        if self.count == 8:
            for copy, far, k in self.corner:
                copy.wait_recv()
                self.late.append(self.send(self.half(far, k), self.half(far, k), one))
        self.first[0].wait_recv()
        for copy in self.late:
            copy.wait_recv()
        for copy in self.pending:
            copy.wait_send()

    COPIES = 9


def scatter_shapes(rows, width):
    half = width // 2
    return [
        pltpu.VMEM((2, 2, rows, width), BF16),
        pltpu.VMEM((2, rows, half), BF16),
        pltpu.VMEM((2, rows, half), BF16),
        pltpu.VMEM((2, rows, half), BF16),
        pltpu.VMEM((2, rows, half), BF16),
        pltpu.VMEM((rows, half), BF16),
        pltpu.VMEM((rows, half), BF16),
        pltpu.VMEM((rows, half), BF16),
        pltpu.VMEM((rows, half), BF16),
    ]


SCATTER_COPIES = 5


def reduce_scatter(sems, team, x, scratch, store):
    r0, s1l, s1r, r1l, r1r, s2l, s2r, r2l, r2r = scratch
    p = team.p
    b0, b1, b2 = bit_of(p, 1), bit_of(p, 2), bit_of(p, 4)
    n0, n1, n2 = 1 - b0, 1 - b1, 1 - b2
    width = x.shape[-1]
    left, right = pl.ds(0, width // 2), pl.ds(width // 2, width // 2)
    send = lambda src, dst, bit: sems.copy(src, dst, team.member(flip(p, bit)))
    wide = lambda v: v.astype(F32)

    first = send(x.at[:, :, n0], r0, 1)
    first.start()
    first.wait_recv()
    for k in range(2):
        s1l[k] = (wide(x[k, n1, b0, :, left]) + wide(r0[k, n1, :, left])).astype(BF16)
    l1 = send(s1l, r1l, 2)
    l1.start()
    for k in range(2):
        s1r[k] = (wide(x[n2, k, b0, :, right]) + wide(r0[n2, k, :, right])).astype(BF16)
    r1 = send(s1r, r1r, 4)
    r1.start()
    l1.wait_recv()
    s2l[...] = (
        wide(x[n2, b1, b0, :, left]) + wide(r0[n2, b1, :, left]) + wide(r1l[n2])
    ).astype(BF16)
    l2 = send(s2l, r2l, 4)
    l2.start()
    r1.wait_recv()
    s2r[...] = (
        wide(x[b2, n1, b0, :, right]) + wide(r0[b2, n1, :, right]) + wide(r1r[n1])
    ).astype(BF16)
    r2 = send(s2r, r2r, 2)
    r2.start()
    l2.wait_recv()
    store(
        left,
        wide(x[b2, b1, b0, :, left])
        + wide(r0[b2, b1, :, left])
        + wide(r1l[b2])
        + wide(r2l[...]),
    )
    r2.wait_recv()
    store(
        right,
        wide(x[b2, b1, b0, :, right])
        + wide(r0[b2, b1, :, right])
        + wide(r1r[b1])
        + wide(r2r[...]),
    )
    for copy in (first, l1, r1, l2, r2):
        copy.wait_send()


def kernel_params(collective_id):
    return pltpu.CompilerParams(
        collective_id=collective_id, has_side_effects=True, vmem_limit_bytes=VMEM_LIMIT
    )


def inputs_kernel(dims, tokens, wq, wk, wv, gains, w_gate, w_up, tok_full, wqkv, gains_full, gate_cut, up_cut,
                  q_in, k_in, v_in, qkv_cut, slab_g, slab_u, cut_g, cut_u, send, recv, local):
    team = Team(*dims)
    B, F = team.B, team.F
    sems = Sems(send, recv)
    loads = [
        pltpu.make_async_copy(src, dst, local.at[i])
        for i, (src, dst) in enumerate(
            [(wq, q_in), (wk, k_in), (wv, v_in), (w_gate, slab_g), (w_up, slab_u), (tokens, tok_full.at[team.p]),
             (gains, gains_full.at[team.f])]
        )
    ]
    for load in loads:
        load.start()
    greet(team_peers(team))
    rows = tokens.shape[0]
    gather = Gather(
        sems, team.p, B * F, team.member, tokens,
        lambda i: tok_full.at[i],
        lambda i, k: tok_full.at[i, pl.ds(k * rows // 2, rows // 2)],
    )
    gather.begin()
    small = [sems.copy(gains, gains_full.at[team.f], peer) for peer in row_peers(team)]
    for copy in small:
        copy.start()
    for load in loads[:3]:
        load.wait()
    for f in range(F):
        for y in range(B):
            h = f * B + y

            @pl.when(team.y == y)
            def _():
                qkv_cut[f, :, 0:QW] = q_in[:, h * QW : (h + 1) * QW]
                qkv_cut[f, :, QW : QW + HEAD_SIZE] = k_in[:, h * HEAD_SIZE : (h + 1) * HEAD_SIZE]
                qkv_cut[f, :, QW + HEAD_SIZE : QW + 2 * HEAD_SIZE] = v_in[:, h * HEAD_SIZE : (h + 1) * HEAD_SIZE]

    sent = []
    for d in range(1, F):
        to = lax.rem(team.f + d, F)
        sent.append(sems.copy(qkv_cut.at[to], wqkv.at[team.f], team.same_row(to)))
        sent[-1].start()
    own = pltpu.make_async_copy(qkv_cut.at[team.f], wqkv.at[team.f], local.at[7])
    own.start()
    gather.relay()
    stores = []
    for i, (slab, cut, out) in enumerate([(slab_g, cut_g, gate_cut), (slab_u, cut_u, up_cut)]):
        loads[3 + i].wait()
        width = cut.shape[-1]

        @pl.loop(0, slab.shape[0] // 32)
        def _(r):
            at = pl.ds(pl.multiple_of(r * 32, 32), 32)
            for f in range(F):
                for y in range(B):
                    q = f * B + y

                    @pl.when(team.y == y)
                    def _():
                        cut[f, at, :] = slab[at, q * width : (q + 1) * width]

        stores.append(pltpu.make_async_copy(cut, out, local.at[8 + i]))
        stores[-1].start()
    gather.end()
    for copy in small + sent:
        copy.wait()
    for copy in loads[5:] + [own] + stores:
        copy.wait()


def gather_inputs(dims, tokens, wq, wk, wv, gains, w_gate, w_up):
    B, F, T = dims
    rows, width = tokens.shape
    depth, ff = w_gate.shape
    cols = ff // (B * F)
    copies = Gather.COPIES + 2 * (F - 1)
    heads = QW + 2 * HEAD_SIZE
    return pl.pallas_call(
        functools.partial(inputs_kernel, dims),
        out_shape=(
            jax.ShapeDtypeStruct((B * F, rows, width), BF16),
            jax.ShapeDtypeStruct((F, depth, heads), BF16),
            jax.ShapeDtypeStruct((F,) + gains.shape, BF16),
            jax.ShapeDtypeStruct((F, depth, cols), BF16),
            jax.ShapeDtypeStruct((F, depth, cols), BF16),
        ),
        in_specs=[ANY] * 7,
        out_specs=[ANY] * 5,
        scratch_shapes=[
            pltpu.VMEM(wq.shape, BF16),
            pltpu.VMEM(wk.shape, BF16),
            pltpu.VMEM(wv.shape, BF16),
            pltpu.VMEM((F, depth, heads), BF16),
            pltpu.VMEM(w_gate.shape, BF16),
            pltpu.VMEM(w_up.shape, BF16),
            pltpu.VMEM((F, depth, cols), BF16),
            pltpu.VMEM((F, depth, cols), BF16),
            pltpu.SemaphoreType.DMA((copies,)),
            pltpu.SemaphoreType.DMA((copies,)),
            pltpu.SemaphoreType.DMA((10,)),
        ],
        compiler_params=kernel_params(1),
        name="gather_inputs",
    )(tokens, wq, wk, wv, gains, w_gate, w_up)


def lane_ids(rows):
    return lax.broadcasted_iota(jnp.int32, (rows, LANES), 1)


def widen_keys(kv, spans, first_row, kx, vx):
    rows = kv.shape[0]
    lane = lane_ids(rows)
    row = lax.broadcasted_iota(jnp.int32, (rows, LANES), 0) + first_row
    inside = (row >= spans[0:1, :]) & (row < spans[1:2, :])
    wide = kv.astype(F32)
    kx[...] = jnp.where(lane < HEAD_SIZE, wide, jnp.where(inside, 1.0, 0.0)).astype(BF16)
    vx[...] = jnp.where(lane < HEAD_SIZE, pltpu.roll(wide, HEAD_SIZE, 1), 1.0).astype(BF16)


def dot_last(a, b):
    return lax.dot_general(a, b, (((1,), (1,)), ((), ())), preferred_element_type=F32)


def attend_kernel(dims, qx, kv, spans, dy, wo, gate_cut, up_cut, kv_all, acc, mixed, dy_full, wo_full, w_gate, w_up,
                  kx, vx, packed, send, recv, line_send, line_recv, local):
    team = Team(*dims)
    B, F, T = dims
    t = team.t
    sems = Sems(send, recv)
    rows = kv.shape[0]
    part = rows // 2
    homes = [
        pltpu.make_async_copy(kv, kv_all.at[t], local.at[0]),
        pltpu.make_async_copy(dy, dy_full.at[team.p], local.at[1]),
        pltpu.make_async_copy(wo, wo_full.at[team.f], local.at[2]),
        pltpu.make_async_copy(gate_cut.at[team.f], w_gate.at[team.f], local.at[3]),
        pltpu.make_async_copy(up_cut.at[team.f], w_up.at[team.f], local.at[4]),
    ]
    for copy in homes:
        copy.start()
    greet(team_peers(team) + line_peers(team))

    def line_copy(d, source, to):
        return pltpu.make_async_remote_copy(
            src_ref=kv, dst_ref=kv_all.at[source], send_sem=line_send.at[d], recv_sem=line_recv.at[source],
            device_id=team.other_team(to), device_id_type=MESH,
        )

    for d in range(1, T):

        @pl.when(t + d < T)
        def _():
            line_copy(d, t, t + d).start()

    half_wo, half_dy = wo.shape[0] // 2, dy.shape[0] // 2
    gather_wo = Gather(
        sems, team.f, F, team.same_row, wo, lambda i: wo_full.at[i],
        lambda i, k: wo_full.at[i, pl.ds(k * half_wo, half_wo)],
    )
    gather_wo.begin()
    sent = []
    for cut, full in ((gate_cut, w_gate), (up_cut, w_up)):
        for d in range(1, F):
            to = lax.rem(team.f + d, F)
            sent.append(sems.copy(cut.at[to], full.at[team.f], team.same_row(to)))
            sent[-1].start()
    gather_dy = Gather(
        sems, team.p, B * F, team.member, dy, lambda i: dy_full.at[i],
        lambda i, k: dy_full.at[i, pl.ds(k * half_dy, half_dy)],
    )
    gather_dy.begin()
    homes[0].wait()
    widen_keys(kv_all[t], spans, t * rows, kx, vx)
    causal = lax.broadcasted_iota(jnp.int32, (part, part), 1) <= lax.broadcasted_iota(jnp.int32, (part, part), 0)

    def piece(q, k, masked):
        scores = dot_last(q, kx[k * part : (k + 1) * part, :])
        weights = jnp.exp(scores)
        if masked:
            weights = jnp.where(causal, weights, 0.0)
        return jnp.dot(weights.astype(BF16), vx[k * part : (k + 1) * part, :], preferred_element_type=F32)

    @pl.loop(0, GROUP)
    def _(h):
        acc[h, 0:part, :] = piece(qx[h, 0:part, :], 0, True)
        low = qx[h, part:rows, :]
        acc[h, part:rows, :] = piece(low, 0, False) + piece(low, 1, True)

    gather_wo.relay()

    @pl.loop(1, t + 1)
    def _(j):
        source = t - j
        line_copy(0, source, t).wait_recv()
        widen_keys(kv_all[source], spans, source * rows, kx, vx)

        @pl.loop(0, GROUP)
        def _(h):
            for k in range(2):
                at = pl.ds(k * part, part)
                q = qx[h, at, :]
                acc[h, at, :] = acc[h, at, :] + piece(q, 0, False) + piece(q, 1, False)

    for h in range(GROUP):
        out = acc[h, :, 0:HEAD_SIZE] / acc[h, :, HEAD_SIZE : 2 * HEAD_SIZE]
        out = out.astype(BF16)
        if h < 2:
            packed[0:rows, h * HEAD_SIZE : (h + 1) * HEAD_SIZE] = out
        else:
            packed[rows : rows + part, 0:HEAD_SIZE] = out[0:part]
            packed[rows : rows + part, HEAD_SIZE : 2 * HEAD_SIZE] = out[part:rows]
    home = pltpu.make_async_copy(packed, mixed.at[team.p], local.at[5])
    home.start()
    half_mixed = packed.shape[0] // 2
    gather_mixed = Gather(
        sems, team.p, B * F, team.member, packed, lambda i: mixed.at[i],
        lambda i, k: mixed.at[i, pl.ds(k * half_mixed, half_mixed)],
    )
    gather_mixed.begin()
    gather_mixed.relay()
    gather_dy.relay()
    gather_mixed.end()
    gather_wo.end()
    gather_dy.end()
    for copy in sent:
        copy.wait()
    for copy in homes[1:] + [home]:
        copy.wait()
    for d in range(1, T):

        @pl.when(t + d < T)
        def _():
            line_copy(d, t, t + d).wait_send()


def attend(dims, qx, kv, spans, dy, wo, gate_cut, up_cut):
    B, F, T = dims
    rows = kv.shape[0]
    copies = 3 * Gather.COPIES + 2 * (F - 1)
    packed = (rows + rows // 2, LANES)
    return pl.pallas_call(
        functools.partial(attend_kernel, dims),
        out_shape=(
            jax.ShapeDtypeStruct((T, rows, LANES), BF16),
            jax.ShapeDtypeStruct((GROUP, rows, LANES), F32),
            jax.ShapeDtypeStruct((B * F,) + packed, BF16),
            jax.ShapeDtypeStruct((B * F,) + dy.shape, BF16),
            jax.ShapeDtypeStruct((F,) + wo.shape, BF16),
            jax.ShapeDtypeStruct(gate_cut.shape, BF16),
            jax.ShapeDtypeStruct(up_cut.shape, BF16),
        ),
        in_specs=[VMEM, ANY, VMEM, ANY, ANY, ANY, ANY],
        out_specs=[VMEM, VMEM, ANY, ANY, ANY, ANY, ANY],
        scratch_shapes=[
            pltpu.VMEM((rows, LANES), BF16),
            pltpu.VMEM((rows, LANES), BF16),
            pltpu.VMEM(packed, BF16),
            pltpu.SemaphoreType.DMA((copies,)),
            pltpu.SemaphoreType.DMA((copies,)),
            pltpu.SemaphoreType.DMA((T,)),
            pltpu.SemaphoreType.DMA((T,)),
            pltpu.SemaphoreType.DMA((6,)),
        ],
        compiler_params=kernel_params(2),
        name="attend",
    )(qx, kv, spans, dy, wo, gate_cut, up_cut)


def attend_back_kernel(dims, qx, dox, kv_all, spans, dq, dkv, kx, vx, dk, dv):
    team = Team(*dims)
    t = team.t
    rows = qx.shape[1]
    part = rows // 2
    dq[...] = jnp.zeros_like(dq)
    causal = lax.broadcasted_iota(jnp.int32, (part, part), 0) <= lax.broadcasted_iota(jnp.int32, (part, part), 1)
    lane = lane_ids(part)

    def piece(h, q_rows, k_rows, masked):
        q = qx[h, q_rows, :]
        do = dox[h, q_rows, :]
        keys = kx[k_rows, :]
        weights = jnp.exp(dot_last(keys, q))
        if masked:
            weights = jnp.where(causal, weights, 0.0)
        dscore = (weights * dot_last(vx[k_rows, :], do)).astype(BF16)
        dv[...] += jnp.dot(weights.astype(BF16), do, preferred_element_type=F32)
        dk[...] += jnp.dot(dscore, q, preferred_element_type=F32)
        dq[h, q_rows, :] += lax.dot_general(dscore, keys, (((0,), (0,)), ((), ())), preferred_element_type=F32)

    def block(source, diagonal):
        widen_keys(kv_all[source], spans, source * rows, kx, vx)
        for k in range(2):
            k_rows = slice(k * part, (k + 1) * part)
            dk[...] = jnp.zeros_like(dk)
            dv[...] = jnp.zeros_like(dv)

            @pl.loop(0, GROUP)
            def _(h):
                for q in range(k if diagonal else 0, 2):
                    piece(h, slice(q * part, (q + 1) * part), k_rows, diagonal and q == k)

            dkv[source, k_rows, :] = jnp.where(
                lane < HEAD_SIZE, dk[...], pltpu.roll(dv[...], HEAD_SIZE, 1)
            ).astype(BF16)

    block(t, True)

    @pl.loop(0, t)
    def _(source):
        block(source, False)


def attend_back(dims, qx, dox, kv_all, spans):
    part = qx.shape[1] // 2
    rows = qx.shape[1]
    return pl.pallas_call(
        functools.partial(attend_back_kernel, dims),
        out_shape=(
            jax.ShapeDtypeStruct(qx.shape, F32),
            jax.ShapeDtypeStruct(kv_all.shape, BF16),
        ),
        in_specs=[VMEM] * 4,
        out_specs=[VMEM] * 2,
        scratch_shapes=[
            pltpu.VMEM((rows, LANES), BF16),
            pltpu.VMEM((rows, LANES), BF16),
            pltpu.VMEM((part, LANES), F32),
            pltpu.VMEM((part, LANES), F32),
        ],
        compiler_params=pltpu.CompilerParams(vmem_limit_bytes=VMEM_LIMIT),
        name="attend_back",
    )(qx, dox, kv_all, spans)


def scatter_kernel(dims, x, out, *rest):
    team = Team(*dims)
    scratch, (send, recv) = rest[:-2], rest[-2:]
    greet([team.member(flip(team.p, bit)) for bit in (1, 2, 4)])

    def store(columns, total):
        out[:, columns] = total

    reduce_scatter(Sems(send, recv), team, x, scratch, store)


def team_scatter(dims, x, collective_id):
    rows, width = x.shape[0] // KEY_VALUE_HEADS, x.shape[1]
    return pl.pallas_call(
        functools.partial(scatter_kernel, dims),
        out_shape=jax.ShapeDtypeStruct((rows, width), F32),
        in_specs=[VMEM],
        out_specs=VMEM,
        scratch_shapes=scatter_shapes(rows, width)
        + [pltpu.SemaphoreType.DMA((SCATTER_COPIES,)), pltpu.SemaphoreType.DMA((SCATTER_COPIES,))],
        compiler_params=kernel_params(collective_id),
        name="team_scatter",
    )(x.reshape(2, 2, 2, rows, width))


def gather_kernel(dims, x, full, send, recv, local):
    team = Team(*dims)
    home = pltpu.make_async_copy(x, full.at[team.p], local)
    home.start()
    greet([team.member(flip(team.p, bit)) for bit in (1, 2, 4)])
    half = x.shape[0] // 2
    gather = Gather(
        Sems(send, recv), team.p, team.B * team.F, team.member, x, lambda i: full.at[i],
        lambda i, k: full.at[i, pl.ds(k * half, half)],
    )
    gather.begin()
    gather.relay()
    gather.end()
    home.wait()


def team_gather(dims, x, collective_id):
    full = pl.pallas_call(
        functools.partial(gather_kernel, dims),
        out_shape=jax.ShapeDtypeStruct((KEY_VALUE_HEADS,) + x.shape, x.dtype),
        in_specs=[ANY],
        out_specs=ANY,
        scratch_shapes=[
            pltpu.SemaphoreType.DMA((Gather.COPIES,)),
            pltpu.SemaphoreType.DMA((Gather.COPIES,)),
            pltpu.SemaphoreType.DMA,
        ],
        compiler_params=kernel_params(collective_id),
        name="team_gather",
    )(x)
    return full.reshape((-1,) + x.shape[1:])


def keys_back_kernel(dims, dkv, x, total, out, landed, *rest):
    team = Team(*dims)
    T, t = team.T, team.t
    scratch, (send, recv, line_send, line_recv) = rest[:-4], rest[-4:]
    greet([team.member(flip(team.p, bit)) for bit in (1, 2, 4)] + line_peers(team))

    def line_copy(d, owner, source):
        return pltpu.make_async_remote_copy(
            src_ref=dkv.at[owner], dst_ref=landed.at[source], send_sem=line_send.at[d],
            recv_sem=line_recv.at[source], device_id=team.other_team(owner), device_id_type=MESH,
        )

    for d in range(1, T):

        @pl.when(t - d >= 0)
        def _():
            line_copy(d, t - d, t).start()

    def store(columns, value):
        out[:, columns] = value

    reduce_scatter(Sems(send, recv), team, x, scratch, store)
    total[...] = dkv[t].astype(F32)
    for d in range(1, T):

        @pl.when(t + d < T)
        def _():
            line_copy(0, t, t + d).wait_recv()
            total[...] += landed[t + d].astype(F32)

    for d in range(1, T):

        @pl.when(t - d >= 0)
        def _():
            line_copy(d, t - d, t).wait_send()


def keys_back(dims, dkv, x):
    T = dims[2]
    rows, width = x.shape[0] // KEY_VALUE_HEADS, x.shape[1]
    return pl.pallas_call(
        functools.partial(keys_back_kernel, dims),
        out_shape=(
            jax.ShapeDtypeStruct(dkv.shape[1:], F32),
            jax.ShapeDtypeStruct((rows, width), F32),
        ),
        in_specs=[VMEM] * 2,
        out_specs=[VMEM] * 2,
        scratch_shapes=[pltpu.VMEM(dkv.shape, BF16)]
        + scatter_shapes(rows, width)
        + [
            pltpu.SemaphoreType.DMA((SCATTER_COPIES,)),
            pltpu.SemaphoreType.DMA((SCATTER_COPIES,)),
            pltpu.SemaphoreType.DMA((T,)),
            pltpu.SemaphoreType.DMA((T,)),
        ],
        compiler_params=kernel_params(5),
        name="keys_back",
    )(dkv, x.reshape(2, 2, 2, rows, width))


HOP = 2
LAG = 3


def grads_kernel(dims, step1, step2, g1, g2, out1, out2, land1, land2, fin1, fin2, red_recv, fin_recv, hand_recv,
                 bulk):
    team = Team(*dims)
    B, F, T = dims
    t, y, f = team.t, team.y, team.f
    depth = g1.shape[0]
    half1, half2 = depth // 2, g2.shape[0] // 2
    n1, n2 = half1 // step1, half2 // step2
    total = n1 + n2
    shard = depth // F
    per_shard = shard // step1
    RED, FIN, HAND, OWN, OVER, HOME, INTO = range(7)
    up_peer, down_peer = lax.rem(t + 1, T), lax.rem(t + T - 1, T)
    peers = row_peers(team)
    if B == 2:
        peers = peers + [team.member(lax.rem(team.p + F, B * F))]
    if T == 2:
        greet(peers + [team.other_team(up_peer)])
    else:
        greet(peers + [team.other_team(up_peer), team.other_team(down_peer)])
    kinds = (
        (g1, land1, fin1, step1, half1, 0),
        (g2, land2, fin2, step2, half2, 1),
    )

    def remote(src, dst, send_sem, recv_sem, device):
        return pltpu.make_async_remote_copy(
            src_ref=src, dst_ref=dst, send_sem=send_sem, recv_sem=recv_sem, device_id=device, device_id_type=MESH
        )

    def each(i, way, body):
        @pl.when((i >= 0) & (i < n2))
        def _():
            body(kinds[1], way, i, i)

        @pl.when((i >= n2) & (i < total))
        def _():
            body(kinds[0], way, i - n2, i)

    def chunk_rows(kind, way, c):
        step, half = kind[3], kind[4]
        return pl.ds(pl.multiple_of(way * half + c * step, 16), step)

    def onward(way):
        return t + 1 - 2 * way

    def back(way):
        return t - 1 + 2 * way

    def is_first(way):
        return t == (T - 1 if way else 0)

    def is_last(way):
        return t == (0 if way else T - 1)

    def reduce_copy(kind, way, at, i):
        g, land, fin, step, half, k = kind
        return remote(g.at[at], land.at[at], bulk.at[RED, k, way], red_recv.at[way, i], team.other_team(onward(way)))

    def final_copy(kind, way, at, i):
        g, land, fin, step, half, k = kind
        return remote(fin.at[at], fin.at[at], bulk.at[FIN, k, way], fin_recv.at[way, i], team.other_team(back(way)))

    def reduce(kind, way, c, i):
        g, land, fin, step, half, k = kind
        at = chunk_rows(kind, way, c)

        @pl.when(is_first(way))
        def _():
            reduce_copy(kind, way, at, i).start()

        @pl.when(jnp.logical_not(is_first(way)))
        def _():
            reduce_copy(kind, way, at, i).wait_recv()
            summed = (g[at, :].astype(F32) + land[at, :].astype(F32)).astype(BF16)

            @pl.when(is_last(way))
            def _():
                fin[at, :] = summed

            @pl.when(jnp.logical_not(is_last(way)))
            def _():
                g[at, :] = summed
                reduce_copy(kind, way, at, i).start()

    def hand1(way, c, at):
        row = way * half1 + c * step1
        to = lax.div(row, shard)
        place = lax.rem(row, shard)
        rows = pl.ds(pl.multiple_of(place, 16), step1)
        return to, place, rows

    def finish(kind, way, c, i):
        g, land, fin, step, half, k = kind
        at = chunk_rows(kind, way, c)

        @pl.when(jnp.logical_not(is_last(way)))
        def _():
            final_copy(kind, way, at, i).wait_recv()

        @pl.when(jnp.logical_not(is_first(way)))
        def _():
            final_copy(kind, way, at, i).start()

        if k == 0:
            to, place, rows = hand1(way, c, at)
            dst = out1.at[f * B + y, rows]

            @pl.when(to == f)
            def _():
                pltpu.make_async_copy(fin.at[at], dst, bulk.at[HOME, 0, 0]).start()
                if B == 2:
                    remote(fin.at[at], dst, bulk.at[OVER, 0, 0], bulk.at[INTO, 0, 0],
                           team.member(lax.rem(team.p + F, B * F))).start()

            @pl.when(to != f)
            def _():
                remote(fin.at[at], dst, bulk.at[HAND, 0, 0], hand_recv.at[f, lax.div(place, step1)],
                       team.same_row(to)).start()
        else:
            dst = out2.at[y, at]
            pltpu.make_async_copy(fin.at[at], dst, bulk.at[HOME, 1, 0]).start()
            if B == 2:
                remote(fin.at[at], dst, bulk.at[OVER, 1, 0], bulk.at[INTO, 1, 0],
                       team.member(lax.rem(team.p + F, B * F))).start()

    def pass_over(kind, way, c, i):
        if kind[5] != 0:
            return
        at = chunk_rows(kind, way, c)
        to, place, rows = hand1(way, c, at)

        @pl.when(to == f)
        def _():
            for d in range(1, F):
                source = lax.rem(f + d, F)
                ref = out1.at[source * B + y, rows]
                remote(fin1.at[at], ref, bulk.at[HAND, 0, 0], hand_recv.at[source, lax.div(place, step1)],
                       team.same_row(f)).wait_recv()
                if B == 2:
                    remote(ref, ref, bulk.at[OVER, 0, 1], bulk.at[INTO, 0, 0],
                           team.member(lax.rem(team.p + F, B * F))).start()

    @pl.loop(0, total + 2 * HOP * (T - 1) + LAG)
    def _(s):
        for way in range(2):
            place = T - 1 - t if way else t
            sent = s - HOP * place
            done = s - HOP * (2 * (T - 1) - place)
            each(sent, way, reduce)
            each(done, way, finish)
            each(done - LAG, way, pass_over)

    def drain(ref, sem):
        pltpu.make_async_copy(ref, ref, sem).wait()

    for way in range(2):
        for g, land, fin, step, half, k in kinds:

            @pl.when(jnp.logical_not(is_last(way)))
            def _():
                drain(g.at[pl.ds(0, half)], bulk.at[RED, k, way])

            @pl.when(jnp.logical_not(is_first(way)))
            def _():
                drain(g.at[pl.ds(0, half)], bulk.at[FIN, k, way])

    drain(g1.at[pl.ds(0, depth - shard)], bulk.at[HAND, 0, 0])
    drain(g1.at[pl.ds(0, shard)], bulk.at[HOME, 0, 0])
    drain(g2, bulk.at[HOME, 1, 0])
    if B == 2:
        drain(g1.at[pl.ds(0, shard)], bulk.at[OVER, 0, 0])
        drain(g1.at[pl.ds(0, depth - shard)], bulk.at[OVER, 0, 1])
        drain(g2, bulk.at[OVER, 1, 0])
        drain(g1, bulk.at[INTO, 0, 0])
        drain(g2, bulk.at[INTO, 1, 0])


def sum_grads(dims, g1, g2):
    B, F, T = dims
    depth = g1.shape[0]
    shard = depth // F
    step1, step2 = 32, 48
    chunks = depth // 2 // step1 + g2.shape[0] // 2 // step2
    return pl.pallas_call(
        functools.partial(grads_load_kernel, dims, step1, step2),
        out_shape=(
            jax.ShapeDtypeStruct((B * F, shard, g1.shape[1]), BF16),
            jax.ShapeDtypeStruct((B,) + g2.shape, BF16),
        ),
        in_specs=[ANY] * 2,
        out_specs=[ANY] * 2,
        scratch_shapes=[
            pltpu.VMEM(g1.shape, BF16),
            pltpu.VMEM(g2.shape, BF16),
            pltpu.VMEM(g1.shape, BF16),
            pltpu.VMEM(g2.shape, BF16),
            pltpu.VMEM(g1.shape, BF16),
            pltpu.VMEM(g2.shape, BF16),
            pltpu.SemaphoreType.DMA((2, chunks)),
            pltpu.SemaphoreType.DMA((2, chunks)),
            pltpu.SemaphoreType.DMA((F, shard // step1)),
            pltpu.SemaphoreType.DMA((7, 2, 2)),
            pltpu.SemaphoreType.DMA((2,)),
        ],
        compiler_params=kernel_params(7),
        name="sum_grads",
    )(g1, g2)


def grads_load_kernel(dims, step1, step2, g1, g2, out1, out2, own1, own2, *rest):
    local = rest[-1]
    loads = [pltpu.make_async_copy(g1, own1, local.at[0]), pltpu.make_async_copy(g2, own2, local.at[1])]
    for load in loads:
        load.start()
    for load in loads:
        load.wait()
    grads_kernel(dims, step1, step2, own1, own2, out1, out2, *rest[:-1])


def doc_layout(lengths, token_index):
    doc_ends = jnp.cumsum(lengths)
    passed = token_index[:, None] >= doc_ends[None, :]
    document_index = jnp.sum(passed.astype(jnp.int32), axis=1)
    doc_start = jnp.max(jnp.where(passed, doc_ends[None, :], 0), axis=1)
    return (document_index, token_index - doc_start)


def rotation(places, width):
    half_width = width // 2
    inverse_freq = jnp.power(ROPE_BASE, -(jnp.arange(half_width, dtype=F32) * 2.0 / width))
    angles = places.astype(F32)[:, None] * inverse_freq[None, :]
    cosine_values = jnp.cos(angles)
    sine_lookup = jnp.sin(angles)
    return (
        jnp.concatenate([cosine_values, cosine_values], 1),
        jnp.concatenate([sine_lookup, sine_lookup], 1),
    )


def apply_rotary(values_in, cosine_values, sine_lookup, sign):
    half_width = values_in.shape[-1] // 2
    swapped = jnp.concatenate([-values_in[..., half_width:], values_in[..., :half_width]], -1)
    return values_in * cosine_values + swapped * (sine_lookup * sign)


def scaled_input(values_in):
    factor = lax.rsqrt(jnp.mean(values_in * values_in, -1, keepdims=True) + EPSILON)
    return (values_in * factor, factor)


def norm_back(upstream, unit_rows, factor, gain_row):
    lifted = upstream * gain_row
    return factor * (lifted - unit_rows * jnp.mean(lifted * unit_rows, -1, keepdims=True))


def dot(a, b, dims=((1,), (0,))):
    return lax.dot_general(a, b, (dims, ((), ())), preferred_element_type=F32)


def in_three(values):
    high = lax.reduce_precision(values, 8, 7)
    rest = values - high
    middle = lax.reduce_precision(rest, 8, 7)
    return high.astype(BF16), middle.astype(BF16), (rest - middle).astype(BF16)


def on_device(
    tokens, lengths, wq, wk, wv, wo, w_gate, w_up, w_down, attn_gain, ffn_gain, q_gain, key_norm_gain, cotangent
):
    F = lax.axis_size("fsdp")
    B = KEY_VALUE_HEADS // F
    T = lax.axis_size("ctx") // B
    dims = (B, F, T)
    own_rows, width = tokens.shape
    rows = own_rows * KEY_VALUE_HEADS
    depth = width // F
    ctx, f = lax.axis_index("ctx"), lax.axis_index("fsdp")
    t, y = ctx // B, ctx % B
    p = y * F + f
    hidden = w_down.shape[0] // B

    gains = jnp.zeros((16, max(depth, LANES)), BF16)
    gains = gains.at[0, :depth].set(attn_gain).at[1, :depth].set(ffn_gain)
    gains = gains.at[2, : HEAD_SIZE // F].set(q_gain).at[3, : HEAD_SIZE // F].set(key_norm_gain)
    tok_full, wqkv, gains_full, gate_cut, up_cut = gather_inputs(dims, tokens, wq, wk, wv, gains, w_gate, w_up)
    gains_full = gains_full.astype(F32)
    gain_attn = gains_full[:, 0, :depth].reshape(-1)
    gain_ffn = gains_full[:, 1, :depth].reshape(-1)
    gain_query = gains_full[:, 2, : HEAD_SIZE // F].reshape(-1)
    gain_key = gains_full[:, 3, : HEAD_SIZE // F].reshape(-1)
    wqkv = wqkv.reshape(width, -1)

    token_index = t * rows + jnp.arange(rows, dtype=jnp.int32)
    docs, places = doc_layout(lengths, token_index)
    cosine_values, sine_lookup = rotation(places, HEAD_SIZE)
    cosine_values, sine_lookup = cosine_values[None], sine_lookup[None]
    ends = jnp.cumsum(lengths)
    ndocs = lengths.shape[0]
    big = jnp.int32(2**30)
    spans = jnp.stack([
        jnp.zeros((LANES,), jnp.int32).at[HEAD_SIZE : HEAD_SIZE + ndocs].set(ends - lengths),
        jnp.full((LANES,), big, jnp.int32).at[HEAD_SIZE : HEAD_SIZE + ndocs].set(ends),
    ])
    spans = jnp.concatenate([spans, jnp.zeros((6, LANES), jnp.int32)])

    inputs = tok_full.reshape(rows, width).astype(F32)
    unit_attn, factor_attn = scaled_input(inputs)
    normed = (unit_attn * gain_attn).astype(BF16)
    projected = dot(normed, wqkv)
    heads = jnp.transpose(projected.reshape(rows, GROUP + 2, HEAD_SIZE), (1, 0, 2))
    q_unit, q_factor = scaled_input(heads[:GROUP])
    k_unit, k_factor = scaled_input(heads[GROUP])
    queries = apply_rotary(q_unit * gain_query, cosine_values, sine_lookup, 1.0).astype(BF16)
    own_keys = apply_rotary(k_unit * gain_key, cosine_values[0], sine_lookup[0], 1.0).astype(BF16)
    own_values = heads[GROUP + 1].astype(BF16)
    scale = HEAD_SIZE ** (-0.5)
    apart = jnp.where(docs[:, None] == jnp.arange(ndocs)[None, :], 0.0, -APART).astype(BF16)
    apart = jnp.broadcast_to(apart[None], (GROUP, rows, ndocs))
    queries = (queries * jnp.asarray(scale, BF16)).astype(BF16)
    qx = jnp.concatenate([queries, apart, jnp.zeros((GROUP, rows, LANES - HEAD_SIZE - ndocs), BF16)], -1)
    kv = jnp.concatenate([own_keys, own_values], -1)
    kv_all, acc, mixed, dy_full, wo_full, gate_w, up_w = attend(
        dims, qx, kv, spans, cotangent, wo, gate_cut, up_cut
    )
    sums = acc[..., HEAD_SIZE : HEAD_SIZE + 1]
    out = acc[..., :HEAD_SIZE] / sums
    log_sums = jnp.log(sums)

    both = mixed[:, :rows].reshape(B, F, rows, 2 * HEAD_SIZE)
    third = mixed[:, rows:].reshape(B, F, rows // 2, 2, HEAD_SIZE)
    third = jnp.swapaxes(third, 2, 3).reshape(B, F, rows, HEAD_SIZE)
    mixed_heads = jnp.concatenate([both, third], -1)
    mixed_heads = jnp.transpose(mixed_heads, (2, 1, 0, 3)).reshape(rows, QUERY_HEADS * HEAD_SIZE)
    own_mixed = jnp.transpose(out, (1, 0, 2)).reshape(rows, QW).astype(BF16)
    wo_full = wo_full.reshape(-1, width)
    gate_w = gate_w.reshape(width, hidden)
    up_w = up_w.reshape(width, hidden)
    down_w = lax.dynamic_slice_in_dim(w_down, y * hidden, hidden, 0)
    own_wo = lax.dynamic_slice_in_dim(wo, y * QW, QW, 0)
    dy_full = dy_full.reshape(rows, width)

    resid = inputs + dot(mixed_heads, wo_full)
    unit_ffn, factor_ffn = scaled_input(resid)
    hidden_in = (unit_ffn * gain_ffn).astype(BF16)
    gate = dot(hidden_in, gate_w)
    upper = dot(hidden_in, up_w)
    sigma = jax.nn.sigmoid(gate)
    silu_gate = gate * sigma
    act_rows = (silu_gate * upper).astype(BF16)
    down_out = dot(act_rows, down_w).astype(BF16)

    grad_act = dot(dy_full, down_w, ((1,), (1,)))
    grad_gate = (grad_act * upper * sigma * (1.0 + gate * (1.0 - sigma))).astype(BF16)
    grad_upper = (grad_act * silu_gate).astype(BF16)
    grad_hidden = (dot(grad_gate, gate_w, ((1,), (1,))) + dot(grad_upper, up_w, ((1,), (1,)))).astype(BF16)
    own_grad_hidden = team_scatter(dims, grad_hidden, 3)

    own_at = lambda a: lax.dynamic_slice_in_dim(a, p * own_rows, own_rows, 0)
    own_resid = own_at(resid)
    own_unit, own_factor = scaled_input(own_resid)
    ffn_gain_term = jnp.sum(own_grad_hidden * own_unit, 0)
    grad_resid = cotangent.astype(F32) + norm_back(own_grad_hidden, own_unit, own_factor, gain_ffn)
    grad_attn = team_gather(dims, grad_resid.astype(BF16), 4)

    grad_mixed = dot(grad_attn, own_wo, ((1,), (1,))).astype(BF16)
    grad_mixed = jnp.transpose(grad_mixed.reshape(rows, GROUP, HEAD_SIZE), (1, 0, 2))
    delta = jnp.sum(grad_mixed.astype(F32) * out, -1, keepdims=True)
    zeros = lambda n: jnp.zeros((GROUP, rows, n), BF16)
    qx_back = jnp.concatenate(
        [queries, apart, *in_three(-log_sums), zeros(LANES - HEAD_SIZE - ndocs - 3)], -1
    )
    dox = jnp.concatenate([grad_mixed, *in_three(-delta), zeros(LANES - HEAD_SIZE - 3)], -1)
    dq, dkv = attend_back(dims, qx_back, dox, kv_all, spans)
    dkv, down_sum = keys_back(dims, dkv, down_out)
    layer_out = (own_resid + down_sum).astype(BF16)

    query_turned = apply_rotary(dq[..., :HEAD_SIZE] * scale, cosine_values, sine_lookup, -1.0)
    key_turned = apply_rotary(dkv[:, :HEAD_SIZE], cosine_values[0], sine_lookup[0], -1.0)
    q_gain_term = jnp.sum(query_turned * q_unit, (0, 1))
    k_gain_term = jnp.sum(key_turned * k_unit, 0)
    grad_q = norm_back(query_turned, q_unit, q_factor, gain_query)
    grad_k = norm_back(key_turned, k_unit, k_factor, gain_key)
    grad_heads = jnp.concatenate([grad_q, grad_k[None], dkv[None, :, HEAD_SIZE:]], 0).astype(BF16)
    grad_heads = jnp.transpose(grad_heads, (1, 0, 2)).reshape(rows, QW + 2 * HEAD_SIZE)
    grad_normed = dot(grad_heads, wqkv, ((1,), (1,))).astype(BF16)
    own_grad_normed = team_scatter(dims, grad_normed, 6)
    own_unit, own_factor = scaled_input(tokens.astype(F32))
    attn_gain_term = jnp.sum(own_grad_normed * own_unit, 0)
    tokens_grad = (grad_resid + norm_back(own_grad_normed, own_unit, own_factor, gain_attn)).astype(BF16)

    over_rows = ((0,), (0,))
    g1 = jnp.concatenate(
        [
            dot(hidden_in, grad_gate, over_rows).astype(BF16),
            dot(hidden_in, grad_upper, over_rows).astype(BF16),
            dot(normed, grad_heads, over_rows).astype(BF16),
        ],
        1,
    )
    g2 = jnp.concatenate(
        [dot(act_rows, dy_full, over_rows).astype(BF16), dot(own_mixed, grad_attn, over_rows).astype(BF16)], 0
    )
    out1, out2 = sum_grads(dims, g1, g2)

    gain_terms = jnp.concatenate([attn_gain_term, ffn_gain_term, q_gain_term, k_gain_term])
    gain_sums = lax.psum(gain_terms, ("ctx", "fsdp"))
    take = lambda a, n: lax.dynamic_slice_in_dim(a, f * n, n, 0)
    attn_gain_grad = take(gain_sums[:width], depth)
    ffn_gain_grad = take(gain_sums[width : 2 * width], depth)
    q_gain_grad = take(gain_sums[2 * width : 2 * width + HEAD_SIZE], HEAD_SIZE // F)
    k_gain_grad = take(gain_sums[2 * width + HEAD_SIZE :], HEAD_SIZE // F)

    def columns(first, count):
        return jnp.transpose(out1[:, :, first : first + count], (1, 0, 2)).reshape(depth, -1).astype(F32)

    down_grad = out2[:, :hidden].reshape(-1, width).astype(F32)
    wo_grad = out2[:, hidden:].reshape(-1, width).astype(F32)
    gate_grad = columns(0, hidden)
    up_grad = columns(hidden, hidden)
    wq_grad = columns(2 * hidden, QW)
    wk_grad = columns(2 * hidden + QW, HEAD_SIZE)
    wv_grad = columns(2 * hidden + QW + HEAD_SIZE, HEAD_SIZE)
    return (
        layer_out, tokens_grad, wq_grad, wk_grad, wv_grad, wo_grad, gate_grad, up_grad, down_grad,
        attn_gain_grad, ffn_gain_grad, q_gain_grad, k_gain_grad,
    )


def solution(mesh):
    rows = P(("ctx", "fsdp"), None)
    shard = P("fsdp", None)
    gain = P("fsdp")
    return jax.shard_map(
        on_device,
        mesh=mesh,
        in_specs=(rows, P(), shard, shard, shard, shard, shard, shard, shard, gain, gain, gain, gain, rows),
        out_specs=(rows, rows, shard, shard, shard, shard, shard, shard, shard, gain, gain, gain, gain),
        check_vma=False,
    )
```

time: 2560 us -> 897 us (0.35)
  waiting for transfers between devices: 2000 us -> 0 us
  Pallas kernels: 0 us -> 523 us
  matrix products: 198 us -> 76 us
  starting transfers between devices: 115 us -> 0 us
  local copies, waits for them, and re-layouts: 47.3 us -> 132 us
  other arithmetic: 107 us -> 80.1 us
    reduce_scatter x8 -> x0, waiting for transfers between devices: 619 us -> none  [the longest x1 157 us: on_device(): lax.psum_scatter(gate_term.astype(jnp.bfloat16), 'fsdp', scatter_dimensio...]
    psum x1 -> x0, waiting for transfers between devices: 530 us -> none  [on_device(): lax.psum(wq_part.astype(jnp.bfloat16), 'ctx').astype(jnp.float32)]
    pallas_call x0 -> x8, Pallas kernels: none -> 523 us  [the longest x1 232 us: sum_grads(): pl.pallas_call(functools.partial(grads_load_kernel, dims, step1, step2),...]
    all_gather x9 -> x0, waiting for transfers between devices: 499 us -> none  [the longest x1 122 us: on_device(): lax.all_gather(w_down, 'fsdp', axis=0, tiled=True)]
    ppermute x16 -> x0, waiting for transfers between devices: 345 us -> none  [the longest x8 311 us: passed_along(): return lax.ppermute(block, axis, route)]
    dot_general x28 -> x15, matrix products: 198 us -> 76 us  [dot(): return lax.dot_general(a, b, (dims, ((), ())), preferred_element_type=F32)]
    ppermute x16 -> x0, starting transfers between devices: 114 us -> none  [the longest x8 66.6 us: passed_along_2(): return lax.ppermute(array, axis, pairs)]
    psum x1, blocking collectives: 22.8 us -> 73.5 us  [on_device(): gain_sums = lax.psum(gain_terms, ('ctx', 'fsdp'))]
  transfers between devices with their start and end apart: 34 -> 0, of which waited for: 25 -> 0; matrix products, arithmetic and copies ran while one was open for 9% -> 0% of each run, Pallas kernels for 0% -> 0%
where the time goes in v1:
time: 897 us; the launch traced here: 886 us
  Pallas kernels  523 us (58%)
  local copies, waits for them, and re-layouts  132 us (15%)
  other arithmetic  80.1 us (9%)
  matrix products  76 us (8%)
  blocking collectives  73.5 us (8%)
    pallas_call x1, Pallas kernels, sum_grads(): pl.pallas_call(functools.partial(grads_load_kernel, dims, step1, step2),...  232 us
    pallas_call x1, Pallas kernels, attend(): pl.pallas_call(functools.partial(attend_kernel, dims), out_shape=(jax.Sha...  122 us
    dot_general x15, matrix products, dot(): return lax.dot_general(a, b, (dims, ((), ())), preferred_element_type=F32)  76 us
    psum x1, blocking collectives, on_device(): gain_sums = lax.psum(gain_terms, ('ctx', 'fsdp'))  73.5 us
    pallas_call x1, Pallas kernels, keys_back(): pl.pallas_call(functools.partial(keys_back_kernel, dims), out_shape=(jax....  57.9 us
    pallas_call x2, Pallas kernels, team_scatter(): pl.pallas_call(functools.partial(scatter_kernel, dims), out_shape=jax.Sha...  47 us
    pallas_call x1, Pallas kernels, gather_inputs(): pl.pallas_call(functools.partial(inputs_kernel, dims), out_shape=(jax.Sha...  33.4 us
    unnamed x77, local copies, waits for them, and re-layouts  30.6 us

profile of v1, /device:TPU:0, one launch (start us, length us, event | category | flops | bytes accessed | tf_op | source)
XLA Modules:
  0.0 886.1 jit_solution(8699092557374984532)
XLA Ops:
  4.2 33.4 %gather_inputs.1 = (bf16[8,128,1536]{2,1,0:T(8,128)(2,1)}, bf16[4,384,320]{2,1,0:T(8,128)(2,1)}, bf16[4,16,384]{2,1,0:T(8,128)(2,1)}, bf16[4,384,864]{2,1,0:T(8,128)(2,1)}, bf16[4,384,864]{2,1,0:T(8,128)(2,1)}) custom-call(bf16[128,1536]{1,0:T(8,128)(2,1)} %tokens.1, bf16[384,1536]{1,0:T(8,128)(2,1)} %wq.1, bf16[384,512]{1,0:T(8,128)(2,1)} %wk.1, ...), custom_call_target="tpu_custom_call" | custom-call | tf_op jit(solution)/shard_map/gather_inputs/pallas_call | solution.py:294
  45.2 4.8 convolution_bitcast_fusion
  64.3 122.3 %attend.1 = (bf16[4,1024,128]{2,1,0:T(8,128)(2,1)}, f32[3,1024,128]{2,1,0:T(8,128)}, bf16[8,1536,128]{2,1,0:T(8,128)(2,1)}, bf16[8,128,1536]{2,1,0:T(8,128)(2,1)...) custom-call(bf16[3,1024,128]{2,1,0:T(8,128)(2,1)} %maximum_maximum_fusion.qx, ...), custom_call_target="tpu_custom_call" | custom-call | tf_op jit(solution)/shard_map/attend/pallas_call | solution.py:458
  191.0 5.7 concatenate.73.qx
  210.2 3.9 copy.84
  216.9 9.7 %multiply_reduce_fusion = (f32[1024]{0:T(1024)S(1)}, f32[1024,1536]{1,0:T(8,128)}) fusion(bf16[1024,1536]{0,1:T(8,128)(2,1)S(1)} %bitcast.127, bf16[1536,1536]{1,0:T(8,128)(2,1)} %bitcast.146, bf16[8,128,1536]{2,1,0:T(8,128)(2,1)S(1)} %copy-done.1), kind=kOutput, calls=%fused_computation.5 | convolution fusion | flops 4838128640 | bytes 17305600 | tf_op jit(solution)/shard_map/dot_general | solution.py:932
  230.3 4.9 fusion.43
  235.1 5.8 fusion.2
  241.0 5.8 multiply_convert_fusion.2
  250.3 4.9 add_convert_fusion
  255.2 24.4 %team_scatter.2 = f32[128,1536]{1,0:T(8,128)} custom-call(bf16[2,2,2,128,1536]{4,3,2,1,0:T(8,128)(2,1)} %bitcast.133), custom_call_target="tpu_custom_call" | custom-call | tf_op jit(solution)/shard_map/team_scatter/pallas_call | solution.py:565
  286.0 18.8 %team_gather.1 = bf16[8,128,1536]{2,1,0:T(8,128)(2,1)} custom-call(bf16[128,1536]{1,0:T(8,128)(2,1)} %fusion.37.x), custom_call_target="tpu_custom_call" | custom-call | tf_op jit(solution)/shard_map/team_gather/pallas_call | solution.py:594
  322.9 5.5 concatenate.74.dox
  328.3 10.9 %attend_back.1 = (f32[3,1024,128]{2,1,0:T(8,128)}, bf16[4,1024,128]{2,1,0:T(8,128)(2,1)}) custom-call(bf16[3,1024,128]{2,1,0:T(8,128)(2,1)} %concatenate.73.qx, bf16[3,1024,128]{2,1,0:T(8,128)(2,1)} %concatenate.74.dox, bf16[4,1024,128]{2,1,0:T(8,128)(2,1)} %get-tuple-element.114.kv_all, s32[8,128]{1,0:T(8,128)} %fusion.32.spans), custom_call_target="tpu_custom_call" | custom-call | tf_op jit(solution)/shard_map/attend_back/pallas_call | solution.py:533
  339.3 7.4 convolution_convert_fusion.1
  346.7 57.9 %keys_back.1 = (f32[1024,128]{1,0:T(8,128)}, f32[128,1536]{1,0:T(8,128)}) custom-call(bf16[4,1024,128]{2,1,0:T(8,128)(2,1)} %get-tuple-element.115.dkv, bf16[2,2,2,128,1536]{4,3,2,1,0:T(8,128)(2,1)} %bitcast.128), custom_call_target="tpu_custom_call" | custom-call | tf_op jit(solution)/shard_map/keys_back/pallas_call | solution.py:650
  414.5 4.6 convolution_convert_fusion
  419.1 22.6 %team_scatter.3 = f32[128,1536]{1,0:T(8,128)} custom-call(bf16[2,2,2,128,1536]{4,3,2,1,0:T(8,128)(2,1)} %bitcast.134), custom_call_target="tpu_custom_call" | custom-call | tf_op jit(solution)/shard_map/team_scatter/pallas_call | solution.py:565
  446.2 4.2 convolution_convert_fusion.3
  450.3 4.6 copy.92
  454.9 6.0 convolution_convert_fusion.2
  461.0 4.5 copy.93
  469.3 11.3 %concatenate.78.g1 = bf16[1536,2048]{1,0:T(8,128)(2,1)} concatenate(bf16[1536,864]{1,0:T(8,128)(2,1)} %copy.92, bf16[1536,864]{1,0:T(8,128)(2,1)} %copy.93, bf16[1536,320]{1,0:T(8,128)(2,1)S(1)} %copy.94), dimensions={1} | concatenate | bytes 12582912 | tf_op jit(solution)/shard_map/concatenate | solution.py:1067
  483.7 4.6 convolution_convert_fusion.4
  490.2 232.5 %sum_grads.1 = (bf16[8,384,2048]{2,1,0:T(8,128)(2,1)}, bf16[2,1056,1536]{2,1,0:T(8,128)(2,1)}) custom-call(bf16[1536,2048]{1,0:T(8,128)(2,1)} %concatenate.78.g1, bf16[1056,1536]{1,0:T(8,128)(2,1)} %pad_maximum_fusion.g2), custom_call_target="tpu_custom_call" | custom-call | tf_op jit(solution)/shard_map/sum_grads/pallas_call | solution.py:859
  741.6 12.2 %convert_bitcast_fusion = (f32[384,8,864]{2,0,1:T(8,128)}, f32[384,8,864]{2,0,1:T(8,128)}) fusion(bf16[8,384,2048]{2,1,0:T(8,128)(2,1)} %get-tuple-element.119), kind=kLoop, calls=%fused_computation | loop fusion | flops 5308416 | bytes 31850496 | tf_op jit(solution)/shard_map/convert_element_type | solution.py:1089
  753.8 12.0 %copy.99 = f32[384,8,864]{0,2,1:T(8,128)} copy(f32[384,8,864]{2,0,1:T(8,128)} %get-tuple-element.179) | data formatting | bytes 21233664 | tf_op jit(solution)/shard_map/convert_element_type | solution.py:1089
  765.8 11.6 %copy.104 = f32[384,6912]{1,0:T(8,128)} copy(f32[384,6912]{0,1:T(8,128)} %bitcast.119) | data formatting | bytes 21233664
  777.4 12.0 %copy.100 = f32[384,8,864]{0,2,1:T(8,128)} copy(f32[384,8,864]{2,0,1:T(8,128)} %get-tuple-element.178) | data formatting | bytes 21233664 | tf_op jit(solution)/shard_map/convert_element_type | solution.py:1089
  789.3 11.6 %copy.105 = f32[384,6912]{1,0:T(8,128)} copy(f32[384,6912]{0,1:T(8,128)} %bitcast.120) | data formatting | bytes 21233664
  803.8 6.0 bitcast_convert_fusion
  809.8 73.5 %psum.7 = f32[3200]{0:T(1024)S(1)} all-reduce(f32[3200]{0:T(1024)S(1)} %concatenate.80), channel_id=1, replica_groups=mesh['ctx'=8,'fsdp'=4] {'ctx','fsdp'}, use_global_device_ids=true, to_apply=%region_18.19 | all-reduce | flops 3200 | bytes 25600 | tf_op jit(solution)/shard_map/psum | solution.py:1081
  (181 shorter events, 124.7 us)
Async XLA Ops:
  38.5 2.8 copy-start
  41.3 2.5 copy-start.21
  51.0 2.2 copy-start.30
  56.5 2.9 copy-start.9
  57.2 2.2 copy-start.6
  57.2 2.2 copy-start.7
  214.1 2.8 copy-start.1
  226.7 3.6 copy-start.28
  230.2 4.9 copy-start.15
  235.1 5.8 copy-start.16
  235.1 5.8 copy-start.27
  235.1 5.8 copy-start.33
  241.0 5.8 copy-start.29
  246.7 3.5 copy-start.31
  246.8 3.5 copy-start.34
  279.6 4.2 copy-start.2
  279.6 4.2 copy-start.13
  346.7 60.6 %copy-start.10 = (f32[1024,32]{1,0:T(8,128)S(1)}, f32[1024,32]{1,0:T(8,128)}, u32[]{:S(2)}) copy-start(f32[1024,32]{1,0:T(8,128)} %copy-done.9) | copy-start | bytes 393220
  346.7 60.7 %copy-start.12 = (f32[1024,32]{1,0:T(8,128)S(1)}, f32[1024,32]{1,0:T(8,128)}, u32[]{:S(2)}) copy-start(f32[1024,32]{1,0:T(8,128)} %get-tuple-element.213) | copy-start | bytes 393220
  404.6 2.7 copy-start.4
  407.3 1.4 copy-start.5
  408.8 1.2 copy-start.20
  412.9 1.6 copy-start.22
  419.1 22.7 %copy-start.8 = (bf16[128,1536]{1,0:T(8,128)(2,1)S(1)}, bf16[128,1536]{1,0:T(8,128)(2,1)}, u32[]{:S(2)}) copy-start(bf16[128,1536]{1,0:T(8,128)(2,1)} %tokens.1) | copy-start | bytes 1179652
  419.1 24.3 %copy-start.14 = (bf16[128,1536]{1,0:T(8,128)(2,1)S(1)}, bf16[128,1536]{1,0:T(8,128)(2,1)}, u32[]{:S(2)}) copy-start(bf16[128,1536]{1,0:T(8,128)(2,1)} %dy.1) | copy-start | bytes 1179652
  419.1 24.3 %copy-start.23 = (f32[128,1536]{1,0:T(8,128)S(1)}, f32[128,1536]{1,0:T(8,128)}, u32[]{:S(2)}) copy-start(f32[128,1536]{1,0:T(8,128)} %get-tuple-element.116) | copy-start | bytes 2359300
  441.8 4.4 copy-start.32
  443.4 2.8 copy-start.17
  450.3 4.6 copy-start.35
  461.0 4.5 copy-start.24
  469.3 11.3 %copy-start.18 = (bf16[1024,3,64]{2,0,1:T(8,128)(2,1)S(1)}, bf16[1024,3,64]{2,0,1:T(8,128)(2,1)}, u32[]{:S(2)}) copy-start(bf16[1024,3,64]{2,0,1:T(8,128)(2,1)} %get-tuple-element.189) | copy-start | bytes 1179652
  480.9 2.8 copy-start.26
  (4 other events, 3.7 us)

commit v2 on v1

v2 whole, which is shorter than its diff:
```python
import functools

import jax
import jax.numpy as jnp
from jax import lax
from jax.experimental import pallas as pl
from jax.experimental.pallas import tpu as pltpu
from jax.sharding import PartitionSpec as P

QUERY_HEADS = 24
KEY_VALUE_HEADS = 8
HEAD_SIZE = 64
GROUP = QUERY_HEADS // KEY_VALUE_HEADS
QW = GROUP * HEAD_SIZE
LANES = 128
NDOCS = 4

EPSILON = 1e-05
ROPE_BASE = 1000000.0
APART = 16384.0

MESH = pl.DeviceIdType.MESH
F32 = jnp.float32
BF16 = jnp.bfloat16
ANY = pl.BlockSpec(memory_space=pl.ANY)
VMEM = pl.BlockSpec(memory_space=pltpu.VMEM)
VMEM_LIMIT = 56 * 1024 * 1024


class Team:
    def __init__(self, B, F, T):
        self.B, self.F, self.T = B, F, T
        ctx, self.f = lax.axis_index("ctx"), lax.axis_index("fsdp")
        self.t, self.y = lax.div(ctx, B), lax.rem(ctx, B)
        self.p = self.y * F + self.f

    def member(self, p):
        return (self.t * self.B + lax.div(p, self.F), lax.rem(p, self.F))

    def same_row(self, f):
        return (self.t * self.B + self.y, f)

    def other_team(self, t):
        return (t * self.B + self.y, self.f)


def flip(p, bit):
    return p + bit * (1 - 2 * lax.rem(lax.div(p, bit), 2))


def bit_of(p, bit):
    return lax.rem(lax.div(p, bit), 2)


class Sems:
    def __init__(self, send, recv):
        self.send, self.recv, self.used = send, recv, 0

    def copy(self, src, dst, device):
        i = self.used
        self.used += 1
        return pltpu.make_async_remote_copy(
            src_ref=src,
            dst_ref=dst,
            send_sem=self.send.at[i],
            recv_sem=self.recv.at[i],
            device_id=device,
            device_id_type=MESH,
        )


def greet(devices):
    barrier = pltpu.get_barrier_semaphore()
    for device in devices:
        pl.semaphore_signal(barrier, inc=1, device_id=device, device_id_type=MESH)
    pl.semaphore_wait(barrier, len(devices))


def team_peers(team):
    n = team.B * team.F
    return [team.member(lax.rem(team.p + d, n)) for d in range(1, n)]


def line_peers(team):
    return [team.other_team(lax.rem(team.t + d, team.T)) for d in range(1, team.T)]


def row_peers(team):
    return [team.same_row(lax.rem(team.f + d, team.F)) for d in range(1, team.F)]


class Gather:
    def __init__(self, sems, me, count, device, own, block, half):
        bits = count.bit_length() - 1
        one, two = flip(me, 1), flip(me, 2)
        send = lambda src, dst, to: sems.copy(src, dst, device(to))
        again = lambda ref, to: send(ref, ref, to)
        self.first = [send(own, block(me), flip(me, 1 << k)) for k in range(bits)]
        self.over = [again(block(two), one)]
        self.halves, self.corner = [], []
        if count == 8:
            four = flip(me, 4)
            far = flip(two, 4)
            self.over.append(again(block(four), one))
            self.halves = [again(half(two, 0), four), again(half(four, 1), two)]
            self.corner = [again(half(far, 0), one), again(half(far, 1), one)]

    def begin(self):
        for copy in self.first:
            copy.start()

    def relay(self):
        self.first[1].wait_recv()
        self.over[0].start()
        if self.halves:
            self.halves[0].start()
            self.first[2].wait_recv()
            self.over[1].start()
            self.halves[1].start()

    def end(self):
        for arrived, onward in zip(self.halves, self.corner):
            arrived.wait_recv()
            onward.start()
        self.first[0].wait_recv()
        for copy in self.over + self.corner:
            copy.wait_recv()
        for copy in self.first + self.over + self.halves + self.corner:
            copy.wait_send()

    COPIES = 9


def scatter_shapes(rows, width):
    half = width // 2
    return [
        pltpu.VMEM((2, 2, rows, width), BF16),
        pltpu.VMEM((2, rows, half), BF16),
        pltpu.VMEM((2, rows, half), BF16),
        pltpu.VMEM((2, rows, half), BF16),
        pltpu.VMEM((2, rows, half), BF16),
        pltpu.VMEM((rows, half), BF16),
        pltpu.VMEM((rows, half), BF16),
        pltpu.VMEM((rows, half), BF16),
        pltpu.VMEM((rows, half), BF16),
    ]


def wide(v):
    return v.astype(F32)


class Scatter:
    COPIES = 5

    def __init__(self, sems, team, x, scratch):
        self.x, self.scratch = x, scratch
        r0, s1l, s1r, r1l, r1r, s2l, s2r, r2l, r2r = scratch
        p = team.p
        self.b = b0, b1, b2 = bit_of(p, 1), bit_of(p, 2), bit_of(p, 4)
        width = x.shape[-1]
        self.left, self.right = pl.ds(0, width // 2), pl.ds(width // 2, width // 2)
        send = lambda src, dst, bit: sems.copy(src, dst, team.member(flip(p, bit)))
        self.first = send(x.at[:, :, 1 - b0], r0, 1)
        self.l1, self.r1 = send(s1l, r1l, 2), send(s1r, r1r, 4)
        self.l2, self.r2 = send(s2l, r2l, 4), send(s2r, r2r, 2)

    def begin(self):
        self.first.start()

    def relay(self):
        x, (r0, s1l, s1r, *_), (b0, b1, b2) = self.x, self.scratch, self.b
        left, right, n1, n2 = self.left, self.right, 1 - b1, 1 - b2
        self.first.wait_recv()
        for k in range(2):
            s1l[k] = (wide(x[k, n1, b0, :, left]) + wide(r0[k, n1, :, left])).astype(BF16)
        self.l1.start()
        for k in range(2):
            s1r[k] = (wide(x[n2, k, b0, :, right]) + wide(r0[n2, k, :, right])).astype(BF16)
        self.r1.start()

    def relay_again(self):
        x, (r0, s1l, s1r, r1l, r1r, s2l, s2r, r2l, r2r), (b0, b1, b2) = self.x, self.scratch, self.b
        left, right, n1, n2 = self.left, self.right, 1 - b1, 1 - b2
        self.l1.wait_recv()
        s2l[...] = (wide(x[n2, b1, b0, :, left]) + wide(r0[n2, b1, :, left]) + wide(r1l[n2])).astype(BF16)
        self.l2.start()
        self.r1.wait_recv()
        s2r[...] = (wide(x[b2, n1, b0, :, right]) + wide(r0[b2, n1, :, right]) + wide(r1r[n1])).astype(BF16)
        self.r2.start()

    def end(self, store):
        x, (r0, s1l, s1r, r1l, r1r, s2l, s2r, r2l, r2r), (b0, b1, b2) = self.x, self.scratch, self.b
        left, right = self.left, self.right
        self.l2.wait_recv()
        store(
            left,
            wide(x[b2, b1, b0, :, left]) + wide(r0[b2, b1, :, left]) + wide(r1l[b2]) + wide(r2l[...]),
        )
        self.r2.wait_recv()
        store(
            right,
            wide(x[b2, b1, b0, :, right]) + wide(r0[b2, b1, :, right]) + wide(r1r[b1]) + wide(r2r[...]),
        )
        for copy in (self.first, self.l1, self.r1, self.l2, self.r2):
            copy.wait_send()


def kernel_params(collective_id):
    return pltpu.CompilerParams(
        collective_id=collective_id, has_side_effects=True, vmem_limit_bytes=VMEM_LIMIT
    )


def inputs_kernel(dims, tokens, wq, wk, wv, gains, w_gate, w_up, tok_full, wqkv, gains_full, gate_cut, up_cut,
                  q_in, k_in, v_in, qkv_cut, slab_g, slab_u, cut_g, cut_u, send, recv, local):
    team = Team(*dims)
    B, F = team.B, team.F
    sems = Sems(send, recv)
    loads = [
        pltpu.make_async_copy(src, dst, local.at[i])
        for i, (src, dst) in enumerate(
            [(wq, q_in), (wk, k_in), (wv, v_in), (w_gate, slab_g), (w_up, slab_u), (tokens, tok_full.at[team.p]),
             (gains, gains_full.at[team.f])]
        )
    ]
    for load in loads:
        load.start()
    greet(team_peers(team))
    rows = tokens.shape[0]
    gather = Gather(
        sems, team.p, B * F, team.member, tokens,
        lambda i: tok_full.at[i],
        lambda i, k: tok_full.at[i, pl.ds(k * rows // 2, rows // 2)],
    )
    gather.begin()
    small = [sems.copy(gains, gains_full.at[team.f], peer) for peer in row_peers(team)]
    for copy in small:
        copy.start()
    for load in loads[:3]:
        load.wait()
    for f in range(F):
        for y in range(B):
            h = f * B + y

            @pl.when(team.y == y)
            def _():
                qkv_cut[f, :, 0:QW] = q_in[:, h * QW : (h + 1) * QW]
                qkv_cut[f, :, QW : QW + HEAD_SIZE] = k_in[:, h * HEAD_SIZE : (h + 1) * HEAD_SIZE]
                qkv_cut[f, :, QW + HEAD_SIZE : QW + 2 * HEAD_SIZE] = v_in[:, h * HEAD_SIZE : (h + 1) * HEAD_SIZE]

    sent = []
    for d in range(1, F):
        to = lax.rem(team.f + d, F)
        sent.append(sems.copy(qkv_cut.at[to], wqkv.at[team.f], team.same_row(to)))
        sent[-1].start()
    own = pltpu.make_async_copy(qkv_cut.at[team.f], wqkv.at[team.f], local.at[7])
    own.start()
    gather.relay()
    stores = []
    for i, (slab, cut, out) in enumerate([(slab_g, cut_g, gate_cut), (slab_u, cut_u, up_cut)]):
        loads[3 + i].wait()
        width = cut.shape[-1]

        @pl.loop(0, slab.shape[0] // 32)
        def _(r):
            at = pl.ds(pl.multiple_of(r * 32, 32), 32)
            for f in range(F):
                for y in range(B):
                    q = f * B + y

                    @pl.when(team.y == y)
                    def _():
                        cut[f, at, :] = slab[at, q * width : (q + 1) * width]

        stores.append(pltpu.make_async_copy(cut, out, local.at[8 + i]))
        stores[-1].start()
    gather.end()
    for copy in small + sent:
        copy.wait()
    for copy in loads[5:] + [own] + stores:
        copy.wait()


def gather_inputs(dims, tokens, wq, wk, wv, gains, w_gate, w_up):
    B, F, T = dims
    rows, width = tokens.shape
    depth, ff = w_gate.shape
    cols = ff // (B * F)
    copies = Gather.COPIES + 2 * (F - 1)
    heads = QW + 2 * HEAD_SIZE
    return pl.pallas_call(
        functools.partial(inputs_kernel, dims),
        out_shape=(
            jax.ShapeDtypeStruct((B * F, rows, width), BF16),
            jax.ShapeDtypeStruct((F, depth, heads), BF16),
            jax.ShapeDtypeStruct((F,) + gains.shape, BF16),
            jax.ShapeDtypeStruct((F, depth, cols), BF16),
            jax.ShapeDtypeStruct((F, depth, cols), BF16),
        ),
        in_specs=[ANY] * 7,
        out_specs=[ANY] * 5,
        scratch_shapes=[
            pltpu.VMEM(wq.shape, BF16),
            pltpu.VMEM(wk.shape, BF16),
            pltpu.VMEM(wv.shape, BF16),
            pltpu.VMEM((F, depth, heads), BF16),
            pltpu.VMEM(w_gate.shape, BF16),
            pltpu.VMEM(w_up.shape, BF16),
            pltpu.VMEM((F, depth, cols), BF16),
            pltpu.VMEM((F, depth, cols), BF16),
            pltpu.SemaphoreType.DMA((copies,)),
            pltpu.SemaphoreType.DMA((copies,)),
            pltpu.SemaphoreType.DMA((10,)),
        ],
        compiler_params=kernel_params(1),
        name="gather_inputs",
    )(tokens, wq, wk, wv, gains, w_gate, w_up)


def lane_ids(rows):
    return lax.broadcasted_iota(jnp.int32, (rows, LANES), 1)


def widen_keys(kv, spans, first_row, kx, vx):
    rows = kv.shape[0]
    lane = lane_ids(rows)
    row = lax.broadcasted_iota(jnp.int32, (rows, LANES), 0) + first_row
    inside = (row >= spans[0:1, :]) & (row < spans[1:2, :])
    wide = kv.astype(F32)
    kx[...] = jnp.where(lane < HEAD_SIZE, wide, jnp.where(inside, 1.0, 0.0)).astype(BF16)
    vx[...] = jnp.where(lane < HEAD_SIZE, pltpu.roll(wide, HEAD_SIZE, 1), 1.0).astype(BF16)


def dot_last(a, b):
    return lax.dot_general(a, b, (((1,), (1,)), ((), ())), preferred_element_type=F32)


def attend_kernel(dims, qx, kv, spans, dy, wo, gate_cut, up_cut, kv_all, acc, mixed, dy_full, wo_full, w_gate, w_up,
                  kx, vx, packed, send, recv, line_send, line_recv, local):
    team = Team(*dims)
    B, F, T = dims
    t = team.t
    sems = Sems(send, recv)
    rows = kv.shape[0]
    part = rows // 2
    homes = [
        pltpu.make_async_copy(kv, kv_all.at[t], local.at[0]),
        pltpu.make_async_copy(dy, dy_full.at[team.p], local.at[1]),
        pltpu.make_async_copy(wo, wo_full.at[team.f], local.at[2]),
        pltpu.make_async_copy(gate_cut.at[team.f], w_gate.at[team.f], local.at[3]),
        pltpu.make_async_copy(up_cut.at[team.f], w_up.at[team.f], local.at[4]),
    ]
    for copy in homes:
        copy.start()
    greet(team_peers(team) + line_peers(team))

    def line_copy(d, source, to):
        return pltpu.make_async_remote_copy(
            src_ref=kv, dst_ref=kv_all.at[source], send_sem=line_send.at[d], recv_sem=line_recv.at[source],
            device_id=team.other_team(to), device_id_type=MESH,
        )

    for d in range(1, T):

        @pl.when(t + d < T)
        def _():
            line_copy(d, t, t + d).start()

    half_wo, half_dy = wo.shape[0] // 2, dy.shape[0] // 2
    gather_wo = Gather(
        sems, team.f, F, team.same_row, wo, lambda i: wo_full.at[i],
        lambda i, k: wo_full.at[i, pl.ds(k * half_wo, half_wo)],
    )
    gather_wo.begin()
    sent = []
    for cut, full in ((gate_cut, w_gate), (up_cut, w_up)):
        for d in range(1, F):
            to = lax.rem(team.f + d, F)
            sent.append(sems.copy(cut.at[to], full.at[team.f], team.same_row(to)))
            sent[-1].start()
    gather_dy = Gather(
        sems, team.p, B * F, team.member, dy, lambda i: dy_full.at[i],
        lambda i, k: dy_full.at[i, pl.ds(k * half_dy, half_dy)],
    )
    gather_dy.begin()
    homes[0].wait()
    widen_keys(kv_all[t], spans, t * rows, kx, vx)
    causal = lax.broadcasted_iota(jnp.int32, (part, part), 1) <= lax.broadcasted_iota(jnp.int32, (part, part), 0)

    def piece(q, k, masked):
        scores = dot_last(q, kx[k * part : (k + 1) * part, :])
        weights = jnp.exp(scores)
        if masked:
            weights = jnp.where(causal, weights, 0.0)
        return jnp.dot(weights.astype(BF16), vx[k * part : (k + 1) * part, :], preferred_element_type=F32)

    @pl.loop(0, GROUP)
    def _(h):
        acc[h, 0:part, :] = piece(qx[h, 0:part, :], 0, True)
        low = qx[h, part:rows, :]
        acc[h, part:rows, :] = piece(low, 0, False) + piece(low, 1, True)

    gather_wo.relay()

    @pl.loop(1, t + 1)
    def _(j):
        source = t - j
        line_copy(0, source, t).wait_recv()
        widen_keys(kv_all[source], spans, source * rows, kx, vx)

        @pl.loop(0, GROUP)
        def _(h):
            for k in range(2):
                at = pl.ds(k * part, part)
                q = qx[h, at, :]
                acc[h, at, :] = acc[h, at, :] + piece(q, 0, False) + piece(q, 1, False)

    for h in range(GROUP):
        out = acc[h, :, 0:HEAD_SIZE] / acc[h, :, HEAD_SIZE : 2 * HEAD_SIZE]
        out = out.astype(BF16)
        if h < 2:
            packed[0:rows, h * HEAD_SIZE : (h + 1) * HEAD_SIZE] = out
        else:
            packed[rows : rows + part, 0:HEAD_SIZE] = out[0:part]
            packed[rows : rows + part, HEAD_SIZE : 2 * HEAD_SIZE] = out[part:rows]
    home = pltpu.make_async_copy(packed, mixed.at[team.p], local.at[5])
    home.start()
    half_mixed = packed.shape[0] // 2
    gather_mixed = Gather(
        sems, team.p, B * F, team.member, packed, lambda i: mixed.at[i],
        lambda i, k: mixed.at[i, pl.ds(k * half_mixed, half_mixed)],
    )
    gather_mixed.begin()
    gather_mixed.relay()
    gather_dy.relay()
    gather_mixed.end()
    gather_wo.end()
    gather_dy.end()
    for copy in sent:
        copy.wait()
    for copy in homes[1:] + [home]:
        copy.wait()
    for d in range(1, T):

        @pl.when(t + d < T)
        def _():
            line_copy(d, t, t + d).wait_send()


def attend(dims, qx, kv, spans, dy, wo, gate_cut, up_cut):
    B, F, T = dims
    rows = kv.shape[0]
    copies = 3 * Gather.COPIES + 2 * (F - 1)
    packed = (rows + rows // 2, LANES)
    return pl.pallas_call(
        functools.partial(attend_kernel, dims),
        out_shape=(
            jax.ShapeDtypeStruct((T, rows, LANES), BF16),
            jax.ShapeDtypeStruct((GROUP, rows, LANES), F32),
            jax.ShapeDtypeStruct((B * F,) + packed, BF16),
            jax.ShapeDtypeStruct((B * F,) + dy.shape, BF16),
            jax.ShapeDtypeStruct((F,) + wo.shape, BF16),
            jax.ShapeDtypeStruct(gate_cut.shape, BF16),
            jax.ShapeDtypeStruct(up_cut.shape, BF16),
        ),
        in_specs=[VMEM, ANY, VMEM, ANY, ANY, ANY, ANY],
        out_specs=[VMEM, VMEM, ANY, ANY, ANY, ANY, ANY],
        scratch_shapes=[
            pltpu.VMEM((rows, LANES), BF16),
            pltpu.VMEM((rows, LANES), BF16),
            pltpu.VMEM(packed, BF16),
            pltpu.SemaphoreType.DMA((copies,)),
            pltpu.SemaphoreType.DMA((copies,)),
            pltpu.SemaphoreType.DMA((T,)),
            pltpu.SemaphoreType.DMA((T,)),
            pltpu.SemaphoreType.DMA((6,)),
        ],
        compiler_params=kernel_params(2),
        name="attend",
    )(qx, kv, spans, dy, wo, gate_cut, up_cut)


HOP = 2
LAG = 3


class GradSum:
    RED, FIN, HAND, OWN, OVER, HOME, INTO = range(7)

    def __init__(self, team, kinds, red_recv, fin_recv, hand_recvs, bulk):
        self.team, self.kinds = team, kinds
        self.red_recv, self.fin_recv, self.hand_recvs, self.bulk = red_recv, fin_recv, hand_recvs, bulk
        self.opposite = team.member(lax.rem(team.p + team.F, team.B * team.F))

    @staticmethod
    def steps(kinds, T):
        last = max(first + rows // 2 // step for rows, step, first in kinds)
        return last + 2 * HOP * (T - 1) + LAG

    def remote(self, src, dst, send_sem, recv_sem, device):
        return pltpu.make_async_remote_copy(
            src_ref=src, dst_ref=dst, send_sem=send_sem, recv_sem=recv_sem, device_id=device, device_id_type=MESH
        )

    def is_first(self, way):
        return self.team.t == (self.team.T - 1 if way else 0)

    def is_last(self, way):
        return self.team.t == (0 if way else self.team.T - 1)

    def rows(self, k, way, c):
        g, land, out, step, first, how = self.kinds[k]
        return pl.ds(pl.multiple_of(way * (g.shape[0] // 2) + c * step, 16), step)

    def reduce_copy(self, k, way, at, i):
        g, land = self.kinds[k][:2]
        to = self.team.other_team(self.team.t + 1 - 2 * way)
        return self.remote(g.at[at], land.at[at], self.bulk.at[self.RED, k, way], self.red_recv.at[way, i], to)

    def final_copy(self, k, way, at, i):
        land = self.kinds[k][1]
        to = self.team.other_team(self.team.t - 1 + 2 * way)
        return self.remote(land.at[at], land.at[at], self.bulk.at[self.FIN, k, way], self.fin_recv.at[way, i], to)

    def reduce(self, k, way, c, i):
        g, land = self.kinds[k][:2]
        at = self.rows(k, way, c)

        @pl.when(self.is_first(way))
        def _():
            self.reduce_copy(k, way, at, i).start()

        @pl.when(jnp.logical_not(self.is_first(way)))
        def _():
            self.reduce_copy(k, way, at, i).wait_recv()
            summed = (wide(g[at, :]) + wide(land[at, :])).astype(BF16)

            @pl.when(self.is_last(way))
            def _():
                land[at, :] = summed

            @pl.when(jnp.logical_not(self.is_last(way)))
            def _():
                g[at, :] = summed
                self.reduce_copy(k, way, at, i).start()

    def place(self, k, way, c):
        g, land, out, step, first, how = self.kinds[k]
        shard = g.shape[0] // self.team.F
        row = way * (g.shape[0] // 2) + c * step
        return lax.div(row, shard), lax.rem(row, shard)

    def finish(self, k, way, c, i):
        g, land, out, step, first, how = self.kinds[k]
        team, bulk = self.team, self.bulk
        B, F, y, f = team.B, team.F, team.y, team.f
        at = self.rows(k, way, c)

        @pl.when(jnp.logical_not(self.is_last(way)))
        def _():
            self.final_copy(k, way, at, i).wait_recv()

        @pl.when(jnp.logical_not(self.is_first(way)))
        def _():
            self.final_copy(k, way, at, i).start()

        if how == "rows":
            to, row = self.place(k, way, c)
            dst = out.at[f * B + y, pl.ds(pl.multiple_of(row, 16), step)]

            @pl.when(to == f)
            def _():
                pltpu.make_async_copy(land.at[at], dst, bulk.at[self.HOME, k, 0]).start()
                if B == 2:
                    self.remote(land.at[at], dst, bulk.at[self.OVER, k, 0], bulk.at[self.INTO, k, 0],
                                self.opposite).start()

            @pl.when(to != f)
            def _():
                self.remote(land.at[at], dst, bulk.at[self.HAND, k, 0], self.hand_recvs[k].at[f, lax.div(row, step)],
                            team.same_row(to)).start()
        elif how == "stay":
            dst = out.at[y, at]
            pltpu.make_async_copy(land.at[at], dst, bulk.at[self.HOME, k, 0]).start()
            if B == 2:
                self.remote(land.at[at], dst, bulk.at[self.OVER, k, 0], bulk.at[self.INTO, k, 0],
                            self.opposite).start()
        else:
            for j in range(F // 2):
                to = way * (F // 2) + j
                src = land.at[pl.ds(16 * to, 16)]
                for row in range(B):
                    member = row * F + to

                    @pl.when(team.p == member)
                    def _():
                        pltpu.make_async_copy(src, out.at[team.p], bulk.at[self.HOME, k, 0]).start()

                    @pl.when(team.p != member)
                    def _():
                        self.remote(src, out.at[team.p], bulk.at[self.HAND, k, 0], bulk.at[self.INTO, k, 0],
                                    (team.t * B + row, to)).start()

    def pass_over(self, k, way, c, i):
        g, land, out, step, first, how = self.kinds[k]
        if how != "rows":
            return
        team = self.team
        to, row = self.place(k, way, c)

        @pl.when(to == team.f)
        def _():
            for d in range(1, team.F):
                source = lax.rem(team.f + d, team.F)
                ref = out.at[source * team.B + team.y, pl.ds(pl.multiple_of(row, 16), step)]
                self.remote(land.at[self.rows(k, way, c)], ref, self.bulk.at[self.HAND, k, 0],
                            self.hand_recvs[k].at[source, lax.div(row, step)], team.same_row(team.f)).wait_recv()
                if team.B == 2:
                    self.remote(ref, ref, self.bulk.at[self.OVER, k, 1], self.bulk.at[self.INTO, k, 0],
                                self.opposite).start()

    def each(self, i, way, body):
        for k, (g, land, out, step, first, how) in enumerate(self.kinds):
            count = g.shape[0] // 2 // step

            pl.when((i >= first) & (i < first + count))(functools.partial(lambda k, c: body(k, way, c, i), k, i - first))

    def step(self, s):
        T, t = self.team.T, self.team.t
        for way in range(2):
            place = T - 1 - t if way else t
            done = s - HOP * (2 * (T - 1) - place)
            self.each(s - HOP * place, way, self.reduce)
            self.each(done, way, self.finish)
            self.each(done - LAG, way, self.pass_over)

    def drain(self, ref, sem):
        pltpu.make_async_copy(ref, ref, sem).wait()

    def end(self):
        bulk, B, F = self.bulk, self.team.B, self.team.F
        for k, (g, land, out, step, first, how) in enumerate(self.kinds):
            rows = g.shape[0]
            some = lambda n: g.at[pl.ds(0, n)]
            for way in range(2):

                @pl.when(jnp.logical_not(self.is_last(way)))
                def _():
                    self.drain(some(rows // 2), bulk.at[self.RED, k, way])

                @pl.when(jnp.logical_not(self.is_first(way)))
                def _():
                    self.drain(some(rows // 2), bulk.at[self.FIN, k, way])

            if how == "rows":
                shard = rows // F
                self.drain(some(rows - shard), bulk.at[self.HAND, k, 0])
                self.drain(some(shard), bulk.at[self.HOME, k, 0])
                if B == 2:
                    self.drain(some(shard), bulk.at[self.OVER, k, 0])
                    self.drain(some(rows - shard), bulk.at[self.OVER, k, 1])
                    self.drain(g, bulk.at[self.INTO, k, 0])
            elif how == "stay":
                self.drain(g, bulk.at[self.HOME, k, 0])
                if B == 2:
                    self.drain(g, bulk.at[self.OVER, k, 0])
                    self.drain(g, bulk.at[self.INTO, k, 0])
            else:
                others = out.at[pl.ds(0, B * F - 1)]
                self.drain(out.at[0], bulk.at[self.HOME, k, 0])
                self.drain(others, bulk.at[self.HAND, k, 0])
                self.drain(others, bulk.at[self.INTO, k, 0])


def rotate_back(u, cosine, sine):
    half = u.shape[-1] // 2
    swapped = jnp.concatenate([-u[:, half:], u[:, :half]], 1)
    return u * cosine - swapped * sine


def unit_and_factor(x):
    factor = lax.rsqrt(jnp.mean(x * x, -1, keepdims=True) + EPSILON)
    return x * factor, factor


def first_steps(dims):
    T = dims[2]
    attention = 8
    keys = attention + 2 * T + 1
    return dict(scatter1=1, scatter2=3, resid=4, relay=6, heads=7, attention=attention, keys=keys,
                again1=keys + 1, again2=keys + 3, tokens=keys + 4, down1=keys + 5, down2=keys + 6, down3=keys + 7)


def grad_kinds(dims, depth, hidden):
    at = first_steps(dims)
    kinds, place = [], 0
    for rows, width, step, ready, how in (
        (hidden, depth, 48, 0, "stay"),
        (depth, hidden, 64, 0, "rows"),
        (depth, hidden, 64, 0, "rows"),
        (QW, depth, 48, at["heads"] + 1, "stay"),
        (depth, QW + 2 * HEAD_SIZE, 96, at["keys"] + 1, "rows"),
        (16 * dims[1], max(depth // dims[1], LANES), 8 * dims[1], at["tokens"] + 1, "gain"),
    ):
        place = max(place, ready)
        kinds.append((rows, width, step, place, how))
        place += rows // 2 // step
    return kinds


def back_kernel(dims, kinds, steps, grad_hidden, down_out, g_down, g_gate, g_up, resid, tokens, cotangent, gains, acc, qx, kv_all, spans,
                heads, cosine, sine, own_wo, wqkv, normed,
                out_down, out_gate, out_up, out_wo, out_heads, out_gains, layer_out, tokens_grad,
                xs, xd, own_down, own_gate, own_up, own_gwo, own_heads, own_gains,
                land_down, land_gate, land_up, land_wo, land_heads, land_gains,
                grad_resid, attn_own, big, dox, mixed, dq, dkv, kv_in, dkv_sum, turned, small, kx, vx, dk, dv, wq_in, *rest):
    scratch1, rest = rest[:9], rest[9:]
    scratch2, rest = rest[:9], rest[9:]
    send, recv, line_send, line_recv, red_recv, fin_recv, hand_gate, hand_up, hand_heads, bulk, local = rest
    team = Team(*dims)
    B, F, T = dims
    t, p = team.t, team.p
    at = first_steps(dims)
    own_rows, width = resid.shape
    rows = qx.shape[1]
    part = rows // 2
    block = rows // 4
    depth = width // F
    sems = Sems(send, recv)
    loads = [
        pltpu.make_async_copy(src, dst, local.at[i])
        for i, (src, dst) in enumerate(
            [(grad_hidden, xs), (g_down, own_down), (g_gate, own_gate), (g_up, own_up), (down_out, xd), (wqkv, wq_in)]
        )
    ]
    for load in loads:
        load.start()
    own_gains[...] = jnp.zeros_like(own_gains)
    greet(team_peers(team) + line_peers(team))
    loads[0].wait()
    scatter = Scatter(sems, team, xs, scratch1)
    scatter.begin()
    again = Scatter(sems, team, xs, scratch1)
    down = Scatter(sems, team, xd, scratch2)
    half = own_rows // 2
    gather = Gather(
        sems, p, B * F, team.member, attn_own,
        lambda i: big.at[pl.ds(pl.multiple_of(i * own_rows, 16), own_rows)],
        lambda i, k: big.at[pl.ds(pl.multiple_of(i * own_rows + k * half, 16), half)],
    )
    sums = GradSum(
        team,
        [
            (own, land, out) + kind[2:]
            for own, land, out, kind in zip(
                (own_down, own_gate, own_up, own_gwo, own_heads, own_gains),
                (land_down, land_gate, land_up, land_wo, land_heads, land_gains),
                (out_down, out_gate, out_up, out_wo, out_heads, out_gains),
                kinds,
            )
        ],
        red_recv, fin_recv, [None, hand_gate, hand_up, None, hand_heads, None], bulk,
    )
    for load in loads[1:]:
        load.wait()
    gain_attn, gain_ffn = gains[0:1, :], gains[1:2, :]
    gain_q, gain_k = gains[2:3, 0:HEAD_SIZE], gains[3:4, 0:HEAD_SIZE]
    home = pltpu.make_async_copy(attn_own, big.at[pl.ds(pl.multiple_of(p * own_rows, 16), own_rows)], local.at[6])
    fetch = pltpu.make_async_copy(normed, big, local.at[7])

    def resid_phase():
        def store(columns, total):
            grad_resid[:, columns] = total

        scatter.end(store)
        term = jnp.zeros((1, width), F32)
        for r in range(0, own_rows, 32):
            here = slice(r, r + 32)
            unit, factor = unit_and_factor(resid[here, :])
            upstream = grad_resid[here, :]
            term = term + jnp.sum(upstream * unit, 0, keepdims=True)
            total = wide(cotangent[here, :]) + norm_back(upstream, unit, factor, gain_ffn)
            grad_resid[here, :] = total
            attn_own[here, :] = total.astype(BF16)
        small[1:2, :] = term
        home.start()
        gather.begin()

    def heads_phase():
        gather.end()
        home.wait()
        lane = lane_ids(block)

        @pl.loop(0, rows // block)
        def _(r):
            here = pl.ds(pl.multiple_of(r * block, block), block)
            grad = dot_last(big[here, :], own_wo[...]).astype(BF16)
            for h in range(GROUP):
                sums_h = acc[h, here, :]
                total = pltpu.roll(sums_h, HEAD_SIZE, 1)
                out = sums_h / total
                mixed[here, h * HEAD_SIZE : (h + 1) * HEAD_SIZE] = out[:, :HEAD_SIZE].astype(BF16)
                do = wide(grad[:, h * HEAD_SIZE : (h + 1) * HEAD_SIZE])
                do = jnp.concatenate([do, jnp.zeros_like(do)], 1)
                delta = -jnp.sum(jnp.where(lane < HEAD_SIZE, do * out, 0.0), 1, keepdims=True)

                def put(x, first, value):
                    for i in range(3):
                        x = jnp.where(lane == first + i, wide(value.astype(BF16)), x)
                        value = value - wide(value.astype(BF16))
                    return x

                dox[h, here, :] = put(do, HEAD_SIZE, delta).astype(BF16)
                log_sum = -jnp.log(jnp.where(lane < HEAD_SIZE, total, sums_h))
                qx[h, here, :] = put(wide(qx[h, here, :]), HEAD_SIZE + NDOCS, log_sum).astype(BF16)

        own_gwo[...] = lax.dot_general(
            mixed[...], big[...], (((0,), (0,)), ((), ())), preferred_element_type=F32
        ).astype(BF16)
        dq[...] = jnp.zeros_like(dq)

    causal = lax.broadcasted_iota(jnp.int32, (part, part), 0) <= lax.broadcasted_iota(jnp.int32, (part, part), 1)

    def piece(h, q_rows, k_rows, masked):
        q = qx[h, q_rows, :]
        do = dox[h, q_rows, :]
        keys = kx[k_rows, :]
        weights = jnp.exp(dot_last(keys, q))
        if masked:
            weights = jnp.where(causal, weights, 0.0)
        dscore = (weights * dot_last(vx[k_rows, :], do)).astype(BF16)
        dv[...] += jnp.dot(weights.astype(BF16), do, preferred_element_type=F32)
        dk[...] += jnp.dot(dscore, q, preferred_element_type=F32)
        dq[h, q_rows, :] += lax.dot_general(dscore, keys, (((0,), (0,)), ((), ())), preferred_element_type=F32)

    def line_copy(owner, source):
        return pltpu.make_async_remote_copy(
            src_ref=dkv.at[owner], dst_ref=dkv.at[source], send_sem=line_send.at[owner],
            recv_sem=line_recv.at[source], device_id=team.other_team(owner), device_id_type=MESH,
        )

    def fetch_keys(source):
        slot = lax.rem(source, 2)
        return pltpu.make_async_copy(kv_all.at[source], kv_in.at[slot], local.at[8 + slot])

    fetch_keys(t * 0).start()

    def attention_unit(source, k):
        @pl.when(k == 0)
        def _():
            fetch_keys(source).wait()

            @pl.when(source < t)
            def _():
                fetch_keys(source + 1).start()

            widen_keys(kv_in[lax.rem(source, 2)], spans, source * rows, kx, vx)

        k_rows = pl.ds(pl.multiple_of(k * part, part), part)
        dk[...] = jnp.zeros_like(dk)
        dv[...] = jnp.zeros_like(dv)

        @pl.when(source < t)
        def _():
            @pl.loop(0, GROUP)
            def _(h):
                for q in range(2):
                    piece(h, slice(q * part, (q + 1) * part), k_rows, False)

        @pl.when(source == t)
        def _():
            for diagonal in range(2):

                @pl.when(k == diagonal)
                def _():
                    @pl.loop(0, GROUP)
                    def _(h):
                        for q in range(diagonal, 2):
                            piece(h, slice(q * part, (q + 1) * part), slice(diagonal * part, (diagonal + 1) * part),
                                  q == diagonal)

        dkv[source, k_rows, :] = jnp.where(
            lane_ids(part) < HEAD_SIZE, dk[...], pltpu.roll(dv[...], HEAD_SIZE, 1)
        ).astype(BF16)

        @pl.when((k == 1) & (source < t))
        def _():
            line_copy(source, t).start()

    def keys_phase():
        fetch.start()
        dkv_sum[...] = wide(dkv[t])
        for d in range(1, T):

            @pl.when(t + d < T)
            def _():
                line_copy(t, t + d).wait_recv()
                dkv_sum[...] += wide(dkv[t + d])

        small[2:4, :] = jnp.zeros((2, width), F32)

        @pl.loop(0, rows // block)
        def _(r):
            here = pl.ds(pl.multiple_of(r * block, block), block)
            cos, sin = cosine[here, :], sine[here, :]
            q_term = jnp.zeros((1, HEAD_SIZE), F32)
            for h in range(GROUP + 1):
                if h < GROUP:
                    u, gain = dq[h, here, 0:HEAD_SIZE] * HEAD_SIZE ** (-0.5), gain_q
                else:
                    u, gain = dkv_sum[here, 0:HEAD_SIZE], gain_k
                u = rotate_back(u, cos, sin)
                unit, factor = unit_and_factor(heads[h, here, :])
                term = jnp.sum(u * unit, 0, keepdims=True)
                if h < GROUP:
                    q_term = q_term + term
                else:
                    small[3:4, 0:HEAD_SIZE] += term
                turned[here, h * HEAD_SIZE : (h + 1) * HEAD_SIZE] = norm_back(u, unit, factor, gain).astype(BF16)
            small[2:3, 0:HEAD_SIZE] += q_term
            h = GROUP + 1
            turned[here, h * HEAD_SIZE : (h + 1) * HEAD_SIZE] = dkv_sum[here, HEAD_SIZE : 2 * HEAD_SIZE].astype(BF16)

        for m in range(2 * 2 * 2):
            xs[m // 4, m // 2 % 2, m % 2] = dot_last(
                turned[m * own_rows : (m + 1) * own_rows, :], wq_in[...]
            ).astype(BF16)
        again.begin()
        fetch.wait()
        for r in range(0, width, 256):
            own_heads[r : r + 256, :] = lax.dot_general(
                big[:, r : r + 256], turned[...], (((0,), (0,)), ((), ())), preferred_element_type=F32
            ).astype(BF16)

    def tokens_phase():
        def store(columns, total):
            tokens_grad[:, columns] = total

        again.end(store)
        down.begin()
        term = jnp.zeros((1, width), F32)
        for r in range(0, own_rows, 32):
            here = slice(r, r + 32)
            unit, factor = unit_and_factor(wide(tokens[here, :]))
            upstream = tokens_grad[here, :]
            term = term + jnp.sum(upstream * unit, 0, keepdims=True)
            tokens_grad[here, :] = grad_resid[here, :] + norm_back(upstream, unit, factor, gain_attn)
        small[0:1, :] = term
        lanes = own_gains.shape[1]
        row = lax.broadcasted_iota(jnp.int32, (16, lanes), 0)

        def cut(i, first, count):
            value = small[i : i + 1, first : first + count]
            if count < lanes:
                value = jnp.concatenate([value, jnp.zeros((1, lanes - count), F32)], 1)
            return jnp.where(row == i, jnp.broadcast_to(value, (16, lanes)), 0.0)

        for i in range(F):
            few = HEAD_SIZE // F
            own_gains[16 * i : 16 * i + 16, :] = (
                cut(0, i * depth, depth) + cut(1, i * depth, depth) + cut(2, i * few, few) + cut(3, i * few, few)
            ).astype(BF16)

    def down_phase():
        def store(columns, total):
            layer_out[:, columns] = resid[:, columns] + total

        down.end(store)

    @pl.loop(0, steps)
    def _(s):
        sums.step(s)
        for name, body in (
            ("scatter1", scatter.relay), ("scatter2", scatter.relay_again), ("resid", resid_phase),
            ("relay", gather.relay), ("heads", heads_phase), ("keys", keys_phase), ("again1", again.relay),
            ("again2", again.relay_again), ("tokens", tokens_phase), ("down1", down.relay),
            ("down2", down.relay_again), ("down3", down_phase),
        ):
            pl.when(s == at[name])(body)
        unit = s - at["attention"]

        @pl.when((unit >= 0) & (lax.div(unit, 2) <= t))
        def _():
            attention_unit(lax.div(unit, 2), lax.rem(unit, 2))

    for d in range(1, T):

        @pl.when(t - d >= 0)
        def _():
            line_copy(t - d, t).wait_send()

    sums.end()


def backward(dims, grad_hidden, down_out, g_down, g_gate, g_up, resid, tokens, cotangent, gains, acc, qx, kv_all, spans,
             heads, cosine, sine, own_wo, wqkv, normed):
    B, F, T = dims
    own_rows, width = resid.shape
    rows = qx.shape[1]
    part = rows // 2
    hidden = g_down.shape[0]
    n = B * F
    kinds = grad_kinds(dims, width, hidden)
    steps = max(
        GradSum.steps([(rows_, step, first) for rows_, _, step, first, _ in kinds], T), first_steps(dims)["down3"] + 1
    )
    positions = max(first + rows_ // 2 // step for rows_, _, step, first, _ in kinds)
    outs = []
    for rows_, wide_, step, first, how in kinds:
        if how == "rows":
            shape = (n, rows_ // F, wide_)
        elif how == "stay":
            shape = (B, rows_, wide_)
        else:
            shape = (n, 16, wide_)
        outs.append(jax.ShapeDtypeStruct(shape, BF16))
    outs += [jax.ShapeDtypeStruct((own_rows, width), F32), jax.ShapeDtypeStruct((own_rows, width), F32)]
    eight = (2, 2, 2, own_rows, width)
    hands = [pltpu.SemaphoreType.DMA((F, kinds[k][0] // F // kinds[k][2])) for k in (1, 2, 4)]
    copies = 3 * Scatter.COPIES + Gather.COPIES
    return pl.pallas_call(
        functools.partial(back_kernel, dims, kinds, steps),
        out_shape=outs,
        in_specs=[ANY] * 5 + [VMEM] * 6 + [ANY] + [VMEM] * 5 + [ANY] * 2,
        out_specs=[ANY] * 6 + [VMEM] * 2,
        scratch_shapes=[
            pltpu.VMEM(eight, BF16),
            pltpu.VMEM(eight, BF16),
        ]
        + [pltpu.VMEM((kind[0], kind[1]), BF16) for kind in kinds] * 2
        + [
            pltpu.VMEM((own_rows, width), F32),
            pltpu.VMEM((own_rows, width), BF16),
            pltpu.VMEM((rows, width), BF16),
            pltpu.VMEM(qx.shape, BF16),
            pltpu.VMEM((rows, QW), BF16),
            pltpu.VMEM(qx.shape, F32),
            pltpu.VMEM(kv_all.shape, BF16),
            pltpu.VMEM((2,) + kv_all.shape[1:], BF16),
            pltpu.VMEM((rows, LANES), F32),
            pltpu.VMEM((rows, QW + 2 * HEAD_SIZE), BF16),
            pltpu.VMEM((8, width), F32),
            pltpu.VMEM((rows, LANES), BF16),
            pltpu.VMEM((rows, LANES), BF16),
            pltpu.VMEM((part, LANES), F32),
            pltpu.VMEM((part, LANES), F32),
            pltpu.VMEM(wqkv.shape, BF16),
        ]
        + scatter_shapes(own_rows, width) * 2
        + [
            pltpu.SemaphoreType.DMA((copies,)),
            pltpu.SemaphoreType.DMA((copies,)),
            pltpu.SemaphoreType.DMA((T,)),
            pltpu.SemaphoreType.DMA((T,)),
            pltpu.SemaphoreType.DMA((2, positions)),
            pltpu.SemaphoreType.DMA((2, positions)),
            *hands,
            pltpu.SemaphoreType.DMA((7, len(kinds), 2)),
            pltpu.SemaphoreType.DMA((10,)),
        ],
        compiler_params=pltpu.CompilerParams(
            collective_id=3, has_side_effects=True, vmem_limit_bytes=60 * 1024 * 1024
        ),
        name="backward",
    )(grad_hidden.reshape(eight), down_out.reshape(eight), g_down, g_gate, g_up, resid, tokens, cotangent, gains, acc, qx,
      kv_all, spans, heads, cosine, sine, own_wo, wqkv, normed)


def place_kernel(n, gate, up, heads, down, wo, gate_out, up_out, wq_out, wk_out, wv_out, down_out, wo_out):
    hidden = gate.shape[-1]
    for q in range(n):
        gate_out[:, q * hidden : (q + 1) * hidden] = wide(gate[q])
        up_out[:, q * hidden : (q + 1) * hidden] = wide(up[q])
        block = wide(heads[q])
        wq_out[:, q * QW : (q + 1) * QW] = block[:, :QW]
        wk_out[:, q * HEAD_SIZE : (q + 1) * HEAD_SIZE] = block[:, QW : QW + HEAD_SIZE]
        wv_out[:, q * HEAD_SIZE : (q + 1) * HEAD_SIZE] = block[:, QW + HEAD_SIZE :]
    down_out[...] = wide(down[...])
    wo_out[...] = wide(wo[...])


def place(gate, up, heads, down, wo):
    n, depth, hidden = gate.shape
    width = down.shape[-1]
    down, wo = down.reshape(-1, width), wo.reshape(-1, width)
    step = 32
    count = depth // step
    many = lambda w: pl.BlockSpec((n, step, w), lambda i: (0, i, 0))
    cut = lambda a: pl.BlockSpec((a.shape[0] // count, width), lambda i: (i, 0))
    out = lambda w: pl.BlockSpec((step, w), lambda i: (i, 0))
    shape = lambda r, w: jax.ShapeDtypeStruct((r, w), F32)
    wq, wk = QW * n, HEAD_SIZE * n
    return pl.pallas_call(
        functools.partial(place_kernel, n),
        grid=(count,),
        out_shape=(
            shape(depth, n * hidden), shape(depth, n * hidden), shape(depth, wq), shape(depth, wk), shape(depth, wk),
            shape(down.shape[0], width), shape(wo.shape[0], width),
        ),
        in_specs=[many(hidden), many(hidden), many(QW + 2 * HEAD_SIZE), cut(down), cut(wo)],
        out_specs=[out(n * hidden), out(n * hidden), out(wq), out(wk), out(wk), cut(down), cut(wo)],
        compiler_params=pltpu.CompilerParams(vmem_limit_bytes=VMEM_LIMIT),
        name="place",
    )(gate, up, heads, down, wo)


def doc_layout(lengths, token_index):
    doc_ends = jnp.cumsum(lengths)
    passed = token_index[:, None] >= doc_ends[None, :]
    document_index = jnp.sum(passed.astype(jnp.int32), axis=1)
    doc_start = jnp.max(jnp.where(passed, doc_ends[None, :], 0), axis=1)
    return (document_index, token_index - doc_start)


def rotation(places, width):
    half_width = width // 2
    inverse_freq = jnp.power(ROPE_BASE, -(jnp.arange(half_width, dtype=F32) * 2.0 / width))
    angles = places.astype(F32)[:, None] * inverse_freq[None, :]
    cosine_values = jnp.cos(angles)
    sine_lookup = jnp.sin(angles)
    return (
        jnp.concatenate([cosine_values, cosine_values], 1),
        jnp.concatenate([sine_lookup, sine_lookup], 1),
    )


def apply_rotary(values_in, cosine_values, sine_lookup, sign):
    half_width = values_in.shape[-1] // 2
    swapped = jnp.concatenate([-values_in[..., half_width:], values_in[..., :half_width]], -1)
    return values_in * cosine_values + swapped * (sine_lookup * sign)


def scaled_input(values_in):
    factor = lax.rsqrt(jnp.mean(values_in * values_in, -1, keepdims=True) + EPSILON)
    return (values_in * factor, factor)


def norm_back(upstream, unit_rows, factor, gain_row):
    lifted = upstream * gain_row
    return factor * (lifted - unit_rows * jnp.mean(lifted * unit_rows, -1, keepdims=True))


def dot(a, b, dims=((1,), (0,))):
    return lax.dot_general(a, b, (dims, ((), ())), preferred_element_type=F32)


def on_device(
    tokens, lengths, wq, wk, wv, wo, w_gate, w_up, w_down, attn_gain, ffn_gain, q_gain, key_norm_gain, cotangent
):
    F = lax.axis_size("fsdp")
    B = KEY_VALUE_HEADS // F
    T = lax.axis_size("ctx") // B
    dims = (B, F, T)
    own_rows, width = tokens.shape
    rows = own_rows * KEY_VALUE_HEADS
    depth = width // F
    ctx, f = lax.axis_index("ctx"), lax.axis_index("fsdp")
    t, y = ctx // B, ctx % B
    p = y * F + f
    hidden = w_down.shape[0] // B

    gains = jnp.zeros((16, max(depth, LANES)), BF16)
    gains = gains.at[0, :depth].set(attn_gain).at[1, :depth].set(ffn_gain)
    gains = gains.at[2, : HEAD_SIZE // F].set(q_gain).at[3, : HEAD_SIZE // F].set(key_norm_gain)
    tok_full, wqkv, gains_full, gate_cut, up_cut = gather_inputs(dims, tokens, wq, wk, wv, gains, w_gate, w_up)
    gains_full = gains_full.astype(F32)
    gain_attn = gains_full[:, 0, :depth].reshape(-1)
    gain_ffn = gains_full[:, 1, :depth].reshape(-1)
    gain_query = gains_full[:, 2, : HEAD_SIZE // F].reshape(-1)
    gain_key = gains_full[:, 3, : HEAD_SIZE // F].reshape(-1)
    wqkv = wqkv.reshape(width, -1)

    token_index = t * rows + jnp.arange(rows, dtype=jnp.int32)
    docs, places = doc_layout(lengths, token_index)
    cosine_values, sine_lookup = rotation(places, HEAD_SIZE)
    cosine_values, sine_lookup = cosine_values[None], sine_lookup[None]
    ends = jnp.cumsum(lengths)
    ndocs = lengths.shape[0]
    big = jnp.int32(2**30)
    spans = jnp.stack([
        jnp.zeros((LANES,), jnp.int32).at[HEAD_SIZE : HEAD_SIZE + ndocs].set(ends - lengths),
        jnp.full((LANES,), big, jnp.int32).at[HEAD_SIZE : HEAD_SIZE + ndocs].set(ends),
    ])
    spans = jnp.concatenate([spans, jnp.zeros((6, LANES), jnp.int32)])

    inputs = tok_full.reshape(rows, width).astype(F32)
    unit_attn, factor_attn = scaled_input(inputs)
    normed = (unit_attn * gain_attn).astype(BF16)
    projected = dot(normed, wqkv)
    heads = jnp.transpose(projected.reshape(rows, GROUP + 2, HEAD_SIZE), (1, 0, 2))
    q_unit, q_factor = scaled_input(heads[:GROUP])
    k_unit, k_factor = scaled_input(heads[GROUP])
    queries = apply_rotary(q_unit * gain_query, cosine_values, sine_lookup, 1.0).astype(BF16)
    own_keys = apply_rotary(k_unit * gain_key, cosine_values[0], sine_lookup[0], 1.0).astype(BF16)
    own_values = heads[GROUP + 1].astype(BF16)
    scale = HEAD_SIZE ** (-0.5)
    apart = jnp.where(docs[:, None] == jnp.arange(ndocs)[None, :], 0.0, -APART).astype(BF16)
    apart = jnp.broadcast_to(apart[None], (GROUP, rows, ndocs))
    queries = (queries * jnp.asarray(scale, BF16)).astype(BF16)
    qx = jnp.concatenate([queries, apart, jnp.zeros((GROUP, rows, LANES - HEAD_SIZE - ndocs), BF16)], -1)
    kv = jnp.concatenate([own_keys, own_values], -1)
    kv_all, acc, mixed, dy_full, wo_full, gate_w, up_w = attend(
        dims, qx, kv, spans, cotangent, wo, gate_cut, up_cut
    )
    both = mixed[:, :rows].reshape(B, F, rows, 2 * HEAD_SIZE)
    third = mixed[:, rows:].reshape(B, F, rows // 2, 2, HEAD_SIZE)
    third = jnp.swapaxes(third, 2, 3).reshape(B, F, rows, HEAD_SIZE)
    mixed_heads = jnp.concatenate([both, third], -1)
    mixed_heads = jnp.transpose(mixed_heads, (2, 1, 0, 3)).reshape(rows, QUERY_HEADS * HEAD_SIZE)
    wo_full = wo_full.reshape(-1, width)
    gate_w = gate_w.reshape(width, hidden)
    up_w = up_w.reshape(width, hidden)
    down_w = lax.dynamic_slice_in_dim(w_down, y * hidden, hidden, 0)
    own_wo = lax.dynamic_slice_in_dim(wo, y * QW, QW, 0)
    dy_full = dy_full.reshape(rows, width)

    resid = inputs + dot(mixed_heads, wo_full)
    unit_ffn, factor_ffn = scaled_input(resid)
    hidden_in = (unit_ffn * gain_ffn).astype(BF16)
    gate = dot(hidden_in, gate_w)
    upper = dot(hidden_in, up_w)
    sigma = jax.nn.sigmoid(gate)
    silu_gate = gate * sigma
    act_rows = (silu_gate * upper).astype(BF16)
    down_out = dot(act_rows, down_w).astype(BF16)

    grad_act = dot(dy_full, down_w, ((1,), (1,)))
    grad_gate = (grad_act * upper * sigma * (1.0 + gate * (1.0 - sigma))).astype(BF16)
    grad_upper = (grad_act * silu_gate).astype(BF16)
    grad_hidden = (dot(grad_gate, gate_w, ((1,), (1,))) + dot(grad_upper, up_w, ((1,), (1,)))).astype(BF16)
    own_resid = lax.dynamic_slice_in_dim(resid, p * own_rows, own_rows, 0)
    over_rows = ((0,), (0,))
    g_down = dot(act_rows, dy_full, over_rows).astype(BF16)
    g_gate = dot(hidden_in, grad_gate, over_rows).astype(BF16)
    g_up = dot(hidden_in, grad_upper, over_rows).astype(BF16)
    all_gains = jnp.zeros((8, width), F32).at[0].set(gain_attn).at[1].set(gain_ffn)
    all_gains = all_gains.at[2, :HEAD_SIZE].set(gain_query).at[3, :HEAD_SIZE].set(gain_key)
    out_down, out_gate, out_up, out_wo, out_heads, out_gains, layer_out, tokens_grad = backward(
        dims, grad_hidden, down_out, g_down, g_gate, g_up, own_resid, tokens, cotangent, all_gains, acc, qx, kv_all,
        spans, heads, cosine_values[0], sine_lookup[0], own_wo, wqkv, normed,
    )
    gate_grad, up_grad, wq_grad, wk_grad, wv_grad, down_grad, wo_grad = place(
        out_gate, out_up, out_heads, out_down, out_wo
    )
    gain_grads = jnp.sum(out_gains.astype(F32), 0)
    few = HEAD_SIZE // F
    return (
        layer_out.astype(BF16), tokens_grad.astype(BF16), wq_grad, wk_grad, wv_grad, wo_grad, gate_grad, up_grad,
        down_grad, gain_grads[0, :depth], gain_grads[1, :depth], gain_grads[2, :few], gain_grads[3, :few],
    )


def solution(mesh):
    rows = P(("ctx", "fsdp"), None)
    shard = P("fsdp", None)
    gain = P("fsdp")
    return jax.shard_map(
        on_device,
        mesh=mesh,
        in_specs=(rows, P(), shard, shard, shard, shard, shard, shard, shard, gain, gain, gain, gain, rows),
        out_specs=(rows, rows, shard, shard, shard, shard, shard, shard, shard, gain, gain, gain, gain),
        check_vma=False,
    )
```

time: 897 us -> 636 us (0.71)
  local copies, waits for them, and re-layouts: 132 us -> 35.6 us
  blocking collectives: 73.5 us -> 0 us
  other arithmetic: 80.1 us -> 24.7 us
  matrix products: 76 us -> 53.1 us
  Pallas kernels: 523 us -> 510 us
    psum x1 -> x0, blocking collectives: 73.5 us -> none  [on_device(): gain_sums = lax.psum(gain_terms, ('ctx', 'fsdp'))]
    convert_element_type x10 -> x3, other arithmetic: 38.1 us -> 4.45 us  [the longest x1 1.92 us: on_device(): layer_out.astype(BF16)]
    convert_element_type x10 -> x2, local copies, waits for them, and re-layouts: 40 us -> 7.4 us  [the longest x1 4.56 us: on_device(): g_up = dot(hidden_in, grad_upper, over_rows).astype(BF16)]
    unnamed x77 -> x42, local copies, waits for them, and re-layouts: 30.6 us -> 2.97 us
    dot_general x15 -> x11, matrix products: 76 us -> 53.1 us  [dot(): return lax.dot_general(a, b, (dims, ((), ())), preferred_element_type=F32)]
    concatenate x4 -> x0, local copies, waits for them, and re-layouts: 22.5 us -> none  [the longest x1 11.3 us: on_device(): jnp.concatenate([dot(hidden_in, grad_gate, over_rows).astype(BF16), dot(h...]
    pallas_call x6 -> x2, Pallas kernels: 367 us -> 355 us  [the longest x1 334 us: backward(): pl.pallas_call(functools.partial(back_kernel, dims, kinds, steps), out_sh...]
where the time goes in v2:
time: 636 us; the launch traced here: 625 us
  Pallas kernels  510 us (80%)
  matrix products  53.1 us (8%)
  local copies, waits for them, and re-layouts  35.6 us (6%)
  other arithmetic  24.7 us (4%)
    pallas_call x1, Pallas kernels, backward(): pl.pallas_call(functools.partial(back_kernel, dims, kinds, steps), out_sh...  334 us
    pallas_call x1, Pallas kernels, attend(): pl.pallas_call(functools.partial(attend_kernel, dims), out_shape=(jax.Sha...  122 us
    dot_general x11, matrix products, dot(): return lax.dot_general(a, b, (dims, ((), ())), preferred_element_type=F32)  53.1 us
    pallas_call x1, Pallas kernels, gather_inputs(): pl.pallas_call(functools.partial(inputs_kernel, dims), out_shape=(jax.Sha...  33.4 us
    pallas_call x1, Pallas kernels, place(): pl.pallas_call(functools.partial(place_kernel, n), grid=(count,), out_sha...  21.1 us

profile of v2, /device:TPU:0, one launch (start us, length us, event | category | flops | bytes accessed | tf_op | source)
XLA Modules:
  0.0 625.2 jit_solution(17115075815978561756)
XLA Ops:
  7.3 1.9 constant_dynamic-slice_fusion.own_wo
  9.2 3.0 multiply_cosine_fusion
  12.3 33.4 %gather_inputs.1 = (bf16[8,128,1536]{2,1,0:T(8,128)(2,1)}, bf16[4,384,320]{2,1,0:T(8,128)(2,1)}, bf16[4,16,384]{2,1,0:T(8,128)(2,1)}, bf16[4,384,864]{2,1,0:T(8,128)(2,1)}, bf16[4,384,864]{2,1,0:T(8,128)(2,1)}) custom-call(bf16[128,1536]{1,0:T(8,128)(2,1)} %tokens.3, bf16[384,1536]{1,0:T(8,128)(2,1)} %wq.1, bf16[384,512]{1,0:T(8,128)(2,1)} %wk.1, ...), custom_call_target="tpu_custom_call" | custom-call | tf_op jit(solution)/shard_map/gather_inputs/pallas_call | solution.py:292
  45.7 2.7 fusion
  50.8 2.3 copy.47
  53.1 2.4 fusion.4.normed
  56.8 2.6 convolution_bitcast_fusion.heads
  65.2 1.4 maximum_maximum_fusion.qx
  66.5 122.3 %attend.1 = (bf16[4,1024,128]{2,1,0:T(8,128)(2,1)}, f32[3,1024,128]{2,1,0:T(8,128)}, bf16[8,1536,128]{2,1,0:T(8,128)(2,1)}, bf16[8,128,1536]{2,1,0:T(8,128)(2,1)...) custom-call(bf16[3,1024,128]{2,1,0:T(8,128)(2,1)} %maximum_maximum_fusion.qx, ...), custom_call_target="tpu_custom_call" | custom-call | tf_op jit(solution)/shard_map/attend/pallas_call | solution.py:456
  188.8 1.3 slice.215
  190.1 3.1 slice.214
  193.2 3.0 copy.51
  196.2 1.3 copy.49
  197.5 2.3 copy.56
  199.8 1.5 reshape.449
  201.4 1.8 pad_maximum_fusion
  203.6 7.7 %multiply_reduce_fusion = (f32[1024]{0:T(1024)S(1)}, f32[1024,1536]{1,0:T(8,128)S(1)}) fusion(bf16[1024,1536]{0,1:T(8,128)(2,1)S(1)} %bitcast.86, bf16[1536,1536]{1,0:T(8,128)(2,1)} %bitcast.102, bf16[8,128,1536]{2,1,0:T(8,128)(2,1)S(1)} %copy-done.2), kind=kOutput, calls=%fused_computation.11 | convolution fusion | flops 4838128640 | bytes 17305600 | tf_op jit(solution)/shard_map/dot_general | solution.py:1145
  214.0 4.8 fusion.24
  218.9 2.9 fusion.7
  221.8 7.8 %multiply_convert_fusion.1 = (bf16[1024,864]{0,1:T(8,128)(2,1)S(1)}, bf16[1024,864]{0,1:T(8,128)(2,1)}, bf16[1024,864]{0,1:T(8,128)(2,1)}) fusion(f32[1024,864]{0,1:T(8,128)} %fusion.24, f32[1024,864]{0,1:T(8,128)S(1)} %fusion.7, bf16[1024,1536]{1,0:T(8,128)(2,1)S(1)} %multiply_convert_fusion, bf16[1536,864]{1,0:T(8,128)(2,1)S(1)} %bitcast.105), kind=kOutput, calls=%fused_computation.13 | convolution fusion | flops 2731180032 | bytes 18186240 | tf_op jit(solution)/shard_map/dot_general | solution.py:1145
  229.6 4.2 convolution_convert_fusion.3.g_down
  233.8 4.9 convolution_convert_fusion
  238.8 3.1 convolution_convert_fusion.2
  241.9 4.2 convolution_convert_fusion.1
  246.1 4.6 copy.54.g_up
  250.6 2.8 copy.53.g_gate
  253.5 5.9 fusion.25
  259.4 4.9 add_convert_fusion
  264.4 333.7 %backward.1 = (bf16[2,864,1536]{2,1,0:T(8,128)(2,1)}, bf16[8,384,864]{2,1,0:T(8,128)(2,1)}, bf16[8,384,864]{2,1,0:T(8,128)(2,1)}, bf16[2,192,1536]{2,1,0:T(8,128...) custom-call(bf16[2,2,2,128,1536]{4,3,2,1,0:T(8,128)(2,1)} %bitcast.8, ...), custom_call_target="tpu_custom_call" | custom-call | tf_op jit(solution)/shard_map/backward/pallas_call | solution.py:1022
  598.1 1.9 convert_element_type.105
  602.0 1.9 convert_element_type.106
  603.9 21.1 %place.1 = (f32[384,6912]{1,0:T(8,128)}, f32[384,6912]{1,0:T(8,128)}, f32[384,1536]{1,0:T(8,128)}, f32[384,512]{1,0:T(8,128)}, f32[384,512]{1,0:T(8,128)}, /*index=5*/f32[1728,1536]{1,0:T(8,128)}, f32[384,1536]{1,0:T(8,128)}) custom-call(bf16[8,384,864]{2,1,0:T(8,128)(2,1)} %get-tuple-element.174.gate, bf16[8,384,864]{2,1,0:T(8,128)(2,1)} %get-tuple-element.175.up, ...), custom_call_target="tpu_custom_call" | custom-call | tf_op jit(solution)/shard_map/place/pallas_call | solution.py:1094
  (97 shorter events, 21.0 us)
Async XLA Ops:
  6.2 6.1 copy-start.11
  45.7 3.7 copy-start.10
  45.7 7.4 %copy-start.1 = (bf16[8,128,1536]{2,1,0:T(8,128)(2,1)S(1)}, bf16[8,128,1536]{2,1,0:T(8,128)(2,1)}, u32[]{:S(2)}) copy-start(bf16[8,128,1536]{2,1,0:T(8,128)(2,1)} %get-tuple-element.160) | copy-start | bytes 9437188
  50.5 5.0 copy-start.9
  55.6 1.2 copy-start.8
  59.4 4.7 copy-start
  59.4 1.4 copy-start.6
  59.4 1.9 copy-start.7
  62.0 2.1 copy-start.3
  62.0 2.1 copy-start.4
  64.0 1.1 copy-start.5
  201.4 2.2 copy-start.2
  212.3 1.8 copy-start.15
  212.3 6.6 %slice-start = ((s8[5308416]{0:T(1024)(128)(4,1)}), s8[4194304]{0:T(1024)(128)(4,1)S(1)}, s32[]{:S(2)}) async-start(s8[5308416]{0:T(1024)(128)(4,1)} %bitcast.100), calls=%async_computation | async-start | bytes 8388608
  214.0 4.8 slice-start.1
  214.0 4.8 copy-start.12
  218.9 2.9 copy-start.13
  233.8 4.9 copy-start.16
  238.8 3.1 copy-start.17
  253.5 6.0 copy-start.14
  253.5 6.0 copy-start.18

commit v3 on v2

--- a/solution.py
+++ b/solution.py
@@ -212,148 +212,114 @@
     )
 
 
-def inputs_kernel(dims, tokens, wq, wk, wv, gains, w_gate, w_up, tok_full, wqkv, gains_full, gate_cut, up_cut,
-                  q_in, k_in, v_in, qkv_cut, slab_g, slab_u, cut_g, cut_u, send, recv, local):
-    team = Team(*dims)
-    B, F = team.B, team.F
-    sems = Sems(send, recv)
-    loads = [
-        pltpu.make_async_copy(src, dst, local.at[i])
-        for i, (src, dst) in enumerate(
-            [(wq, q_in), (wk, k_in), (wv, v_in), (w_gate, slab_g), (w_up, slab_u), (tokens, tok_full.at[team.p]),
-             (gains, gains_full.at[team.f])]
-        )
-    ]
-    for load in loads:
-        load.start()
-    greet(team_peers(team))
-    rows = tokens.shape[0]
-    gather = Gather(
-        sems, team.p, B * F, team.member, tokens,
-        lambda i: tok_full.at[i],
-        lambda i, k: tok_full.at[i, pl.ds(k * rows // 2, rows // 2)],
-    )
-    gather.begin()
-    small = [sems.copy(gains, gains_full.at[team.f], peer) for peer in row_peers(team)]
-    for copy in small:
-        copy.start()
-    for load in loads[:3]:
-        load.wait()
-    for f in range(F):
-        for y in range(B):
-            h = f * B + y
-
-            @pl.when(team.y == y)
-            def _():
-                qkv_cut[f, :, 0:QW] = q_in[:, h * QW : (h + 1) * QW]
-                qkv_cut[f, :, QW : QW + HEAD_SIZE] = k_in[:, h * HEAD_SIZE : (h + 1) * HEAD_SIZE]
-                qkv_cut[f, :, QW + HEAD_SIZE : QW + 2 * HEAD_SIZE] = v_in[:, h * HEAD_SIZE : (h + 1) * HEAD_SIZE]
-
-    sent = []
-    for d in range(1, F):
-        to = lax.rem(team.f + d, F)
-        sent.append(sems.copy(qkv_cut.at[to], wqkv.at[team.f], team.same_row(to)))
-        sent[-1].start()
-    own = pltpu.make_async_copy(qkv_cut.at[team.f], wqkv.at[team.f], local.at[7])
-    own.start()
-    gather.relay()
-    stores = []
-    for i, (slab, cut, out) in enumerate([(slab_g, cut_g, gate_cut), (slab_u, cut_u, up_cut)]):
-        loads[3 + i].wait()
-        width = cut.shape[-1]
-
-        @pl.loop(0, slab.shape[0] // 32)
-        def _(r):
-            at = pl.ds(pl.multiple_of(r * 32, 32), 32)
-            for f in range(F):
-                for y in range(B):
-                    q = f * B + y
-
-                    @pl.when(team.y == y)
-                    def _():
-                        cut[f, at, :] = slab[at, q * width : (q + 1) * width]
-
-        stores.append(pltpu.make_async_copy(cut, out, local.at[8 + i]))
-        stores[-1].start()
-    gather.end()
-    for copy in small + sent:
-        copy.wait()
-    for copy in loads[5:] + [own] + stores:
-        copy.wait()
-
-
-def gather_inputs(dims, tokens, wq, wk, wv, gains, w_gate, w_up):
-    B, F, T = dims
-    rows, width = tokens.shape
-    depth, ff = w_gate.shape
-    cols = ff // (B * F)
-    copies = Gather.COPIES + 2 * (F - 1)
-    heads = QW + 2 * HEAD_SIZE
-    return pl.pallas_call(
-        functools.partial(inputs_kernel, dims),
-        out_shape=(
-            jax.ShapeDtypeStruct((B * F, rows, width), BF16),
-            jax.ShapeDtypeStruct((F, depth, heads), BF16),
-            jax.ShapeDtypeStruct((F,) + gains.shape, BF16),
-            jax.ShapeDtypeStruct((F, depth, cols), BF16),
-            jax.ShapeDtypeStruct((F, depth, cols), BF16),
-        ),
-        in_specs=[ANY] * 7,
-        out_specs=[ANY] * 5,
-        scratch_shapes=[
-            pltpu.VMEM(wq.shape, BF16),
-            pltpu.VMEM(wk.shape, BF16),
-            pltpu.VMEM(wv.shape, BF16),
-            pltpu.VMEM((F, depth, heads), BF16),
-            pltpu.VMEM(w_gate.shape, BF16),
-            pltpu.VMEM(w_up.shape, BF16),
-            pltpu.VMEM((F, depth, cols), BF16),
-            pltpu.VMEM((F, depth, cols), BF16),
-            pltpu.SemaphoreType.DMA((copies,)),
-            pltpu.SemaphoreType.DMA((copies,)),
-            pltpu.SemaphoreType.DMA((10,)),
-        ],
-        compiler_params=kernel_params(1),
-        name="gather_inputs",
-    )(tokens, wq, wk, wv, gains, w_gate, w_up)
+def unit_and_factor(x):
+    factor = lax.rsqrt(jnp.mean(x * x, -1, keepdims=True) + EPSILON)
+    return x * factor, factor
 
 
 def lane_ids(rows):
     return lax.broadcasted_iota(jnp.int32, (rows, LANES), 1)
+
+
+def inside_document(spans, rows, first_row):
+    row = lax.broadcasted_iota(jnp.int32, (rows, LANES), 0) + first_row
+    return (row >= spans[0:1, :]) & (row < spans[1:2, :])
 
 
 def widen_keys(kv, spans, first_row, kx, vx):
     rows = kv.shape[0]
     lane = lane_ids(rows)
-    row = lax.broadcasted_iota(jnp.int32, (rows, LANES), 0) + first_row
-    inside = (row >= spans[0:1, :]) & (row < spans[1:2, :])
-    wide = kv.astype(F32)
-    kx[...] = jnp.where(lane < HEAD_SIZE, wide, jnp.where(inside, 1.0, 0.0)).astype(BF16)
-    vx[...] = jnp.where(lane < HEAD_SIZE, pltpu.roll(wide, HEAD_SIZE, 1), 1.0).astype(BF16)
+    inside = inside_document(spans, rows, first_row)
+    both = wide(kv)
+    kx[...] = jnp.where(lane < HEAD_SIZE, both, jnp.where(inside, 1.0, 0.0)).astype(BF16)
+    vx[...] = jnp.where(lane < HEAD_SIZE, pltpu.roll(both, HEAD_SIZE, 1), 1.0).astype(BF16)
 
 
 def dot_last(a, b):
     return lax.dot_general(a, b, (((1,), (1,)), ((), ())), preferred_element_type=F32)
 
 
-def attend_kernel(dims, qx, kv, spans, dy, wo, gate_cut, up_cut, kv_all, acc, mixed, dy_full, wo_full, w_gate, w_up,
-                  kx, vx, packed, send, recv, line_send, line_recv, local):
+def rotate(u, cosine, sine):
+    half = u.shape[-1] // 2
+    swapped = jnp.concatenate([-u[:, half:], u[:, :half]], 1)
+    return u * cosine + swapped * sine
+
+
+def front_kernel(dims, tokens, wq, wk, wv, wo, w_gate, w_up, dy, gains, cosine, sine, spans,
+                 tok_full, wqkv, normed, heads, qx, kv_all, acc, mixed, dy_full, wo_full, gate_full, up_full, all_gains,
+                 tok, q_in, k_in, v_in, qkv_cut, qkv, gains_in, slab_g, slab_u, cut_g, cut_u, norm, kv, kx, vx, packed,
+                 send, recv, line_send, line_recv, local):
     team = Team(*dims)
     B, F, T = dims
-    t = team.t
+    t, y, f, p = team.t, team.y, team.f, team.p
     sems = Sems(send, recv)
-    rows = kv.shape[0]
-    part = rows // 2
-    homes = [
-        pltpu.make_async_copy(kv, kv_all.at[t], local.at[0]),
-        pltpu.make_async_copy(dy, dy_full.at[team.p], local.at[1]),
-        pltpu.make_async_copy(wo, wo_full.at[team.f], local.at[2]),
-        pltpu.make_async_copy(gate_cut.at[team.f], w_gate.at[team.f], local.at[3]),
-        pltpu.make_async_copy(up_cut.at[team.f], w_up.at[team.f], local.at[4]),
-    ]
-    for copy in homes:
+    own_rows, width = tokens.shape
+    rows = own_rows * B * F
+    depth = width // F
+    part, block = rows // 2, rows // 4
+    hidden = cut_g.shape[-1]
+    parity = lax.rem(t, 2)
+
+    def home(src, dst, i):
+        copy = pltpu.make_async_copy(src, dst, local.at[i])
         copy.start()
+        return copy
+
+    token_rows = lambda i: pl.ds(pl.multiple_of(i * own_rows, 16), own_rows)
+    shard_rows = lambda i: pl.ds(pl.multiple_of(i * depth, 16), depth)
+    token_load = home(tokens, tok.at[token_rows(p)], 0)
+    small_loads = [home(wq, q_in, 1), home(wk, k_in, 2), home(wv, v_in, 3)]
+    gain_load = home(gains, gains_in.at[f], 4)
+    slab_loads = [home(w_gate, slab_g, 5), home(w_up, slab_u, 6)]
+    homes = [home(dy, dy_full.at[p], 7), home(wo, wo_full.at[f], 8)]
     greet(team_peers(team) + line_peers(team))
+
+    half = own_rows // 2
+    gather_tok = Gather(
+        sems, p, B * F, team.member, tokens, lambda i: tok.at[token_rows(i)],
+        lambda i, k: tok.at[pl.ds(pl.multiple_of(i * own_rows + k * half, 16), half)],
+    )
+    gather_dy = Gather(
+        sems, p, B * F, team.member, dy, lambda i: dy_full.at[i], lambda i, k: dy_full.at[i, pl.ds(k * half, half)]
+    )
+    few = packed.shape[0] // 2
+    gather_mixed = Gather(
+        sems, p, B * F, team.member, packed, lambda i: mixed.at[i], lambda i, k: mixed.at[i, pl.ds(k * few, few)]
+    )
+    partners = []
+    for m in range(1, F):
+        to = f
+        for bit in (1, 2, 4):
+            if m & bit:
+                to = flip(to, bit)
+        partners.append(to)
+    gain_sends = [sems.copy(gains, gains_in.at[f], team.same_row(to)) for to in partners]
+    qkv_sends = [sems.copy(qkv_cut.at[to], qkv.at[shard_rows(f)], team.same_row(to)) for to in partners]
+    half_depth = depth // 2
+    some = pl.ds(pl.multiple_of(parity * half_depth, 16), half_depth)
+    near = team.other_team(t + 1 - 2 * parity)
+    wide_sends, wide_shares = [], []
+    for cut, full in ((cut_g, gate_full), (cut_u, up_full)):
+        sends = [sems.copy(cut.at[partners[0]], full.at[f], team.same_row(partners[0]))]
+        shares = []
+        for to in partners[1:]:
+            sends.append(sems.copy(cut.at[to, some], full.at[f, some], team.same_row(to)))
+            shares.append(sems.copy(full.at[to, some], full.at[to, some], near))
+        wide_sends.append(sends)
+        wide_shares.append(shares)
+    if B == 2 and F == 4:
+        one, two = flip(f, 1), flip(f, 2)
+        other = team.member(lax.rem(p + F, B * F))
+        wo_half = lambda k: pl.ds(pl.multiple_of(k * half_depth, 16), half_depth)
+        mine, theirs = wo_half(y), wo_half(1 - y)
+        wo_first = [
+            sems.copy(wo, wo_full.at[f], team.same_row(one)),
+            sems.copy(wo.at[mine], wo_full.at[f, mine], team.same_row(two)),
+        ]
+        ref = wo_full.at[two, mine]
+        wo_relay = [sems.copy(ref, ref, other), sems.copy(ref, ref, team.same_row(one))]
+        ref = wo_full.at[two, theirs]
+        wo_last = [sems.copy(ref, ref, team.same_row(one))]
 
     def line_copy(d, source, to):
         return pltpu.make_async_remote_copy(
@@ -361,31 +327,101 @@
             device_id=team.other_team(to), device_id_type=MESH,
         )
 
+    gather_tok.begin()
+    for copy in gain_sends:
+        copy.start()
+    for load in small_loads:
+        load.wait()
+    for i in range(F):
+        for row in range(B):
+            h = i * B + row
+
+            @pl.when(y == row)
+            def _():
+                qkv_cut[i, :, 0:QW] = q_in[:, h * QW : (h + 1) * QW]
+                qkv_cut[i, :, QW : QW + HEAD_SIZE] = k_in[:, h * HEAD_SIZE : (h + 1) * HEAD_SIZE]
+                qkv_cut[i, :, QW + HEAD_SIZE : QW + 2 * HEAD_SIZE] = v_in[:, h * HEAD_SIZE : (h + 1) * HEAD_SIZE]
+
+    for copy in qkv_sends:
+        copy.start()
+    qkv[shard_rows(f), :] = qkv_cut[f]
+    gather_tok.relay()
+    for i, (slab, cut, full) in enumerate([(slab_g, cut_g, gate_full), (slab_u, cut_u, up_full)]):
+        slab_loads[i].wait()
+
+        @pl.loop(0, depth // 32)
+        def _(r):
+            here = pl.ds(pl.multiple_of(r * 32, 32), 32)
+            for j in range(F):
+                for row in range(B):
+                    q = j * B + row
+
+                    @pl.when(y == row)
+                    def _():
+                        cut[j, here, :] = slab[here, q * hidden : (q + 1) * hidden]
+
+        for copy in wide_sends[i]:
+            copy.start()
+        homes.append(home(cut.at[f], full.at[f], 9 + i))
+    gather_tok.end()
+    token_load.wait()
+    gain_load.wait()
+    for copy in gain_sends:
+        copy.wait_recv()
+    homes.append(home(tok, tok_full, 11))
+
+    all_gains[...] = jnp.zeros_like(all_gains)
+    for i in range(F):
+        for k, count in ((0, depth), (1, depth), (2, HEAD_SIZE // F), (3, HEAD_SIZE // F)):
+            all_gains[k : k + 1, i * count : (i + 1) * count] = wide(gains_in[i])[k : k + 1, 0:count]
+    gain_q, gain_k = all_gains[2:3, 0:HEAD_SIZE], all_gains[3:4, 0:HEAD_SIZE]
+
+    @pl.loop(0, rows // block)
+    def _(r):
+        here = pl.ds(pl.multiple_of(r * block, block), block)
+        unit, factor = unit_and_factor(wide(tok[here, :]))
+        norm[here, :] = (unit * all_gains[0:1, :]).astype(BF16)
+
+    for copy in qkv_sends:
+        copy.wait_recv()
+    homes += [home(norm, normed, 12), home(qkv, wqkv, 13)]
+
+    @pl.loop(0, rows // block)
+    def _(r):
+        here = pl.ds(pl.multiple_of(r * block, block), block)
+        projected = jnp.dot(norm[here, :], qkv[...], preferred_element_type=F32)
+        lane = lane_ids(block)
+        apart = jnp.where(inside_document(spans, block, t * rows + r * block), 0.0, -APART)
+        cos, sin = cosine[here, :], sine[here, :]
+        for h in range(GROUP + 1):
+            x = projected[:, h * HEAD_SIZE : (h + 1) * HEAD_SIZE]
+            heads[h, here, :] = x
+            unit, factor = unit_and_factor(x)
+            turned = rotate(unit * (gain_q if h < GROUP else gain_k), cos, sin).astype(BF16)
+            if h < GROUP:
+                q = wide(turned) * HEAD_SIZE ** (-0.5)
+                qx[h, here, :] = jnp.where(lane < HEAD_SIZE, jnp.concatenate([q, q], 1), apart).astype(BF16)
+        values = projected[:, (GROUP + 1) * HEAD_SIZE : (GROUP + 2) * HEAD_SIZE]
+        kv[here, :] = jnp.concatenate([wide(turned), values], 1).astype(BF16)
+
     for d in range(1, T):
 
         @pl.when(t + d < T)
         def _():
             line_copy(d, t, t + d).start()
 
-    half_wo, half_dy = wo.shape[0] // 2, dy.shape[0] // 2
-    gather_wo = Gather(
-        sems, team.f, F, team.same_row, wo, lambda i: wo_full.at[i],
-        lambda i, k: wo_full.at[i, pl.ds(k * half_wo, half_wo)],
-    )
-    gather_wo.begin()
-    sent = []
-    for cut, full in ((gate_cut, w_gate), (up_cut, w_up)):
-        for d in range(1, F):
-            to = lax.rem(team.f + d, F)
-            sent.append(sems.copy(cut.at[to], full.at[team.f], team.same_row(to)))
-            sent[-1].start()
-    gather_dy = Gather(
-        sems, team.p, B * F, team.member, dy, lambda i: dy_full.at[i],
-        lambda i, k: dy_full.at[i, pl.ds(k * half_dy, half_dy)],
-    )
+    if B == 2 and F == 4:
+        for copy in wo_first:
+            copy.start()
+    else:
+        gather_wo = Gather(
+            sems, f, F, team.same_row, wo, lambda i: wo_full.at[i],
+            lambda i, k: wo_full.at[i, pl.ds(k * half_depth, half_depth)],
+        )
+        gather_wo.begin()
     gather_dy.begin()
-    homes[0].wait()
-    widen_keys(kv_all[t], spans, t * rows, kx, vx)
+    kv_all[t] = kv[...]
+    widen_keys(kv[...], spans, t * rows, kx, vx)
     causal = lax.broadcasted_iota(jnp.int32, (part, part), 1) <= lax.broadcasted_iota(jnp.int32, (part, part), 0)
 
     def piece(q, k, masked):
@@ -401,7 +437,12 @@
         low = qx[h, part:rows, :]
         acc[h, part:rows, :] = piece(low, 0, False) + piece(low, 1, True)
 
-    gather_wo.relay()
+    def share(i):
+        for arrived, onward in zip(wide_sends[i][1:], wide_shares[i]):
+            arrived.wait_recv()
+            onward.start()
+
+    share(0)
 
     @pl.loop(1, t + 1)
     def _(j):
@@ -412,9 +453,9 @@
         @pl.loop(0, GROUP)
         def _(h):
             for k in range(2):
-                at = pl.ds(k * part, part)
-                q = qx[h, at, :]
-                acc[h, at, :] = acc[h, at, :] + piece(q, 0, False) + piece(q, 1, False)
+                here = pl.ds(k * part, part)
+                q = qx[h, here, :]
+                acc[h, here, :] = acc[h, here, :] + piece(q, 0, False) + piece(q, 1, False)
 
     for h in range(GROUP):
         out = acc[h, :, 0:HEAD_SIZE] / acc[h, :, HEAD_SIZE : 2 * HEAD_SIZE]
@@ -424,22 +465,38 @@
         else:
             packed[rows : rows + part, 0:HEAD_SIZE] = out[0:part]
             packed[rows : rows + part, HEAD_SIZE : 2 * HEAD_SIZE] = out[part:rows]
-    home = pltpu.make_async_copy(packed, mixed.at[team.p], local.at[5])
-    home.start()
-    half_mixed = packed.shape[0] // 2
-    gather_mixed = Gather(
-        sems, team.p, B * F, team.member, packed, lambda i: mixed.at[i],
-        lambda i, k: mixed.at[i, pl.ds(k * half_mixed, half_mixed)],
-    )
+    homes.append(home(packed, mixed.at[p], 14))
     gather_mixed.begin()
+    share(1)
+    if B == 2 and F == 4:
+        wo_first[1].wait_recv()
+        for copy in wo_relay:
+            copy.start()
+    else:
+        gather_wo.relay()
+    gather_dy.relay()
     gather_mixed.relay()
-    gather_dy.relay()
+    if B == 2 and F == 4:
+        wo_relay[0].wait_recv()
+        wo_last[0].start()
     gather_mixed.end()
-    gather_wo.end()
     gather_dy.end()
-    for copy in sent:
-        copy.wait()
-    for copy in homes[1:] + [home]:
+    if B == 2 and F == 4:
+        for copy in (wo_first[0], wo_relay[1], wo_last[0]):
+            copy.wait_recv()
+        for copy in wo_first + wo_relay + wo_last:
+            copy.wait_send()
+    else:
+        gather_wo.end()
+    for sends, shares in zip(wide_sends, wide_shares):
+        sends[0].wait_recv()
+        for copy in shares:
+            copy.wait_recv()
+        for copy in sends + shares:
+            copy.wait_send()
+    for copy in gain_sends + qkv_sends:
+        copy.wait_send()
+    for copy in homes:
         copy.wait()
     for d in range(1, T):
 
@@ -448,37 +505,175 @@
             line_copy(d, t, t + d).wait_send()
 
 
-def attend(dims, qx, kv, spans, dy, wo, gate_cut, up_cut):
+def front(dims, tokens, wq, wk, wv, wo, w_gate, w_up, dy, gains, cosine, sine, spans):
     B, F, T = dims
-    rows = kv.shape[0]
-    copies = 3 * Gather.COPIES + 2 * (F - 1)
+    own_rows, width = tokens.shape
+    n = B * F
+    rows = own_rows * n
+    depth, ff = w_gate.shape
+    hidden = ff // n
+    few = QW + 2 * HEAD_SIZE
+    copies = 4 * Gather.COPIES + 2 * (F - 1) + 2 * (2 * F - 3)
     packed = (rows + rows // 2, LANES)
+    shape = lambda *s: jax.ShapeDtypeStruct(s, BF16)
+    wide_shape = lambda *s: jax.ShapeDtypeStruct(s, F32)
+    vmem = lambda *s: pltpu.VMEM(s, BF16)
     return pl.pallas_call(
-        functools.partial(attend_kernel, dims),
+        functools.partial(front_kernel, dims),
         out_shape=(
-            jax.ShapeDtypeStruct((T, rows, LANES), BF16),
-            jax.ShapeDtypeStruct((GROUP, rows, LANES), F32),
-            jax.ShapeDtypeStruct((B * F,) + packed, BF16),
-            jax.ShapeDtypeStruct((B * F,) + dy.shape, BF16),
-            jax.ShapeDtypeStruct((F,) + wo.shape, BF16),
-            jax.ShapeDtypeStruct(gate_cut.shape, BF16),
-            jax.ShapeDtypeStruct(up_cut.shape, BF16),
+            shape(rows, width), shape(width, few), shape(rows, width), wide_shape(GROUP + 1, rows, HEAD_SIZE),
+            shape(GROUP, rows, LANES), shape(T, rows, LANES), wide_shape(GROUP, rows, LANES), shape(n, *packed),
+            shape(n, own_rows, width), shape(F, depth, width), shape(F, depth, hidden), shape(F, depth, hidden),
+            wide_shape(8, width),
         ),
-        in_specs=[VMEM, ANY, VMEM, ANY, ANY, ANY, ANY],
-        out_specs=[VMEM, VMEM, ANY, ANY, ANY, ANY, ANY],
+        in_specs=[ANY] * 9 + [VMEM] * 3,
+        out_specs=[ANY] * 3 + [VMEM] * 4 + [ANY] * 5 + [VMEM],
         scratch_shapes=[
-            pltpu.VMEM((rows, LANES), BF16),
-            pltpu.VMEM((rows, LANES), BF16),
-            pltpu.VMEM(packed, BF16),
+            vmem(rows, width), vmem(*wq.shape), vmem(*wk.shape), vmem(*wv.shape), vmem(F, depth, few), vmem(width, few),
+            vmem(F, *gains.shape), vmem(depth, ff), vmem(depth, ff), vmem(F, depth, hidden), vmem(F, depth, hidden),
+            vmem(rows, width), vmem(rows, LANES), vmem(rows, LANES), vmem(rows, LANES), vmem(*packed),
             pltpu.SemaphoreType.DMA((copies,)),
             pltpu.SemaphoreType.DMA((copies,)),
             pltpu.SemaphoreType.DMA((T,)),
             pltpu.SemaphoreType.DMA((T,)),
-            pltpu.SemaphoreType.DMA((6,)),
+            pltpu.SemaphoreType.DMA((15,)),
         ],
-        compiler_params=kernel_params(2),
-        name="attend",
-    )(qx, kv, spans, dy, wo, gate_cut, up_cut)
+        compiler_params=kernel_params(1),
+        name="front",
+    )(tokens, wq, wk, wv, wo, w_gate, w_up, dy, gains, cosine, sine, spans)
+
+
+def feed_kernel(dims, tok_in, mixed_in, wo_in, gate_in, up_in, down_in, dy_in, gain, grad_hidden, down_out, g_down,
+                g_gate, g_up, own_resid, tok, mixed, wo, w_gate, w_up, w_down, dy, rows_in, hid, act, dgate, dup,
+                resid, dhid, down, gd, gg, gu, local):
+    B, F, T = dims
+    ctx, f = lax.axis_index("ctx"), lax.axis_index("fsdp")
+    y = lax.rem(ctx, B)
+    p = y * F + f
+    rows, width = tok.shape
+    own_rows = own_resid.shape[0]
+    hidden = w_gate.shape[1]
+    block = resid.shape[0]
+    n = B * F
+    loads = [
+        pltpu.make_async_copy(src, dst, local.at[i])
+        for i, (src, dst) in enumerate(
+            [(mixed_in, mixed), (wo_in, wo), (tok_in, tok), (gate_in, w_gate), (up_in, w_up),
+             (down_in.at[pl.ds(pl.multiple_of(y * hidden, 16), hidden)], w_down), (dy_in, dy)]
+        )
+    ]
+    for load in loads:
+        load.start()
+    for load in loads[:3]:
+        load.wait()
+    half = rows // 2
+
+    @pl.loop(0, rows // block)
+    def _(r):
+        here = pl.ds(pl.multiple_of(r * block, block), block)
+        third = pl.ds(pl.multiple_of(rows + lax.rem(r * block, half), block), block)
+        for i in range(n):
+            h = i % F * B + i // F
+            first = h * QW
+            rows_in[:, first : first + 2 * HEAD_SIZE] = mixed[i, here, :]
+            last = mixed[i, third, :]
+            last = jnp.where(r * block < half, wide(last[:, :HEAD_SIZE]), wide(last[:, HEAD_SIZE:]))
+            rows_in[:, first + 2 * HEAD_SIZE : first + QW] = last.astype(BF16)
+        resid[...] = wide(tok[here, :]) + jnp.dot(rows_in[...], wo[...], preferred_element_type=F32)
+
+        @pl.when(r == lax.div(p * own_rows, block))
+        def _():
+            own_resid[...] = resid[pl.ds(pl.multiple_of(lax.rem(p * own_rows, block), 8), own_rows), :]
+
+        unit, factor = unit_and_factor(resid[...])
+        hid[here, :] = (unit * gain[1:2, :]).astype(BF16)
+
+    for load in loads[3:]:
+        load.wait()
+
+    @pl.loop(0, rows // block)
+    def _(r):
+        here = pl.ds(pl.multiple_of(r * block, block), block)
+        gate = jnp.dot(hid[here, :], w_gate[...], preferred_element_type=F32)
+        upper = jnp.dot(hid[here, :], w_up[...], preferred_element_type=F32)
+        sigma = 1.0 / (1.0 + jnp.exp(-gate))
+        silu = gate * sigma
+        acts = (silu * upper).astype(BF16)
+        act[here, :] = acts
+        dact = dot_last(dy[here, :], w_down[...])
+        dgates = (dact * upper * sigma * (1.0 + gate * (1.0 - sigma))).astype(BF16)
+        dups = (dact * silu).astype(BF16)
+        dgate[here, :] = dgates
+        dup[here, :] = dups
+        down[here, :] = jnp.dot(acts, w_down[...], preferred_element_type=F32).astype(BF16)
+        dhid[here, :] = (dot_last(dgates, w_gate[...]) + dot_last(dups, w_up[...])).astype(BF16)
+
+    stores = []
+
+    def store(src, dst):
+        stores.append(pltpu.make_async_copy(src, dst, local.at[7 + len(stores)]))
+        stores[-1].start()
+
+    store(dhid, grad_hidden)
+    store(down, down_out)
+    over_rows = lambda a, b: lax.dot_general(a, b, (((0,), (0,)), ((), ())), preferred_element_type=F32).astype(BF16)
+
+    for first in range(0, hidden, 256):
+        count = min(256, hidden - first)
+        gd[first : first + count, :] = over_rows(act[:, first : first + count], dy[...])
+    store(gd, g_down)
+
+    @pl.loop(0, width // 256)
+    def _(r):
+        here = pl.ds(pl.multiple_of(r * 256, 256), 256)
+        lhs = hid[:, here]
+        gg[here, :] = over_rows(lhs, dgate[...])
+        gu[here, :] = over_rows(lhs, dup[...])
+
+    store(gg, g_gate)
+    store(gu, g_up)
+    for copy in stores:
+        copy.wait()
+
+
+def feed(dims, tok, mixed, wo, w_gate, w_up, w_down, dy, gains):
+    rows, width = tok.shape
+    hidden = w_gate.shape[1]
+    own_rows = rows // KEY_VALUE_HEADS
+    block = 256
+    shape = lambda s: jax.ShapeDtypeStruct(s, BF16)
+    return pl.pallas_call(
+        functools.partial(feed_kernel, dims),
+        out_shape=(
+            shape((rows, width)), shape((rows, width)), shape((hidden, width)), shape((width, hidden)),
+            shape((width, hidden)), jax.ShapeDtypeStruct((own_rows, width), F32),
+        ),
+        in_specs=[ANY] * 7 + [VMEM],
+        out_specs=[ANY] * 5 + [VMEM],
+        scratch_shapes=[
+            pltpu.VMEM((rows, width), BF16),
+            pltpu.VMEM(mixed.shape, BF16),
+            pltpu.VMEM(wo.shape, BF16),
+            pltpu.VMEM(w_gate.shape, BF16),
+            pltpu.VMEM(w_up.shape, BF16),
+            pltpu.VMEM((hidden, width), BF16),
+            pltpu.VMEM((rows, width), BF16),
+            pltpu.VMEM((block, width), BF16),
+            pltpu.VMEM((rows, width), BF16),
+            pltpu.VMEM((rows, hidden), BF16),
+            pltpu.VMEM((rows, hidden), BF16),
+            pltpu.VMEM((rows, hidden), BF16),
+            pltpu.VMEM((block, width), F32),
+            pltpu.VMEM((rows, width), BF16),
+            pltpu.VMEM((rows, width), BF16),
+            pltpu.VMEM((hidden, width), BF16),
+            pltpu.VMEM((width, hidden), BF16),
+            pltpu.VMEM((width, hidden), BF16),
+            pltpu.SemaphoreType.DMA((12,)),
+        ],
+        compiler_params=pltpu.CompilerParams(vmem_limit_bytes=VMEM_LIMIT),
+        name="feed",
+    )(tok, mixed, wo, w_gate, w_up, w_down, dy, gains)
 
 
 HOP = 2
@@ -671,17 +866,6 @@
                 self.drain(out.at[0], bulk.at[self.HOME, k, 0])
                 self.drain(others, bulk.at[self.HAND, k, 0])
                 self.drain(others, bulk.at[self.INTO, k, 0])
-
-
-def rotate_back(u, cosine, sine):
-    half = u.shape[-1] // 2
-    swapped = jnp.concatenate([-u[:, half:], u[:, :half]], 1)
-    return u * cosine - swapped * sine
-
-
-def unit_and_factor(x):
-    factor = lax.rsqrt(jnp.mean(x * x, -1, keepdims=True) + EPSILON)
-    return x * factor, factor
 
 
 def first_steps(dims):
@@ -910,7 +1094,7 @@
                     u, gain = dq[h, here, 0:HEAD_SIZE] * HEAD_SIZE ** (-0.5), gain_q
                 else:
                     u, gain = dkv_sum[here, 0:HEAD_SIZE], gain_k
-                u = rotate_back(u, cos, sin)
+                u = rotate(u, cos, -sin)
                 unit, factor = unit_and_factor(heads[h, here, :])
                 term = jnp.sum(u * unit, 0, keepdims=True)
                 if h < GROUP:
@@ -1125,24 +1309,9 @@
     )
 
 
-def apply_rotary(values_in, cosine_values, sine_lookup, sign):
-    half_width = values_in.shape[-1] // 2
-    swapped = jnp.concatenate([-values_in[..., half_width:], values_in[..., :half_width]], -1)
-    return values_in * cosine_values + swapped * (sine_lookup * sign)
-
-
-def scaled_input(values_in):
-    factor = lax.rsqrt(jnp.mean(values_in * values_in, -1, keepdims=True) + EPSILON)
-    return (values_in * factor, factor)
-
-
 def norm_back(upstream, unit_rows, factor, gain_row):
     lifted = upstream * gain_row
     return factor * (lifted - unit_rows * jnp.mean(lifted * unit_rows, -1, keepdims=True))
-
-
-def dot(a, b, dims=((1,), (0,))):
-    return lax.dot_general(a, b, (dims, ((), ())), preferred_element_type=F32)
 
 
 def on_device(
@@ -1163,18 +1332,9 @@
     gains = jnp.zeros((16, max(depth, LANES)), BF16)
     gains = gains.at[0, :depth].set(attn_gain).at[1, :depth].set(ffn_gain)
     gains = gains.at[2, : HEAD_SIZE // F].set(q_gain).at[3, : HEAD_SIZE // F].set(key_norm_gain)
-    tok_full, wqkv, gains_full, gate_cut, up_cut = gather_inputs(dims, tokens, wq, wk, wv, gains, w_gate, w_up)
-    gains_full = gains_full.astype(F32)
-    gain_attn = gains_full[:, 0, :depth].reshape(-1)
-    gain_ffn = gains_full[:, 1, :depth].reshape(-1)
-    gain_query = gains_full[:, 2, : HEAD_SIZE // F].reshape(-1)
-    gain_key = gains_full[:, 3, : HEAD_SIZE // F].reshape(-1)
-    wqkv = wqkv.reshape(width, -1)
-
     token_index = t * rows + jnp.arange(rows, dtype=jnp.int32)
     docs, places = doc_layout(lengths, token_index)
     cosine_values, sine_lookup = rotation(places, HEAD_SIZE)
-    cosine_values, sine_lookup = cosine_values[None], sine_lookup[None]
     ends = jnp.cumsum(lengths)
     ndocs = lengths.shape[0]
     big = jnp.int32(2**30)
@@ -1184,61 +1344,17 @@
     ])
     spans = jnp.concatenate([spans, jnp.zeros((6, LANES), jnp.int32)])
 
-    inputs = tok_full.reshape(rows, width).astype(F32)
-    unit_attn, factor_attn = scaled_input(inputs)
-    normed = (unit_attn * gain_attn).astype(BF16)
-    projected = dot(normed, wqkv)
-    heads = jnp.transpose(projected.reshape(rows, GROUP + 2, HEAD_SIZE), (1, 0, 2))
-    q_unit, q_factor = scaled_input(heads[:GROUP])
-    k_unit, k_factor = scaled_input(heads[GROUP])
-    queries = apply_rotary(q_unit * gain_query, cosine_values, sine_lookup, 1.0).astype(BF16)
-    own_keys = apply_rotary(k_unit * gain_key, cosine_values[0], sine_lookup[0], 1.0).astype(BF16)
-    own_values = heads[GROUP + 1].astype(BF16)
-    scale = HEAD_SIZE ** (-0.5)
-    apart = jnp.where(docs[:, None] == jnp.arange(ndocs)[None, :], 0.0, -APART).astype(BF16)
-    apart = jnp.broadcast_to(apart[None], (GROUP, rows, ndocs))
-    queries = (queries * jnp.asarray(scale, BF16)).astype(BF16)
-    qx = jnp.concatenate([queries, apart, jnp.zeros((GROUP, rows, LANES - HEAD_SIZE - ndocs), BF16)], -1)
-    kv = jnp.concatenate([own_keys, own_values], -1)
-    kv_all, acc, mixed, dy_full, wo_full, gate_w, up_w = attend(
-        dims, qx, kv, spans, cotangent, wo, gate_cut, up_cut
+    (tok_full, wqkv, normed, heads, qx, kv_all, acc, mixed, dy_full, wo_full, gate_w, up_w, all_gains) = front(
+        dims, tokens, wq, wk, wv, wo, w_gate, w_up, cotangent, gains, cosine_values, sine_lookup, spans
     )
-    both = mixed[:, :rows].reshape(B, F, rows, 2 * HEAD_SIZE)
-    third = mixed[:, rows:].reshape(B, F, rows // 2, 2, HEAD_SIZE)
-    third = jnp.swapaxes(third, 2, 3).reshape(B, F, rows, HEAD_SIZE)
-    mixed_heads = jnp.concatenate([both, third], -1)
-    mixed_heads = jnp.transpose(mixed_heads, (2, 1, 0, 3)).reshape(rows, QUERY_HEADS * HEAD_SIZE)
-    wo_full = wo_full.reshape(-1, width)
-    gate_w = gate_w.reshape(width, hidden)
-    up_w = up_w.reshape(width, hidden)
-    down_w = lax.dynamic_slice_in_dim(w_down, y * hidden, hidden, 0)
     own_wo = lax.dynamic_slice_in_dim(wo, y * QW, QW, 0)
-    dy_full = dy_full.reshape(rows, width)
-
-    resid = inputs + dot(mixed_heads, wo_full)
-    unit_ffn, factor_ffn = scaled_input(resid)
-    hidden_in = (unit_ffn * gain_ffn).astype(BF16)
-    gate = dot(hidden_in, gate_w)
-    upper = dot(hidden_in, up_w)
-    sigma = jax.nn.sigmoid(gate)
-    silu_gate = gate * sigma
-    act_rows = (silu_gate * upper).astype(BF16)
-    down_out = dot(act_rows, down_w).astype(BF16)
-
-    grad_act = dot(dy_full, down_w, ((1,), (1,)))
-    grad_gate = (grad_act * upper * sigma * (1.0 + gate * (1.0 - sigma))).astype(BF16)
-    grad_upper = (grad_act * silu_gate).astype(BF16)
-    grad_hidden = (dot(grad_gate, gate_w, ((1,), (1,))) + dot(grad_upper, up_w, ((1,), (1,)))).astype(BF16)
-    own_resid = lax.dynamic_slice_in_dim(resid, p * own_rows, own_rows, 0)
-    over_rows = ((0,), (0,))
-    g_down = dot(act_rows, dy_full, over_rows).astype(BF16)
-    g_gate = dot(hidden_in, grad_gate, over_rows).astype(BF16)
-    g_up = dot(hidden_in, grad_upper, over_rows).astype(BF16)
-    all_gains = jnp.zeros((8, width), F32).at[0].set(gain_attn).at[1].set(gain_ffn)
-    all_gains = all_gains.at[2, :HEAD_SIZE].set(gain_query).at[3, :HEAD_SIZE].set(gain_key)
+    grad_hidden, down_out, g_down, g_gate, g_up, own_resid = feed(
+        dims, tok_full, mixed, wo_full.reshape(-1, width), gate_w.reshape(width, hidden),
+        up_w.reshape(width, hidden), w_down, dy_full.reshape(rows, width), all_gains,
+    )
     out_down, out_gate, out_up, out_wo, out_heads, out_gains, layer_out, tokens_grad = backward(
         dims, grad_hidden, down_out, g_down, g_gate, g_up, own_resid, tokens, cotangent, all_gains, acc, qx, kv_all,
-        spans, heads, cosine_values[0], sine_lookup[0], own_wo, wqkv, normed,
+        spans, heads, cosine_values, sine_lookup, own_wo, wqkv, normed,
     )
     gate_grad, up_grad, wq_grad, wk_grad, wv_grad, down_grad, wo_grad = place(
         out_gate, out_up, out_heads, out_down, out_wo

time: 636 us -> 548 us (0.86)
  matrix products: 53.1 us -> 0 us
  local copies, waits for them, and re-layouts: 35.6 us -> 6.13 us
  other arithmetic: 24.7 us -> 10.2 us
  Pallas kernels: 510 us -> 523 us
    dot_general x11 -> x0, matrix products: 53.1 us -> none  [dot(): return lax.dot_general(a, b, (dims, ((), ())), preferred_element_type=F32)]
    pallas_call x1, Pallas kernels: 334 us -> 345 us  [backward(): pl.pallas_call(functools.partial(back_kernel, dims, kinds, steps), out_sh...]
    convert_element_type x3 -> x0, local copies, waits for them, and re-layouts: 7.43 us -> none  [the longest x1 4.56 us: on_device(): g_up = dot(hidden_in, grad_upper, over_rows).astype(BF16)]
    reshape x3 -> x0, local copies, waits for them, and re-layouts: 6.84 us -> none  [the longest x2 3.85 us: on_device(): third = jnp.swapaxes(third, 2, 3).reshape(B, F, rows, HEAD_SIZE)]
    slice x7 -> x0, local copies, waits for them, and re-layouts: 6.54 us -> none  [the longest x1 3.07 us: on_device(): both = mixed[:, :rows].reshape(B, F, rows, 2 * HEAD_SIZE)]
where the time goes in v3:
time: 548 us; the launch traced here: 540 us
  Pallas kernels  523 us (95%)
  other arithmetic  10.2 us (2%)
  local copies, waits for them, and re-layouts  6.13 us (1%)
    pallas_call x1, Pallas kernels, backward(): pl.pallas_call(functools.partial(back_kernel, dims, kinds, steps), out_sh...  345 us
    pallas_call x1, Pallas kernels, front(): pl.pallas_call(functools.partial(front_kernel, dims), out_shape=(shape(ro...  109 us
    pallas_call x1, Pallas kernels, feed(): pl.pallas_call(functools.partial(feed_kernel, dims), out_shape=(shape((ro...  47.8 us
    pallas_call x1, Pallas kernels, place(): pl.pallas_call(functools.partial(place_kernel, n), grid=(count,), out_sha...  21.1 us

profile of v3, /device:TPU:0, one launch (start us, length us, event | category | flops | bytes accessed | tf_op | source)
XLA Modules:
  0.0 540.1 jit_solution(9368351505231305140)
XLA Ops:
  0.7 0.8 reduce-window.4
  1.5 0.7 subtract_bitcast_fusion
  2.2 0.1 pad.19.clone
  2.2 0.7 reshape.225
  2.9 0.7 reshape.226
  3.6 0.7 fusion.spans
  4.3 0.1 select_reduce_fusion
  4.5 0.8 scatter.24
  5.3 0.8 scatter.25.gains
  6.1 0.0 copy-start
  6.1 1.9 constant_dynamic-slice_fusion.own_wo
  8.0 1.9 multiply_sine_fusion
  9.9 1.3 pad_maximum_fusion
  11.2 0.0 copy-done
  11.2 108.6 %front.1 = (bf16[1024,1536]{1,0:T(8,128)(2,1)}, bf16[1536,320]{1,0:T(8,128)(2,1)}, bf16[1024,1536]{1,0:T(8,128)(2,1)}, f32[4,1024,64]{2,1,0:T(8,128)}, bf16[3,10...) custom-call(bf16[128,1536]{1,0:T(8,128)(2,1)} %tokens.3, ...), custom_call_target="tpu_custom_call" | custom-call | tf_op jit(solution)/shard_map/front/pallas_call | solution.py:521
  119.8 47.8 %feed.1 = (bf16[1024,1536]{1,0:T(8,128)(2,1)}, bf16[1024,1536]{1,0:T(8,128)(2,1)}, bf16[864,1536]{1,0:T(8,128)(2,1)}, bf16[1536,864]{1,0:T(8,128)(2,1)}, bf16[1536,864]{1,0:T(8,128)(2,1)}, /*index=5*/f32[128,1536]{1,0:T(8,128)}) custom-call(bf16[1024,1536]{1,0:T(8,128)(2,1)} %get-tuple-element.119.tok_in, bf16[8,1536,128]{2,1,0:T(8,128)(2,1)} %get-tuple-element.120.mixed_in, ...), custom_call_target="tpu_custom_call" | custom-call | tf_op jit(solution)/shard_map/feed/pallas_call | solution.py:645
  167.7 345.4 %backward.1 = (bf16[2,864,1536]{2,1,0:T(8,128)(2,1)}, bf16[8,384,864]{2,1,0:T(8,128)(2,1)}, bf16[8,384,864]{2,1,0:T(8,128)(2,1)}, bf16[2,192,1536]{2,1,0:T(8,128...) custom-call(bf16[2,2,2,128,1536]{4,3,2,1,0:T(8,128)(2,1)} %bitcast.2, ...), custom_call_target="tpu_custom_call" | custom-call | tf_op jit(solution)/shard_map/backward/pallas_call | solution.py:1206
  513.0 1.9 convert_element_type.17
  514.9 0.9 convert_reduce_fusion
  515.9 0.5 slice_bitcast_fusion
  516.4 0.6 slice_reduce_fusion
  517.0 1.9 convert_element_type.18
  518.9 21.1 %place.1 = (f32[384,6912]{1,0:T(8,128)}, f32[384,6912]{1,0:T(8,128)}, f32[384,1536]{1,0:T(8,128)}, f32[384,512]{1,0:T(8,128)}, f32[384,512]{1,0:T(8,128)}, /*index=5*/f32[1728,1536]{1,0:T(8,128)}, f32[384,1536]{1,0:T(8,128)}) custom-call(bf16[8,384,864]{2,1,0:T(8,128)(2,1)} %get-tuple-element.140.gate, bf16[8,384,864]{2,1,0:T(8,128)(2,1)} %get-tuple-element.141.up, ...), custom_call_target="tpu_custom_call" | custom-call | tf_op jit(solution)/shard_map/place/pallas_call | solution.py:1278
  (6 shorter events, 0.1 us)
Async XLA Ops:
  6.1 5.1 copy-start

commit v4 on v3

v4 whole, which is shorter than its diff:
```python
import functools

import jax
import jax.numpy as jnp
import numpy as np
from jax import lax
from jax.experimental import pallas as pl
from jax.experimental.pallas import tpu as pltpu
from jax.sharding import PartitionSpec as P

QUERY_HEADS = 24
KEY_VALUE_HEADS = 8
HEAD_SIZE = 64
GROUP = QUERY_HEADS // KEY_VALUE_HEADS
QW = GROUP * HEAD_SIZE
LANES = 128
NDOCS = 4

EPSILON = 1e-05
ROPE_BASE = 1000000.0
APART = 16384.0

MESH = pl.DeviceIdType.MESH
F32 = jnp.float32
BF16 = jnp.bfloat16
ANY = pl.BlockSpec(memory_space=pl.ANY)
VMEM = pl.BlockSpec(memory_space=pltpu.VMEM)
VMEM_LIMIT = 56 * 1024 * 1024


class Team:
    def __init__(self, B, F, T):
        self.B, self.F, self.T = B, F, T
        ctx, self.f = lax.axis_index("ctx"), lax.axis_index("fsdp")
        self.t, self.y = lax.div(ctx, B), lax.rem(ctx, B)
        self.p = self.y * F + self.f

    def member(self, p):
        return (self.t * self.B + lax.div(p, self.F), lax.rem(p, self.F))

    def same_row(self, f):
        return (self.t * self.B + self.y, f)

    def other_team(self, t):
        return (t * self.B + self.y, self.f)


def flip(p, bit):
    return p + bit * (1 - 2 * lax.rem(lax.div(p, bit), 2))


def bit_of(p, bit):
    return lax.rem(lax.div(p, bit), 2)


class Sems:
    def __init__(self, send, recv):
        self.send, self.recv, self.used = send, recv, 0

    def copy(self, src, dst, device):
        i = self.used
        self.used += 1
        return pltpu.make_async_remote_copy(
            src_ref=src,
            dst_ref=dst,
            send_sem=self.send.at[i],
            recv_sem=self.recv.at[i],
            device_id=device,
            device_id_type=MESH,
        )


def greet(devices):
    barrier = pltpu.get_barrier_semaphore()
    for device in devices:
        pl.semaphore_signal(barrier, inc=1, device_id=device, device_id_type=MESH)
    pl.semaphore_wait(barrier, len(devices))


def team_peers(team):
    n = team.B * team.F
    return [team.member(lax.rem(team.p + d, n)) for d in range(1, n)]


def line_peers(team):
    return [team.other_team(lax.rem(team.t + d, team.T)) for d in range(1, team.T)]


def row_peers(team):
    return [team.same_row(lax.rem(team.f + d, team.F)) for d in range(1, team.F)]


class Gather:
    def __init__(self, sems, me, count, device, own, block, half, order="both"):
        bits = count.bit_length() - 1
        one, two = flip(me, 1), flip(me, 2)
        send = lambda src, dst, to: sems.copy(src, dst, device(to))
        again = lambda ref, to: send(ref, ref, to)
        self.first = [send(own, block(me), flip(me, 1 << k)) for k in range(bits)]
        self.over = [again(block(two), one)]
        self.halves, self.corner = [], []
        if count == 8:
            four = flip(me, 4)
            far = flip(two, 4)
            self.over.append(again(block(four), one))
            if order == "both":
                self.halves = [again(half(two, 0), four), again(half(four, 1), two)]
                self.corner = [again(half(far, 0), one), again(half(far, 1), one)]
            else:
                self.halves = [again(block(two), four)]
                self.corner = [again(block(far), one)]

    def begin(self):
        for copy in self.first:
            copy.start()

    def relay(self):
        self.first[1].wait_recv()
        self.over[0].start()
        if self.halves:
            self.halves[0].start()
            self.first[2].wait_recv()
            for copy in self.halves[1:]:
                copy.start()
            self.over[1].start()

    def end(self):
        for arrived, onward in zip(self.halves, self.corner):
            arrived.wait_recv()
            onward.start()
        self.first[0].wait_recv()
        for copy in self.over + self.corner:
            copy.wait_recv()
        for copy in self.first + self.over + self.halves + self.corner:
            copy.wait_send()

    COPIES = 9


def scatter_parts(width, order):
    if order == "both":
        return [(0, width // 2, 2, 4), (width // 2, width // 2, 4, 2)]
    return [(0, width, 2, 4)]


def scatter_shapes(rows, width, order):
    shapes = [pltpu.VMEM((2, 2, rows, width), BF16)]
    for _, columns, _, _ in scatter_parts(width, order):
        shapes += [pltpu.VMEM((2, rows, columns), BF16)] * 2 + [pltpu.VMEM((rows, columns), BF16)] * 2
    return shapes


def wide(v):
    return v.astype(F32)


class Scatter:
    COPIES = 5

    def __init__(self, sems, team, x, scratch, order):
        self.x, self.r0 = x, scratch[0]
        p = team.p
        self.b = bit_of(p, 1), bit_of(p, 2), bit_of(p, 4)
        send = lambda src, dst, bit: sems.copy(src, dst, team.member(flip(p, bit)))
        self.first = send(x.at[:, :, 1 - self.b[0]], self.r0, 1)
        self.parts = []
        for i, (at, columns, one, two) in enumerate(scatter_parts(x.shape[-1], order)):
            s1, r1, s2, r2 = scratch[1 + 4 * i : 5 + 4 * i]
            self.parts.append((pl.ds(at, columns), one, s1, r1, s2, r2, send(s1, r1, one), send(s2, r2, two)))

    def term(self, b2, b1, columns):
        return wide(self.x[b2, b1, self.b[0], :, columns]) + wide(self.r0[b2, b1, :, columns])

    def begin(self):
        self.first.start()

    def relay(self):
        b0, b1, b2 = self.b
        self.first.wait_recv()
        for columns, one, s1, r1, s2, r2, send1, send2 in self.parts:
            for k in range(2):
                s1[k] = (self.term(k, 1 - b1, columns) if one == 2 else self.term(1 - b2, k, columns)).astype(BF16)
            send1.start()

    def relay_again(self):
        b0, b1, b2 = self.b
        for columns, one, s1, r1, s2, r2, send1, send2 in self.parts:
            send1.wait_recv()
            if one == 2:
                total = self.term(1 - b2, b1, columns) + wide(r1[1 - b2])
            else:
                total = self.term(b2, 1 - b1, columns) + wide(r1[1 - b1])
            s2[...] = total.astype(BF16)
            send2.start()

    def end(self, store):
        b0, b1, b2 = self.b
        for columns, one, s1, r1, s2, r2, send1, send2 in self.parts:
            send2.wait_recv()
            store(columns, self.term(b2, b1, columns) + wide(r1[b2 if one == 2 else b1]) + wide(r2[...]))
        for copy in [self.first] + [copy for part in self.parts for copy in part[6:]]:
            copy.wait_send()


def kernel_params(collective_id):
    return pltpu.CompilerParams(
        collective_id=collective_id, has_side_effects=True, vmem_limit_bytes=VMEM_LIMIT
    )


def unit_and_factor(x):
    factor = lax.rsqrt(jnp.mean(x * x, -1, keepdims=True) + EPSILON)
    return x * factor, factor


def lane_ids(rows):
    return lax.broadcasted_iota(jnp.int32, (rows, LANES), 1)


def inside_document(spans, rows, first_row):
    row = lax.broadcasted_iota(jnp.int32, (rows, LANES), 0) + first_row
    return (row >= spans[0:1, :]) & (row < spans[1:2, :])


def widen_keys(kv, spans, first_row, kx, vx):
    rows = kv.shape[0]
    lane = lane_ids(rows)
    inside = inside_document(spans, rows, first_row)
    both = wide(kv)
    kx[...] = jnp.where(lane < HEAD_SIZE, both, jnp.where(inside, 1.0, 0.0)).astype(BF16)
    vx[...] = jnp.where(lane < HEAD_SIZE, pltpu.roll(both, HEAD_SIZE, 1), 1.0).astype(BF16)


def dot_last(a, b):
    return lax.dot_general(a, b, (((1,), (1,)), ((), ())), preferred_element_type=F32)


def fill_tables(t, lengths, freq, cosine, sine, spans):
    rows = cosine.shape[0]
    ends, total = [], 0
    for d in range(NDOCS):
        total = total + lengths[d]
        ends.append(total)
    lane = lax.broadcasted_iota(jnp.int32, spans.shape, 1)
    row = lax.broadcasted_iota(jnp.int32, spans.shape, 0)
    first, past = jnp.zeros(spans.shape, jnp.int32), jnp.full(spans.shape, 2**30, jnp.int32)
    for d in range(NDOCS):
        first = jnp.where(lane == HEAD_SIZE + d, ends[d] - lengths[d], first)
        past = jnp.where(lane == HEAD_SIZE + d, ends[d], past)
    spans[...] = jnp.where(row == 0, first, past)
    half = HEAD_SIZE // 2
    parts = LANES // half
    few = rows // parts
    shape = (few, LANES)
    token = lax.broadcasted_iota(jnp.int32, shape, 0) + lax.div(lax.broadcasted_iota(jnp.int32, shape, 1), half) * few
    token = token + t * rows
    start = jnp.zeros(shape, jnp.int32)
    for d in range(NDOCS):
        start = jnp.where(token >= ends[d], ends[d], start)
    angles = (token - start).astype(F32) * freq[...]
    cos, sin = jnp.cos(angles), jnp.sin(angles)
    for i in range(parts):
        here, lanes = slice(i * few, (i + 1) * few), slice(i * half, (i + 1) * half)
        cosine[here, :] = jnp.concatenate([cos[:, lanes]] * parts, 1)
        sine[here, :] = jnp.concatenate([-sin[:, lanes], sin[:, lanes]] * (parts // 2), 1)


def front_kernel(dims, tokens, wq, wk, wv, wo, w_gate, w_up, gains, freq, lengths,
                 cosine, sine, spans, tok_full, wqkv, normed, heads, qx, kv_all, acc, mixed, wo_full, wide_full, all_gains,
                 tok, q_in, k_in, v_in, qkv_cut, qkv, gains_in, slab_g, slab_u, cut, norm, kv, kx, vx, packed,
                 send, recv, line_send, line_recv, local):
    team = Team(*dims)
    B, F, T = dims
    t, y, f, p = team.t, team.y, team.f, team.p
    sems = Sems(send, recv)
    own_rows, width = tokens.shape
    rows = own_rows * B * F
    depth = width // F
    part, block = rows // 2, rows // 4
    hidden = cut.shape[-1] // 2
    parity = lax.rem(t, 2)

    def home(src, dst, i):
        copy = pltpu.make_async_copy(src, dst, local.at[i])
        copy.start()
        return copy

    token_rows = lambda i: pl.ds(pl.multiple_of(i * own_rows, 16), own_rows)
    shard_rows = lambda i: pl.ds(pl.multiple_of(i * depth, 16), depth)
    token_load = home(tokens, tok.at[token_rows(p)], 0)
    small_loads = [home(wq, q_in, 1), home(wk, k_in, 2), home(wv, v_in, 3)]
    gain_load = home(gains, gains_in.at[f], 4)
    slab_loads = [home(w_gate, slab_g, 5), home(w_up, slab_u, 6)]
    homes = [home(wo, wo_full.at[f], 7)]
    greet(team_peers(team) + line_peers(team))

    half = own_rows // 2
    gather_tok = Gather(
        sems, p, B * F, team.member, tokens, lambda i: tok.at[token_rows(i)],
        lambda i, k: tok.at[pl.ds(pl.multiple_of(i * own_rows + k * half, 16), half)],
        "tall",
    )
    few = packed.shape[1] // 2

    def gather_half(which):
        return Gather(
            sems, p, B * F, team.member, packed.at[which], lambda i: mixed.at[which, i],
            lambda i, k: mixed.at[which, i, pl.ds(k * few, few)],
            "both" if which else "tall",
        )

    gather_mixed = [gather_half(0), gather_half(1)]
    partners = []
    for m in range(1, F):
        to = f
        for bit in (1, 2, 4):
            if m & bit:
                to = flip(to, bit)
        partners.append(to)
    gain_sends = [sems.copy(gains, gains_in.at[f], team.same_row(to)) for to in partners]
    half_depth = depth // 2
    some = pl.ds(pl.multiple_of(parity * half_depth, 16), half_depth)
    near = team.other_team(t + 1 - 2 * parity)
    some_of = lambda i: pl.ds(pl.multiple_of(i * depth + parity * half_depth, 16), half_depth)
    qkv_sends = [sems.copy(qkv_cut.at[partners[0]], qkv.at[shard_rows(f)], team.same_row(partners[0]))]
    qkv_shares = []
    for to in partners[1:]:
        qkv_sends.append(sems.copy(qkv_cut.at[to, some], qkv.at[some_of(f)], team.same_row(to)))
        qkv_shares.append(sems.copy(qkv.at[some_of(to)], qkv.at[some_of(to)], near))
    wide_near = sems.copy(cut.at[partners[0]], wide_full.at[f], team.same_row(partners[0]))
    wide_sends, wide_shares = [[], []], [[], []]
    quarter = half_depth // 2
    for i in range(2):
        some = pl.ds(pl.multiple_of(parity * half_depth + i * quarter, 16), quarter)
        for to in partners[1:]:
            wide_sends[i].append(sems.copy(cut.at[to, some], wide_full.at[f, some], team.same_row(to)))
            wide_shares[i].append(sems.copy(wide_full.at[to, some], wide_full.at[to, some], near))
    if B == 2 and F == 4:
        one, two = flip(f, 1), flip(f, 2)
        other = team.member(lax.rem(p + F, B * F))
        wo_half = lambda k: pl.ds(pl.multiple_of(k * half_depth, 16), half_depth)
        mine, theirs = wo_half(y), wo_half(1 - y)
        wo_first = [
            sems.copy(wo, wo_full.at[f], team.same_row(one)),
            sems.copy(wo.at[mine], wo_full.at[f, mine], team.same_row(two)),
        ]
        ref = wo_full.at[two, mine]
        wo_relay = [sems.copy(ref, ref, other), sems.copy(ref, ref, team.same_row(one))]
        ref = wo_full.at[two, theirs]
        wo_last = [sems.copy(ref, ref, team.same_row(one))]

    def line_copy(d, source, to, r):
        here = pl.ds(pl.multiple_of(r * block, block), block)
        return pltpu.make_async_remote_copy(
            src_ref=kv.at[here], dst_ref=kv_all.at[source, here], send_sem=line_send.at[d, r],
            recv_sem=line_recv.at[source, r], device_id=team.other_team(to), device_id_type=MESH,
        )

    gather_tok.begin()
    for copy in gain_sends:
        copy.start()
    fill_tables(t, lengths, freq, cosine, sine, spans)
    for load in small_loads:
        load.wait()
    for i in range(F):
        for row in range(B):
            h = i * B + row

            @pl.when(y == row)
            def _():
                qkv_cut[i, :, 0:QW] = q_in[:, h * QW : (h + 1) * QW]
                qkv_cut[i, :, QW : QW + HEAD_SIZE] = k_in[:, h * HEAD_SIZE : (h + 1) * HEAD_SIZE]
                qkv_cut[i, :, QW + HEAD_SIZE : QW + 2 * HEAD_SIZE] = v_in[:, h * HEAD_SIZE : (h + 1) * HEAD_SIZE]

    for copy in qkv_sends:
        copy.start()
    qkv[shard_rows(f), :] = qkv_cut[f]
    for load in slab_loads:
        load.wait()

    @pl.loop(0, depth // 32)
    def _(r):
        here = pl.ds(pl.multiple_of(r * 32, 32), 32)
        for j in range(F):
            for row in range(B):
                q = j * B + row

                @pl.when(y == row)
                def _():
                    cut[j, here, 0:hidden] = slab_g[here, q * hidden : (q + 1) * hidden]
                    cut[j, here, hidden : 2 * hidden] = slab_u[here, q * hidden : (q + 1) * hidden]

    gather_tok.relay()
    for arrived, onward in zip(qkv_sends[1:], qkv_shares):
        arrived.wait_recv()
        onward.start()
    for copy in wide_sends[0] + [wide_near]:
        copy.start()
    if B == 2 and F == 4:
        for copy in wo_first:
            copy.start()
    else:
        gather_wo = Gather(
            sems, f, F, team.same_row, wo, lambda i: wo_full.at[i],
            lambda i, k: wo_full.at[i, pl.ds(k * half_depth, half_depth)],
        )
        gather_wo.begin()
    for copy in wide_sends[1]:
        copy.start()
    homes.append(home(cut.at[f], wide_full.at[f], 9))
    gather_tok.end()
    token_load.wait()
    gain_load.wait()
    for copy in gain_sends:
        copy.wait_recv()
    homes.append(home(tok, tok_full, 11))

    all_gains[...] = jnp.zeros_like(all_gains)
    for i in range(F):
        for k, count in ((0, depth), (1, depth), (2, HEAD_SIZE // F), (3, HEAD_SIZE // F)):
            all_gains[k : k + 1, i * count : (i + 1) * count] = wide(gains_in[i])[k : k + 1, 0:count]
    gain_q, gain_k = all_gains[2:3, 0:HEAD_SIZE], all_gains[3:4, 0:HEAD_SIZE]

    @pl.loop(0, rows // block)
    def _(r):
        here = pl.ds(pl.multiple_of(r * block, block), block)
        unit, factor = unit_and_factor(wide(tok[here, :]))
        norm[here, :] = (unit * all_gains[0:1, :]).astype(BF16)

    for copy in qkv_sends[:1] + qkv_shares:
        copy.wait_recv()
    homes += [home(norm, normed, 12), home(qkv, wqkv, 13)]

    lane = lane_ids(block)
    same_head = lax.div(lax.broadcasted_iota(jnp.int32, (LANES, LANES), 0), HEAD_SIZE) == lax.div(
        lax.broadcasted_iota(jnp.int32, (LANES, LANES), 1), HEAD_SIZE
    )
    same_head = jnp.where(same_head, 1.0, 0.0).astype(BF16)
    gain_pairs = [jnp.concatenate([gain_q, gain_q], 1), jnp.concatenate([gain_q, gain_k], 1)]

    @pl.loop(0, rows // block)
    def _(r):
        here = pl.ds(pl.multiple_of(r * block, block), block)
        projected = jnp.dot(norm[here, :], qkv[...], preferred_element_type=F32)
        apart = jnp.where(inside_document(spans, block, t * rows + r * block), 0.0, -APART)
        cos, sin = cosine[here, :], sine[here, :]
        turned = []
        for i in range(2):
            x = projected[:, i * LANES : (i + 1) * LANES]
            heads[i, here, :] = x
            square = x * x
            high = square.astype(BF16)
            rest = (square - wide(high)).astype(BF16)
            total = jnp.dot(high, same_head, preferred_element_type=F32) + jnp.dot(
                rest, same_head, preferred_element_type=F32
            )
            u = x * lax.rsqrt(total * (1.0 / HEAD_SIZE) + EPSILON) * gain_pairs[i]
            first = lax.rem(lane, HEAD_SIZE) < HEAD_SIZE // 2
            swapped = jnp.where(first, pltpu.roll(u, LANES - HEAD_SIZE // 2, 1), pltpu.roll(u, HEAD_SIZE // 2, 1))
            turned.append(wide((u * cos + swapped * sin).astype(BF16)))
        for h in range(GROUP):
            q = turned[h // 2] * HEAD_SIZE ** (-0.5)
            q = pltpu.roll(q, HEAD_SIZE, 1) if h % 2 else q
            qx[h, here, :] = jnp.where(lane < HEAD_SIZE, q, apart).astype(BF16)
        values = projected[:, (GROUP + 1) * HEAD_SIZE : (GROUP + 2) * HEAD_SIZE]
        keys = pltpu.roll(turned[1], HEAD_SIZE, 1)
        kv[here, :] = jnp.where(lane < HEAD_SIZE, keys, jnp.concatenate([values, values], 1)).astype(BF16)
        for d in range(1, T):

            @pl.when(t + d < T)
            def _():
                line_copy(d, t, t + d, r).start()

    kv_all[t] = kv[...]
    widen_keys(kv[...], spans, t * rows, kx.at[t], vx.at[t])
    causal = lax.broadcasted_iota(jnp.int32, (part, part), 1) <= lax.broadcasted_iota(jnp.int32, (part, part), 0)

    def piece(q, source, k, masked):
        scores = dot_last(q, kx[source, k * part : (k + 1) * part, :])
        weights = jnp.exp(scores)
        if masked:
            weights = jnp.where(causal, weights, 0.0)
        return jnp.dot(weights.astype(BF16), vx[source, k * part : (k + 1) * part, :], preferred_element_type=F32)

    def pass_weights(i):
        for arrived, onward in zip(wide_sends[i], wide_shares[i]):
            arrived.wait_recv()
            onward.start()

    def pass_wo():
        if B == 2 and F == 4:
            wo_first[1].wait_recv()
            for copy in wo_relay:
                copy.start()
        else:
            gather_wo.relay()

    for which in range(2):
        mine = slice(which * part, (which + 1) * part)

        @pl.loop(0, GROUP)
        def _(h):
            q = qx[h, mine, :]
            total = piece(q, t, which, True)
            acc[h, mine, :] = total + piece(q, t, 0, False) if which else total

        pass_weights(which)
        if which:
            gather_mixed[0].relay()

        @pl.loop(1, t + 1)
        def _(j):
            source = t - j
            if which == 0:
                for r in range(4):
                    line_copy(0, source, t, r).wait_recv()
                widen_keys(kv_all[source], spans, source * rows, kx.at[source], vx.at[source])

            @pl.loop(0, GROUP)
            def _(h):
                q = qx[h, mine, :]
                acc[h, mine, :] = acc[h, mine, :] + piece(q, source, 0, False) + piece(q, source, 1, False)

        for h in range(GROUP):
            out = acc[h, mine, 0:HEAD_SIZE] / acc[h, mine, HEAD_SIZE : 2 * HEAD_SIZE]
            out = out.astype(BF16)
            if h < 2:
                packed[which, 0:part, h * HEAD_SIZE : (h + 1) * HEAD_SIZE] = out
            else:
                packed[which, part : part + part // 2, 0:HEAD_SIZE] = out[0 : part // 2]
                packed[which, part : part + part // 2, HEAD_SIZE : 2 * HEAD_SIZE] = out[part // 2 : part]
        homes.append(home(packed.at[which], mixed.at[which, p], 14 + which))
        gather_mixed[which].begin()
        if which == 0:
            pass_wo()

    gather_mixed[0].end()
    gather_mixed[1].relay()
    if B == 2 and F == 4:
        wo_relay[0].wait_recv()
        wo_last[0].start()
    gather_mixed[1].end()
    if B == 2 and F == 4:
        for copy in (wo_first[0], wo_relay[1], wo_last[0]):
            copy.wait_recv()
        for copy in wo_first + wo_relay + wo_last:
            copy.wait_send()
    else:
        gather_wo.end()
    for copy in [wide_near] + wide_shares[0] + wide_shares[1]:
        copy.wait_recv()
    for copy in [wide_near] + wide_sends[0] + wide_sends[1] + wide_shares[0] + wide_shares[1]:
        copy.wait_send()
    for copy in gain_sends + qkv_sends + qkv_shares:
        copy.wait_send()
    for copy in homes:
        copy.wait()
    for d in range(1, T):

        @pl.when(t + d < T)
        def _():
            for r in range(4):
                line_copy(d, t, t + d, r).wait_send()


def front(dims, tokens, wq, wk, wv, wo, w_gate, w_up, gains, freq, lengths):
    B, F, T = dims
    own_rows, width = tokens.shape
    n = B * F
    rows = own_rows * n
    depth, ff = w_gate.shape
    hidden = ff // n
    few = QW + 2 * HEAD_SIZE
    copies = 4 * Gather.COPIES + (F - 1) + 3 * (2 * F - 3)
    packed = (rows // 2 + rows // 4, LANES)
    shape = lambda *s: jax.ShapeDtypeStruct(s, BF16)
    wide_shape = lambda *s: jax.ShapeDtypeStruct(s, F32)
    vmem = lambda *s: pltpu.VMEM(s, BF16)
    return pl.pallas_call(
        functools.partial(front_kernel, dims),
        out_shape=(
            wide_shape(rows, LANES), wide_shape(rows, LANES), jax.ShapeDtypeStruct((8, LANES), jnp.int32),
            shape(rows, width), shape(width, few), shape(rows, width), wide_shape((GROUP + 1) // 2, rows, LANES),
            shape(GROUP, rows, LANES), shape(T, rows, LANES), wide_shape(GROUP, rows, LANES), shape(2, n, *packed),
            shape(F, depth, width), shape(F, depth, 2 * hidden),
            wide_shape(8, width),
        ),
        in_specs=[ANY] * 8 + [VMEM, pl.BlockSpec(memory_space=pltpu.SMEM)],
        out_specs=[VMEM] * 3 + [ANY] * 3 + [VMEM] * 4 + [ANY] * 3 + [VMEM],
        scratch_shapes=[
            vmem(rows, width), vmem(*wq.shape), vmem(*wk.shape), vmem(*wv.shape), vmem(F, depth, few), vmem(width, few),
            vmem(F, *gains.shape), vmem(depth, ff), vmem(depth, ff), vmem(F, depth, 2 * hidden),
            vmem(rows, width), vmem(rows, LANES), vmem(T, rows, LANES), vmem(T, rows, LANES), vmem(2, *packed),
            pltpu.SemaphoreType.DMA((copies,)),
            pltpu.SemaphoreType.DMA((copies,)),
            pltpu.SemaphoreType.DMA((T, 4)),
            pltpu.SemaphoreType.DMA((T, 4)),
            pltpu.SemaphoreType.DMA((16,)),
        ],
        compiler_params=kernel_params(1),
        name="front",
    )(tokens, wq, wk, wv, wo, w_gate, w_up, gains, freq, lengths)


def feed_kernel(dims, tok_in, mixed_in, wo_in, wide_in, down_in, dy_in, gain, grad_hidden, g_down,
                g_wide, g_last, own_resid, layer_out, tok, mixed, wo, w_wide, w_down, dy, rows_in, hid, both, act, dwide,
                resid, down, gd, gw, gl, *rest):
    scratch, (send, recv, local) = rest[:9], rest[9:]
    team = Team(*dims)
    B, F, y, p = team.B, team.F, team.y, team.p
    rows, width = tok.shape
    own_rows = own_resid.shape[0]
    hidden = w_down.shape[0]
    early = gw.shape[1]
    block = resid.shape[0]
    n = B * F
    dy_rows = lambda i: pl.ds(pl.multiple_of(i * own_rows, 16), own_rows)
    loads = [
        pltpu.make_async_copy(src, dst, local.at[i])
        for i, (src, dst) in enumerate(
            [(mixed_in, mixed), (wo_in, wo), (tok_in, tok), (wide_in, w_wide),
             (down_in.at[pl.ds(pl.multiple_of(y * hidden, 16), hidden)], w_down), (dy_in, dy.at[dy_rows(p)])]
        )
    ]
    for load in loads:
        load.start()
    greet([team.member(flip(p, bit)) for bit in (1, 2, 4)])
    sems = Sems(send, recv)
    scatter = Scatter(sems, team, down, scratch, "both")
    half = own_rows // 2
    gather = Gather(
        sems, p, n, team.member, dy_in, lambda i: dy.at[dy_rows(i)],
        lambda i, k: dy.at[pl.ds(pl.multiple_of(i * own_rows + k * half, 16), half)],
    )
    gather.begin()
    for load in loads[:3]:
        load.wait()

    @pl.loop(0, rows // block)
    def _(r):
        here = pl.ds(pl.multiple_of(r * block, block), block)
        which, later = lax.div(r, 2), lax.rem(r, 2)
        place = pl.ds(pl.multiple_of(later * block, block), block)
        for i in range(n):
            h = i % F * B + i // F
            first = h * QW
            rows_in[:, first : first + 2 * HEAD_SIZE] = mixed[which, i, place, :]
            last = mixed[which, i, 2 * block : 3 * block, :]
            last = jnp.where(later == 0, wide(last[:, :HEAD_SIZE]), wide(last[:, HEAD_SIZE:]))
            rows_in[:, first + 2 * HEAD_SIZE : first + QW] = last.astype(BF16)
        pl.when(r == 2)(gather.relay)
        resid[...] = wide(tok[here, :]) + jnp.dot(rows_in[...], wo[...], preferred_element_type=F32)

        @pl.when(r == lax.div(p * own_rows, block))
        def _():
            own_resid[...] = resid[pl.ds(pl.multiple_of(lax.rem(p * own_rows, block), 8), own_rows), :]

        unit, factor = unit_and_factor(resid[...])
        hid[here, :] = (unit * gain[1:2, :]).astype(BF16)

    for load in loads[3:]:
        load.wait()

    @pl.loop(0, rows // block)
    def _(r):
        here = pl.ds(pl.multiple_of(r * block, block), block)
        product = jnp.dot(hid[here, :], w_wide[...], preferred_element_type=F32)
        gate, upper = product[:, :hidden], product[:, hidden:]
        both[0, here, :] = gate
        both[1, here, :] = upper
        sigma = 1.0 / (1.0 + jnp.exp(-gate))
        acts = (gate * sigma * upper).astype(BF16)
        act[here, :] = acts
        out = jnp.dot(acts, w_down[...], preferred_element_type=F32).astype(BF16)
        for i in range(block // own_rows):
            m = r * (block // own_rows) + i
            down[lax.div(m, 4), lax.rem(lax.div(m, 2), 2), lax.rem(m, 2)] = out[i * own_rows : (i + 1) * own_rows]

    scatter.begin()
    gather.end()

    @pl.loop(0, rows // block)
    def _(r):
        here = pl.ds(pl.multiple_of(r * block, block), block)
        pl.when(r == 1)(scatter.relay)
        gate, upper = both[0, here, :], both[1, here, :]
        sigma = 1.0 / (1.0 + jnp.exp(-gate))
        dact = dot_last(dy[here, :], w_down[...])
        dwide[here, 0:hidden] = (dact * upper * sigma * (1.0 + gate * (1.0 - sigma))).astype(BF16)
        dwide[here, hidden : 2 * hidden] = (dact * (gate * sigma)).astype(BF16)
        tok[here, :] = dot_last(dwide[here, :], w_wide[...]).astype(BF16)

    stores = []

    def store(src, dst):
        stores.append(pltpu.make_async_copy(src, dst, local.at[6 + len(stores)]))
        stores[-1].start()

    store(tok, grad_hidden)
    scatter.relay_again()
    over_rows = lambda a, b: lax.dot_general(a, b, (((0,), (0,)), ((), ())), preferred_element_type=F32).astype(BF16)

    for first in range(0, hidden, 256):
        count = min(256, hidden - first)
        gd[first : first + count, :] = over_rows(act[:, first : first + count], dy[...])
    store(gd, g_down)

    @pl.loop(0, width // 256)
    def _(r):
        here = pl.ds(pl.multiple_of(r * 256, 256), 256)
        product = over_rows(hid[:, here], dwide[...])
        gw[here, :] = product[:, :early]
        gl[here, 0 : 2 * hidden - early] = product[:, early:]
        pltpu.make_async_copy(gw.at[here], g_wide.at[here], local.at[10]).start()
        pltpu.make_async_copy(gl.at[here], g_last.at[here], local.at[11]).start()

    def put(columns, total):
        layer_out[:, columns] = own_resid[:, columns] + total

    scatter.end(put)
    for copy in stores:
        copy.wait()
    pltpu.make_async_copy(gw, g_wide, local.at[10]).wait()
    pltpu.make_async_copy(gl, g_last, local.at[11]).wait()


def feed(dims, tok, mixed, wo, w_wide, w_down, dy, gains):
    rows, width = tok.shape
    hidden = w_wide.shape[1] // 2
    own_rows = rows // KEY_VALUE_HEADS
    early = early_lanes(hidden)
    last = 2 * hidden - early + QW + 2 * HEAD_SIZE
    block = rows // 4
    shape = lambda s: jax.ShapeDtypeStruct(s, BF16)
    return pl.pallas_call(
        functools.partial(feed_kernel, dims),
        out_shape=(
            shape((rows, width)), shape((hidden, width)), shape((width, early)), shape((width, last)),
            jax.ShapeDtypeStruct((own_rows, width), F32), jax.ShapeDtypeStruct((own_rows, width), F32),
        ),
        in_specs=[ANY] * 6 + [VMEM],
        out_specs=[ANY] * 4 + [VMEM] * 2,
        scratch_shapes=[
            pltpu.VMEM((rows, width), BF16),
            pltpu.VMEM(mixed.shape, BF16),
            pltpu.VMEM(wo.shape, BF16),
            pltpu.VMEM(w_wide.shape, BF16),
            pltpu.VMEM((hidden, width), BF16),
            pltpu.VMEM((rows, width), BF16),
            pltpu.VMEM((block, width), BF16),
            pltpu.VMEM((rows, width), BF16),
            pltpu.VMEM((2, rows, hidden), F32),
            pltpu.VMEM((rows, hidden), BF16),
            pltpu.VMEM((rows, 2 * hidden), BF16),
            pltpu.VMEM((block, width), F32),
            pltpu.VMEM((2, 2, 2, own_rows, width), BF16),
            pltpu.VMEM((hidden, width), BF16),
            pltpu.VMEM((width, early), BF16),
            pltpu.VMEM((width, last), BF16),
        ]
        + scatter_shapes(own_rows, width, "both")
        + [
            pltpu.SemaphoreType.DMA((Scatter.COPIES + Gather.COPIES,)),
            pltpu.SemaphoreType.DMA((Scatter.COPIES + Gather.COPIES,)),
            pltpu.SemaphoreType.DMA((12,)),
        ],
        compiler_params=pltpu.CompilerParams(
            collective_id=2, has_side_effects=True, vmem_limit_bytes=60 * 1024 * 1024
        ),
        name="feed",
    )(tok, mixed, wo, w_wide, w_down, dy, gains)


HOP = 2
LAG = 3
ORDER = "both"


class GradSum:
    RED, LEFT, RIGHT, HAND, OVER, HOME, INTO = range(7)

    def __init__(self, team, kinds, red_recv, fin_recv, hand_recvs, bulk):
        self.team, self.kinds = team, kinds
        self.red_recv, self.fin_recv, self.hand_recvs, self.bulk = red_recv, fin_recv, hand_recvs, bulk
        self.opposite = team.member(lax.rem(team.p + team.F, team.B * team.F))
        self.low, self.high = team.T // 2 - 1, team.T // 2

    @staticmethod
    def steps(kinds, T):
        return max(first + rows // step for rows, step, first in kinds) + HOP * T + LAG

    def remote(self, src, dst, send_sem, recv_sem, device):
        return pltpu.make_async_remote_copy(
            src_ref=src, dst_ref=dst, send_sem=send_sem, recv_sem=recv_sem, device_id=device, device_id_type=MESH
        )

    def where(self, k, c):
        g, step, how = self.kinds[k][0], self.kinds[k][4], self.kinds[k][6]
        if how != "rows":
            return pl.ds(pl.multiple_of(c * step, 16), step), None, None
        F = self.team.F
        turn = lax.rem(c, F)
        to = lax.rem(turn, 2) * (F // 2) + lax.div(turn, 2)
        row = lax.div(c, F) * step
        return pl.ds(pl.multiple_of(to * (g.shape[0] // F) + row, 16), step), to, row

    def spare(self, k, c):
        step = self.kinds[k][4]
        return pl.ds(pl.multiple_of(lax.div(c, 2) * step, 16), step)

    def reduce(self, k, c, i, root):
        g, land, land2 = self.kinds[k][:3]
        team = self.team
        t, T = team.t, team.T
        at, _, _ = self.where(k, c)
        red = self.bulk.at[self.RED, k, 0]

        def inward(side, dst):
            to = team.other_team(t + 1 - 2 * side)
            self.remote(g.at[at], dst, red, self.red_recv.at[side, i], to).start()

        def add():
            g[at, :] = (wide(g[at, :]) + wide(land[at, :])).astype(BF16)

        @pl.when(t < root)
        def _():
            @pl.when(t > 0)
            def _():
                self.remote(g.at[at], land.at[at], red, self.red_recv.at[0, i], team.other_team(t)).wait_recv()
                add()

            inward(0, land.at[at])

        @pl.when(t > root)
        def _():
            @pl.when(t < T - 1)
            def _():
                self.remote(g.at[at], land.at[at], red, self.red_recv.at[1, i], team.other_team(t)).wait_recv()
                add()

            @pl.when(t - 1 == root)
            def _():
                inward(1, land2.at[self.spare(k, c)])

            @pl.when(t - 1 != root)
            def _():
                inward(1, land.at[at])

    def finish(self, k, c, i, root):
        g, land, land2, out, step, first, how = self.kinds[k]
        team, bulk = self.team, self.bulk
        B, F, T, t, y, f = team.B, team.F, team.T, team.t, team.y, team.f
        at, to, row = self.where(k, c)
        red = bulk.at[self.RED, k, 0]

        def outward(side):
            to_team = team.other_team(t - 1 + 2 * side)
            sem = bulk.at[self.RIGHT if side else self.LEFT, k, 0]
            return self.remote(land.at[at], land.at[at], sem, self.fin_recv.at[i], to_team)

        @pl.when(t == root)
        def _():
            total = wide(g[at, :])
            if self.low > 0:
                self.remote(g.at[at], land.at[at], red, self.red_recv.at[0, i], team.other_team(t)).wait_recv()
                total = total + wide(land[at, :])
                self.remote(g.at[at], land2.at[self.spare(k, c)], red, self.red_recv.at[1, i],
                            team.other_team(t)).wait_recv()
                total = total + wide(land2[self.spare(k, c), :])
            land[at, :] = total.astype(BF16)

        @pl.when(t != root)
        def _():
            outward(0).wait_recv()

        @pl.when((t <= root) & (t > 0))
        def _():
            outward(0).start()

        @pl.when((t >= root) & (t < T - 1))
        def _():
            outward(1).start()

        if how == "rows":
            dst = out.at[f * B + y, pl.ds(pl.multiple_of(row, 16), step)]

            @pl.when(to == f)
            def _():
                pltpu.make_async_copy(land.at[at], dst, bulk.at[self.HOME, k, 0]).start()
                if B == 2:
                    self.remote(land.at[at], dst, bulk.at[self.OVER, k, 0], bulk.at[self.INTO, k, 0],
                                self.opposite).start()

            @pl.when(to != f)
            def _():
                self.remote(land.at[at], dst, bulk.at[self.HAND, k, 0], self.hand_recvs[k].at[f, lax.div(row, step)],
                            team.same_row(to)).start()
        elif how == "stay":
            dst = out.at[y, at]
            pltpu.make_async_copy(land.at[at], dst, bulk.at[self.HOME, k, 0]).start()
            if B == 2:
                self.remote(land.at[at], dst, bulk.at[self.OVER, k, 0], bulk.at[self.INTO, k, 0],
                            self.opposite).start()
        else:
            for index in range(F):
                src = land.at[pl.ds(16 * index, 16)]
                for line in range(B):

                    @pl.when(team.p == line * F + index)
                    def _():
                        pltpu.make_async_copy(src, out.at[team.p], bulk.at[self.HOME, k, 0]).start()

                    @pl.when(team.p != line * F + index)
                    def _():
                        self.remote(src, out.at[team.p], bulk.at[self.HAND, k, 0], bulk.at[self.INTO, k, 0],
                                    (t * B + line, index)).start()

    def pass_over(self, k, c, i, root):
        g, land, land2, out, step, first, how = self.kinds[k]
        if how != "rows":
            return
        team = self.team
        at, to, row = self.where(k, c)

        @pl.when(to == team.f)
        def _():
            for d in range(1, team.F):
                source = lax.rem(team.f + d, team.F)
                ref = out.at[source * team.B + team.y, pl.ds(pl.multiple_of(row, 16), step)]
                self.remote(land.at[at], ref, self.bulk.at[self.HAND, k, 0],
                            self.hand_recvs[k].at[source, lax.div(row, step)], team.same_row(team.f)).wait_recv()
                if team.B == 2:
                    self.remote(ref, ref, self.bulk.at[self.OVER, k, 1], self.bulk.at[self.INTO, k, 0],
                                self.opposite).start()

    def each(self, i, body):
        root = self.low + lax.rem(lax.max(i, 0), 2)
        for k, (g, land, land2, out, step, first, how) in enumerate(self.kinds):
            count = g.shape[0] // step
            pl.when((i >= first) & (i < first + count))(functools.partial(body, k, i - first, i, root))

    def step(self, s):
        T, t = self.team.T, self.team.t
        self.each(s - HOP * lax.min(t, T - 1 - t), self.reduce)
        for parity in range(2):
            root = self.low + parity
            distance = jnp.where(t < root, root - t, t - root)
            i = s - HOP * (T // 2 + distance)
            for wait, body in ((0, self.finish), (LAG, self.pass_over)):
                j = i - wait
                pl.when((j >= 0) & (lax.rem(lax.max(j, 0), 2) == parity))(functools.partial(self.each, j, body))

    def drain(self, ref, sem):
        pltpu.make_async_copy(ref, ref, sem).wait()

    def end(self):
        bulk, B, F, T, t = self.bulk, self.team.B, self.team.F, self.team.T, self.team.t
        low, high = self.low, self.high
        for k, (g, land, land2, out, step, first, how) in enumerate(self.kinds):
            rows = g.shape[0]
            some = lambda n: g.at[pl.ds(0, n)]
            count = rows // step
            even = (count + 1 - first % 2) // 2 * step
            odd = rows - even

            def drain_some(condition, n, which):
                if n:

                    @pl.when(condition)
                    def _():
                        self.drain(some(n), bulk.at[which, k, 0])

            drain_some((t != low) & (t != high), rows, self.RED)
            drain_some(t == low, odd, self.RED)
            drain_some(t == high, even, self.RED)
            drain_some((t > 0) & (t <= low), rows, self.LEFT)
            drain_some(t == high, odd, self.LEFT)
            drain_some((t < T - 1) & (t >= high), rows, self.RIGHT)
            drain_some(t == low, even, self.RIGHT)
            if how == "rows":
                shard = rows // F
                self.drain(some(rows - shard), bulk.at[self.HAND, k, 0])
                self.drain(some(shard), bulk.at[self.HOME, k, 0])
                if B == 2:
                    self.drain(some(shard), bulk.at[self.OVER, k, 0])
                    self.drain(some(rows - shard), bulk.at[self.OVER, k, 1])
                    self.drain(g, bulk.at[self.INTO, k, 0])
            elif how == "stay":
                self.drain(g, bulk.at[self.HOME, k, 0])
                if B == 2:
                    self.drain(g, bulk.at[self.OVER, k, 0])
                    self.drain(g, bulk.at[self.INTO, k, 0])
            else:
                others = out.at[pl.ds(0, B * F - 1)]
                self.drain(out.at[0], bulk.at[self.HOME, k, 0])
                self.drain(others, bulk.at[self.HAND, k, 0])
                self.drain(others, bulk.at[self.INTO, k, 0])


def first_steps(dims):
    at = dict(scatter1=3, scatter2=12, resid=18, relay=24, heads=31, own_wo=35)
    at["attention"] = at["own_wo"] + 1
    at["keys"] = at["attention"] + 2 * GROUP * dims[2] + 2
    at["turn"] = at["keys"] + 1
    at["normed"] = at["turn"] + 4
    at["products"] = at["normed"] + 2
    at["again1"] = at["products"] + 3
    at["again2"] = at["again1"] + 6
    at["tokens"] = at["again2"] + 7
    return at


def early_lanes(hidden):
    return 2 * hidden // LANES * LANES


def grad_kinds(dims, depth, hidden):
    at = first_steps(dims)
    early = early_lanes(hidden)
    kinds, place = [], 0
    for rows, width, step, ready, how in (
        (hidden, depth, 32, 0, "stay"),
        (depth, early, 32, 0, "rows"),
        (QW, depth, 48, at["own_wo"] + 1, "stay"),
        (depth, 2 * hidden - early + QW + 2 * HEAD_SIZE, 96, at["products"] + 3, "rows"),
        (16 * dims[1], max(depth // dims[1], LANES), 16 * dims[1], at["tokens"] + 1, "gain"),
    ):
        place = max(place, ready)
        kinds.append((rows, width, step, place, how))
        place += rows // step
    return kinds


def back_kernel(dims, kinds, steps, grad_hidden, g_down, g_wide, g_last, resid, tokens, cotangent, gains, acc, qx, kv_all, spans,
                heads, cosine, sine, wo, wqkv, normed,
                out_down, out_wide, out_wo, out_last, out_gains, tokens_grad,
                xs, own_down, own_wide, own_gwo, own_last, own_gains,
                land_down, land_wide, land_wo, land_last, land_gains,
                also_down, also_wide, also_wo, also_last, also_gains,
                grad_resid, attn_own, big, dox, mixed, dq, dkv, kv_in, dkv_sum, turned, small, kx, vx, dk, dv, wq_in, own_wo, *rest):
    count = len(scatter_parts(resid.shape[-1], ORDER)) * 4 + 1
    scratch1, rest = rest[:count], rest[count:]
    send, recv, line_send, line_recv, red_recv, fin_recv, hand_wide, hand_last, bulk, local = rest
    team = Team(*dims)
    B, F, T = dims
    t, p = team.t, team.p
    at = first_steps(dims)
    own_rows, width = resid.shape
    rows = qx.shape[1]
    part = rows // 2
    block = rows // 4
    depth = width // F
    sems = Sems(send, recv)
    loads = [
        pltpu.make_async_copy(src, dst, local.at[i])
        for i, (src, dst) in enumerate(
            [(grad_hidden, xs), (g_down, own_down), (g_wide, own_wide), (g_last, own_last), (wqkv, wq_in),
             (wo.at[pl.ds(pl.multiple_of(team.y * QW, 16), QW)], own_wo)]
        )
    ]
    for load in loads:
        load.start()
    own_gains[...] = jnp.zeros_like(own_gains)
    greet(team_peers(team) + line_peers(team))
    loads[0].wait()
    scatter = Scatter(sems, team, xs, scratch1, ORDER)
    scatter.begin()
    again = Scatter(sems, team, xs, scratch1, ORDER)
    half = own_rows // 2
    gather = Gather(
        sems, p, B * F, team.member, attn_own,
        lambda i: big.at[pl.ds(pl.multiple_of(i * own_rows, 16), own_rows)],
        lambda i, k: big.at[pl.ds(pl.multiple_of(i * own_rows + k * half, 16), half)],
    )
    sums = GradSum(
        team,
        [
            (own, land, also, out) + kind[2:]
            for own, land, also, out, kind in zip(
                (own_down, own_wide, own_gwo, own_last, own_gains),
                (land_down, land_wide, land_wo, land_last, land_gains),
                (also_down, also_wide, also_wo, also_last, also_gains),
                (out_down, out_wide, out_wo, out_last, out_gains),
                kinds,
            )
        ],
        red_recv, fin_recv, [None, hand_wide, None, hand_last, None], bulk,
    )
    loads[1].wait()
    gain_attn, gain_ffn = gains[0:1, :], gains[1:2, :]
    gain_q, gain_k = gains[2:3, 0:HEAD_SIZE], gains[3:4, 0:HEAD_SIZE]
    home = pltpu.make_async_copy(attn_own, big.at[pl.ds(pl.multiple_of(p * own_rows, 16), own_rows)], local.at[6])
    fetch = pltpu.make_async_copy(normed, big, local.at[7])

    def resid_phase():
        def store(columns, total):
            grad_resid[:, columns] = total

        scatter.end(store)
        term = jnp.zeros((1, width), F32)
        for r in range(0, own_rows, 32):
            here = slice(r, r + 32)
            unit, factor = unit_and_factor(resid[here, :])
            upstream = grad_resid[here, :]
            term = term + jnp.sum(upstream * unit, 0, keepdims=True)
            total = wide(cotangent[here, :]) + norm_back(upstream, unit, factor, gain_ffn)
            grad_resid[here, :] = total
            attn_own[here, :] = total.astype(BF16)
        small[1:2, :] = term
        home.start()
        gather.begin()

    def heads_phase():
        gather.end()
        home.wait()

    def heads_unit(r):
        lane = lane_ids(block)
        here = pl.ds(pl.multiple_of(r * block, block), block)
        grad = dot_last(big[here, :], own_wo[...]).astype(BF16)
        for h in range(GROUP):
            sums_h = acc[h, here, :]
            total = pltpu.roll(sums_h, HEAD_SIZE, 1)
            out = sums_h / total
            mixed[here, h * HEAD_SIZE : (h + 1) * HEAD_SIZE] = out[:, :HEAD_SIZE].astype(BF16)
            do = wide(grad[:, h * HEAD_SIZE : (h + 1) * HEAD_SIZE])
            do = jnp.concatenate([do, jnp.zeros_like(do)], 1)
            delta = -jnp.sum(jnp.where(lane < HEAD_SIZE, do * out, 0.0), 1, keepdims=True)

            def put(x, first, value):
                for i in range(3):
                    x = jnp.where(lane == first + i, wide(value.astype(BF16)), x)
                    value = value - wide(value.astype(BF16))
                return x

            dox[h, here, :] = put(do, HEAD_SIZE, delta).astype(BF16)
            log_sum = -jnp.log(jnp.where(lane < HEAD_SIZE, total, sums_h))
            qx[h, here, :] = put(wide(qx[h, here, :]), HEAD_SIZE + NDOCS, log_sum).astype(BF16)

    def own_wo_phase():
        own_gwo[...] = lax.dot_general(
            mixed[...], big[...], (((0,), (0,)), ((), ())), preferred_element_type=F32
        ).astype(BF16)
        dq[...] = jnp.zeros_like(dq)

    causal = lax.broadcasted_iota(jnp.int32, (part, part), 0) <= lax.broadcasted_iota(jnp.int32, (part, part), 1)

    def piece(h, q_rows, k_rows, masked):
        q = qx[h, q_rows, :]
        do = dox[h, q_rows, :]
        keys = kx[k_rows, :]
        weights = jnp.exp(dot_last(keys, q))
        if masked:
            weights = jnp.where(causal, weights, 0.0)
        dscore = (weights * dot_last(vx[k_rows, :], do)).astype(BF16)
        dv[...] += jnp.dot(weights.astype(BF16), do, preferred_element_type=F32)
        dk[...] += jnp.dot(dscore, q, preferred_element_type=F32)
        dq[h, q_rows, :] += lax.dot_general(dscore, keys, (((0,), (0,)), ((), ())), preferred_element_type=F32)

    def line_copy(owner, source):
        return pltpu.make_async_remote_copy(
            src_ref=dkv.at[owner], dst_ref=dkv.at[source], send_sem=line_send.at[owner],
            recv_sem=line_recv.at[source], device_id=team.other_team(owner), device_id_type=MESH,
        )

    def fetch_keys(source):
        slot = lax.rem(source, 2)
        return pltpu.make_async_copy(kv_all.at[source], kv_in.at[slot], local.at[8 + slot])

    fetch_keys(t * 0).start()

    def attention_unit(source, k, h):
        @pl.when((k == 0) & (h == 0))
        def _():
            fetch_keys(source).wait()

            @pl.when(source < t)
            def _():
                fetch_keys(source + 1).start()

            widen_keys(kv_in[lax.rem(source, 2)], spans, source * rows, kx, vx)

        @pl.when(h == 0)
        def _():
            dk[...] = jnp.zeros_like(dk)
            dv[...] = jnp.zeros_like(dv)

        k_rows = pl.ds(pl.multiple_of(k * part, part), part)

        @pl.when(source < t)
        def _():
            for q in range(2):
                piece(h, slice(q * part, (q + 1) * part), k_rows, False)

        @pl.when(source == t)
        def _():
            for diagonal in range(2):

                @pl.when(k == diagonal)
                def _():
                    for q in range(diagonal, 2):
                        piece(h, slice(q * part, (q + 1) * part), slice(diagonal * part, (diagonal + 1) * part),
                              q == diagonal)

        @pl.when(h == GROUP - 1)
        def _():
            dkv[source, k_rows, :] = jnp.where(
                lane_ids(part) < HEAD_SIZE, dk[...], pltpu.roll(dv[...], HEAD_SIZE, 1)
            ).astype(BF16)

            @pl.when((k == 1) & (source < t))
            def _():
                line_copy(source, t).start()

    def keys_phase():
        fetch.start()
        dkv_sum[...] = wide(dkv[t])
        for d in range(1, T):

            @pl.when(t + d < T)
            def _():
                line_copy(t, t + d).wait_recv()
                dkv_sum[...] += wide(dkv[t + d])

        small[2:4, :] = jnp.zeros((2, width), F32)

    def turn_unit(r):
        here = pl.ds(pl.multiple_of(r * block, block), block)
        cos, sin = cosine[here, 0:HEAD_SIZE], sine[here, 0:HEAD_SIZE]
        q_term = jnp.zeros((1, HEAD_SIZE), F32)
        for h in range(GROUP + 1):
            if h < GROUP:
                u, gain = dq[h, here, 0:HEAD_SIZE] * HEAD_SIZE ** (-0.5), gain_q
            else:
                u, gain = dkv_sum[here, 0:HEAD_SIZE], gain_k
            u = u * cos - jnp.concatenate([u[:, HEAD_SIZE // 2 :], u[:, : HEAD_SIZE // 2]], 1) * sin
            unit, factor = unit_and_factor(heads[h // 2, here, h % 2 * HEAD_SIZE : (h % 2 + 1) * HEAD_SIZE])
            term = jnp.sum(u * unit, 0, keepdims=True)
            if h < GROUP:
                q_term = q_term + term
            else:
                small[3:4, 0:HEAD_SIZE] += term
            turned[here, h * HEAD_SIZE : (h + 1) * HEAD_SIZE] = norm_back(u, unit, factor, gain).astype(BF16)
        small[2:3, 0:HEAD_SIZE] += q_term
        h = GROUP + 1
        turned[here, h * HEAD_SIZE : (h + 1) * HEAD_SIZE] = dkv_sum[here, HEAD_SIZE : 2 * HEAD_SIZE].astype(BF16)

    def normed_unit(i):
        for m in range(4):
            here = pl.ds(pl.multiple_of((4 * i + m) * own_rows, own_rows), own_rows)
            xs[i, m // 2, m % 2] = dot_last(turned[here, :], wq_in[...]).astype(BF16)

    def products_phase():
        again.begin()
        fetch.wait()

    def products_unit(i):
        for j in range(2):
            r = pl.multiple_of((2 * i + j) * (width // 6), LANES)
            here = pl.ds(r, width // 6)
            own_last[here, own_last.shape[1] - turned.shape[1] :] = lax.dot_general(
                big[:, here], turned[...], (((0,), (0,)), ((), ())), preferred_element_type=F32
            ).astype(BF16)

    def tokens_phase():
        def store(columns, total):
            tokens_grad[:, columns] = total

        again.end(store)
        term = jnp.zeros((1, width), F32)
        for r in range(0, own_rows, 32):
            here = slice(r, r + 32)
            unit, factor = unit_and_factor(wide(tokens[here, :]))
            upstream = tokens_grad[here, :]
            term = term + jnp.sum(upstream * unit, 0, keepdims=True)
            tokens_grad[here, :] = grad_resid[here, :] + norm_back(upstream, unit, factor, gain_attn)
        small[0:1, :] = term
        lanes = own_gains.shape[1]
        row = lax.broadcasted_iota(jnp.int32, (16, lanes), 0)

        def cut(i, first, count):
            value = small[i : i + 1, first : first + count]
            if count < lanes:
                value = jnp.concatenate([value, jnp.zeros((1, lanes - count), F32)], 1)
            return jnp.where(row == i, jnp.broadcast_to(value, (16, lanes)), 0.0)

        for i in range(F):
            few = HEAD_SIZE // F
            own_gains[16 * i : 16 * i + 16, :] = (
                cut(0, i * depth, depth) + cut(1, i * depth, depth) + cut(2, i * few, few) + cut(3, i * few, few)
            ).astype(BF16)

    def late_loads():
        for load in loads[2:]:
            load.wait()

    @pl.loop(0, steps)
    def _(s):
        pl.when(s == at["scatter1"])(late_loads)
        sums.step(s)
        for name, body in (
            ("scatter1", scatter.relay), ("scatter2", scatter.relay_again), ("resid", resid_phase),
            ("relay", gather.relay), ("heads", heads_phase), ("own_wo", own_wo_phase), ("keys", keys_phase),
            ("products", products_phase), ("again1", again.relay), ("again2", again.relay_again),
            ("tokens", tokens_phase),
        ):
            pl.when(s == at[name])(body)
        for name, count, body in (
            ("heads", 4, heads_unit), ("turn", 4, turn_unit), ("normed", 2, normed_unit),
            ("products", 3, products_unit),
        ):
            i = s - at[name]
            pl.when((i >= 0) & (i < count))(functools.partial(body, i))
        unit = s - at["attention"]
        source = lax.div(unit, 2 * GROUP)

        @pl.when((unit >= 0) & (source <= t))
        def _():
            attention_unit(source, lax.rem(lax.div(unit, GROUP), 2), lax.rem(unit, GROUP))

    for d in range(1, T):

        @pl.when(t - d >= 0)
        def _():
            line_copy(t - d, t).wait_send()

    sums.end()


def backward(dims, grad_hidden, g_down, g_wide, g_last, resid, tokens, cotangent, gains, acc, qx, kv_all, spans,
             heads, cosine, sine, wo, wqkv, normed):
    B, F, T = dims
    own_rows, width = resid.shape
    rows = qx.shape[1]
    part = rows // 2
    hidden = g_down.shape[0]
    n = B * F
    kinds = grad_kinds(dims, width, hidden)
    steps = max(
        GradSum.steps([(rows_, step, first) for rows_, _, step, first, _ in kinds], T), first_steps(dims)["tokens"] + 1
    )
    positions = max(first + rows_ // step for rows_, _, step, first, _ in kinds)
    outs = []
    for rows_, wide_, step, first, how in kinds:
        if how == "rows":
            shape = (n, rows_ // F, wide_)
        elif how == "stay":
            shape = (B, rows_, wide_)
        else:
            shape = (n, 16, wide_)
        outs.append(jax.ShapeDtypeStruct(shape, BF16))
    outs.append(jax.ShapeDtypeStruct((own_rows, width), F32))
    eight = (2, 2, 2, own_rows, width)
    hands = [pltpu.SemaphoreType.DMA((F, kinds[k][0] // F // kinds[k][2])) for k in (1, 3)]
    copies = 2 * Scatter.COPIES + Gather.COPIES
    return pl.pallas_call(
        functools.partial(back_kernel, dims, kinds, steps),
        out_shape=outs,
        in_specs=[ANY] * 4 + [VMEM] * 6 + [ANY] + [VMEM] * 4 + [ANY] * 3,
        out_specs=[ANY] * 5 + [VMEM],
        scratch_shapes=[pltpu.VMEM(eight, BF16)]
        + [pltpu.VMEM((kind[0], kind[1]), BF16) for kind in kinds] * 2
        + [pltpu.VMEM(((kind[0] // kind[2] + 1) // 2 * kind[2], kind[1]), BF16) for kind in kinds]
        + [
            pltpu.VMEM((own_rows, width), F32),
            pltpu.VMEM((own_rows, width), BF16),
            pltpu.VMEM((rows, width), BF16),
            pltpu.VMEM(qx.shape, BF16),
            pltpu.VMEM((rows, QW), BF16),
            pltpu.VMEM(qx.shape, F32),
            pltpu.VMEM(kv_all.shape, BF16),
            pltpu.VMEM((2,) + kv_all.shape[1:], BF16),
            pltpu.VMEM((rows, LANES), F32),
            pltpu.VMEM((rows, QW + 2 * HEAD_SIZE), BF16),
            pltpu.VMEM((8, width), F32),
            pltpu.VMEM((rows, LANES), BF16),
            pltpu.VMEM((rows, LANES), BF16),
            pltpu.VMEM((part, LANES), F32),
            pltpu.VMEM((part, LANES), F32),
            pltpu.VMEM(wqkv.shape, BF16),
            pltpu.VMEM((QW, width), BF16),
        ]
        + scatter_shapes(own_rows, width, ORDER)
        + [
            pltpu.SemaphoreType.DMA((copies,)),
            pltpu.SemaphoreType.DMA((copies,)),
            pltpu.SemaphoreType.DMA((T,)),
            pltpu.SemaphoreType.DMA((T,)),
            pltpu.SemaphoreType.DMA((2, positions)),
            pltpu.SemaphoreType.DMA((positions,)),
            *hands,
            pltpu.SemaphoreType.DMA((7, len(kinds), 2)),
            pltpu.SemaphoreType.DMA((11,)),
        ],
        compiler_params=pltpu.CompilerParams(
            collective_id=3, has_side_effects=True, vmem_limit_bytes=60 * 1024 * 1024
        ),
        name="backward",
    )(grad_hidden.reshape(eight), g_down, g_wide, g_last, resid, tokens, cotangent, gains, acc, qx,
      kv_all, spans, heads, cosine, sine, wo, wqkv, normed)


def place_kernel(n, hidden, both, last, down, wo, layer, tokens, gains, gate_out, up_out, wq_out, wk_out, wv_out, down_out,
                 wo_out, layer_out, tokens_out, *gain_outs):
    early = both.shape[-1]
    tail = 2 * hidden - early
    for q in range(n):
        block, rest = wide(both[q]), wide(last[q])
        gate_out[:, q * hidden : (q + 1) * hidden] = block[:, :hidden]
        up_out[:, q * hidden : (q + 1) * hidden] = jnp.concatenate([block[:, hidden:], rest[:, :tail]], 1)
        wq_out[:, q * QW : (q + 1) * QW] = rest[:, tail : tail + QW]
        wk_out[:, q * HEAD_SIZE : (q + 1) * HEAD_SIZE] = rest[:, tail + QW : tail + QW + HEAD_SIZE]
        wv_out[:, q * HEAD_SIZE : (q + 1) * HEAD_SIZE] = rest[:, tail + QW + HEAD_SIZE :]
    down_out[...] = wide(down[...])
    wo_out[...] = wide(wo[...])

    @pl.when(pl.program_id(0) == 0)
    def _():
        layer_out[...] = layer[...].astype(BF16)
        tokens_out[...] = tokens[...].astype(BF16)
        total = wide(gains[0])
        for i in range(1, n):
            total = total + wide(gains[i])
        for i, gain_out in enumerate(gain_outs):
            gain_out[...] = total[i, : gain_out.shape[0]]


def place(hidden, both, last, down, wo, layer, tokens, gains):
    n, depth, early = both.shape
    width = down.shape[-1]
    down, wo = down.reshape(-1, width), wo.reshape(-1, width)
    step = 64
    count = depth // step
    many = lambda a: pl.BlockSpec((n, step, a.shape[-1]), lambda i: (0, i, 0))
    cut = lambda a: pl.BlockSpec((a.shape[0] // count, width), lambda i: (i, 0))
    out = lambda w: pl.BlockSpec((step, w), lambda i: (i, 0))
    whole = lambda dims: pl.BlockSpec(dims, lambda i: (0,) * len(dims))
    shape = lambda r, w: jax.ShapeDtypeStruct((r, w), F32)
    wq, wk = QW * n, HEAD_SIZE * n
    sizes = [depth, depth, HEAD_SIZE * depth // width, HEAD_SIZE * depth // width]
    return pl.pallas_call(
        functools.partial(place_kernel, n, hidden),
        grid=(count,),
        out_shape=(
            shape(depth, n * hidden), shape(depth, n * hidden), shape(depth, wq), shape(depth, wk), shape(depth, wk),
            shape(down.shape[0], width), shape(wo.shape[0], width), jax.ShapeDtypeStruct(layer.shape, BF16),
            jax.ShapeDtypeStruct(tokens.shape, BF16), *[jax.ShapeDtypeStruct((size,), F32) for size in sizes],
        ),
        in_specs=[many(both), many(last), cut(down), cut(wo), whole(layer.shape), whole(tokens.shape),
                  whole(gains.shape)],
        out_specs=[out(n * hidden), out(n * hidden), out(wq), out(wk), out(wk), cut(down), cut(wo),
                   whole(layer.shape), whole(tokens.shape), *[whole((size,)) for size in sizes]],
        compiler_params=pltpu.CompilerParams(vmem_limit_bytes=VMEM_LIMIT),
        name="place",
    )(both, last, down, wo, layer, tokens, gains)


def norm_back(upstream, unit_rows, factor, gain_row):
    lifted = upstream * gain_row
    return factor * (lifted - unit_rows * jnp.mean(lifted * unit_rows, -1, keepdims=True))


def on_device(
    tokens, lengths, wq, wk, wv, wo, w_gate, w_up, w_down, attn_gain, ffn_gain, q_gain, key_norm_gain, cotangent
):
    F = lax.axis_size("fsdp")
    B = KEY_VALUE_HEADS // F
    T = lax.axis_size("ctx") // B
    dims = (B, F, T)
    own_rows, width = tokens.shape
    rows = own_rows * KEY_VALUE_HEADS
    depth = width // F
    t = lax.axis_index("ctx") // B
    hidden = w_down.shape[0] // B

    lanes = max(depth, LANES)
    line = lambda a: jnp.pad(a, (0, lanes - a.shape[0]))
    gains = jnp.concatenate([line(attn_gain), line(ffn_gain), line(q_gain), line(key_norm_gain)])
    gains = jnp.pad(gains.reshape(4, lanes), ((0, 12), (0, 0)))
    half = HEAD_SIZE // 2
    freq = np.power(np.float32(ROPE_BASE), -(np.arange(LANES, dtype=np.float32) % half * np.float32(2.0) / HEAD_SIZE))
    freq = jnp.asarray(np.broadcast_to(freq, (8, LANES))[:1], F32)
    (cosine, sine, spans, tok_full, wqkv, normed, heads, qx, kv_all, acc, mixed, wo_full, wide_w, all_gains) = front(
        dims, tokens, wq, wk, wv, wo, w_gate, w_up, gains, freq, lengths
    )
    grad_hidden, g_down, g_wide, g_last, own_resid, layer_out = feed(
        dims, tok_full, mixed, wo_full.reshape(-1, width), wide_w.reshape(width, 2 * hidden), w_down,
        cotangent, all_gains,
    )
    out_down, out_wide, out_wo, out_last, out_gains, tokens_grad = backward(
        dims, grad_hidden, g_down, g_wide, g_last, own_resid, tokens, cotangent, all_gains, acc, qx, kv_all,
        spans, heads, cosine, sine, wo, wqkv, normed,
    )
    (gate_grad, up_grad, wq_grad, wk_grad, wv_grad, down_grad, wo_grad, layer_out, tokens_grad, *gain_grads) = place(
        hidden, out_wide, out_last, out_down, out_wo, layer_out, tokens_grad, out_gains
    )
    return (
        layer_out, tokens_grad, wq_grad, wk_grad, wv_grad, wo_grad, gate_grad, up_grad,
        down_grad, *gain_grads,
    )


def solution(mesh):
    rows = P(("ctx", "fsdp"), None)
    shard = P("fsdp", None)
    gain = P("fsdp")
    return jax.shard_map(
        on_device,
        mesh=mesh,
        in_specs=(rows, P(), shard, shard, shard, shard, shard, shard, shard, gain, gain, gain, gain, rows),
        out_specs=(rows, rows, shard, shard, shard, shard, shard, shard, shard, gain, gain, gain, gain),
        check_vma=False,
    )
```

time: 548 us -> 467 us (0.85); the launches traced: 540 us -> 465 us
  Pallas kernels: 523 us -> 463 us
  other arithmetic: 10.2 us -> 0.74 us
  local copies, waits for them, and re-layouts: 6.13 us -> 0.62 us
    pallas_call x1, Pallas kernels: 345 us -> 292 us  [backward(): pl.pallas_call(functools.partial(back_kernel, dims, kinds, steps), out_sh...]
    pallas_call x2, Pallas kernels: 130 us -> 114 us  [the longest x1 91.9 us: front(): pl.pallas_call(functools.partial(front_kernel, dims), out_shape=(wide_sha...]
    pallas_call x1, Pallas kernels: 47.8 us -> 57.4 us  [feed(): pl.pallas_call(functools.partial(feed_kernel, dims), out_shape=(shape((ro...]
where the time goes in v4:
time: 467 us; the launch traced here: 465 us
  Pallas kernels  463 us (99%)
    pallas_call x1, Pallas kernels, backward(): pl.pallas_call(functools.partial(back_kernel, dims, kinds, steps), out_sh...  292 us
    pallas_call x1, Pallas kernels, front(): pl.pallas_call(functools.partial(front_kernel, dims), out_shape=(wide_sha...  91.9 us
    pallas_call x1, Pallas kernels, feed(): pl.pallas_call(functools.partial(feed_kernel, dims), out_shape=(shape((ro...  57.4 us
    pallas_call x1, Pallas kernels, place(): pl.pallas_call(functools.partial(place_kernel, n, hidden), grid=(count,),...  22 us

profile of v4, /device:TPU:0, one launch (start us, length us, event | category | flops | bytes accessed | tf_op | source)
XLA Modules:
  0.0 465.2 jit_solution(7804342398305813427)
XLA Ops:
  0.6 0.7 fusion.4
  1.4 0.6 pad.13.gains
  2.0 91.9 %front.1 = (f32[1024,128]{1,0:T(8,128)}, f32[1024,128]{1,0:T(8,128)}, s32[8,128]{1,0:T(8,128)}, bf16[1024,1536]{1,0:T(8,128)(2,1)}, bf16[1536,320]{1,0:T(8,128)(...) custom-call(bf16[128,1536]{1,0:T(8,128)(2,1)} %tokens.3, ...), custom_call_target="tpu_custom_call" | custom-call | tf_op jit(solution)/shard_map/front/pallas_call | solution.py:579
  94.0 57.4 %feed.1 = (bf16[1024,1536]{1,0:T(8,128)(2,1)}, bf16[864,1536]{1,0:T(8,128)(2,1)}, bf16[1536,1664]{1,0:T(8,128)(2,1)}, bf16[1536,384]{1,0:T(8,128)(2,1)}, f32[128,1536]{1,0:T(8,128)}, /*index=5*/f32[128,1536]{1,0:T(8,128)}) custom-call(bf16[1024,1536]{1,0:T(8,128)(2,1)} %get-tuple-element.52.tok_in, bf16[2,8,768,128]{3,2,1,0:T(8,128)(2,1)} %get-tuple-element.53.mixed_in, ...), custom_call_target="tpu_custom_call" | custom-call | tf_op jit(solution)/shard_map/feed/pallas_call | solution.py:735
  151.4 291.6 %backward.1 = (bf16[2,864,1536]{2,1,0:T(8,128)(2,1)}, bf16[8,384,1664]{2,1,0:T(8,128)(2,1)}, bf16[2,192,1536]{2,1,0:T(8,128)(2,1)}, bf16[8,384,384]{2,1,0:T(8,12...) custom-call(bf16[2,2,2,128,1536]{4,3,2,1,0:T(8,128)(2,1)} %bitcast.8, ...), custom_call_target="tpu_custom_call" | custom-call | tf_op jit(solution)/shard_map/backward/pallas_call | solution.py:1356
  443.0 22.0 %place.1 = (f32[384,6912]{1,0:T(8,128)}, f32[384,6912]{1,0:T(8,128)}, f32[384,1536]{1,0:T(8,128)}, f32[384,512]{1,0:T(8,128)}, f32[384,512]{1,0:T(8,128)}, /*ind...) custom-call(bf16[8,384,1664]{2,1,0:T(8,128)(2,1)} %get-tuple-element, ...), custom_call_target="tpu_custom_call" | custom-call | tf_op jit(solution)/shard_map/place/pallas_call | solution.py:1441
  (1 shorter events, 0.0 us)

commit v5 on v4

--- a/solution.py
+++ b/solution.py
@@ -648,7 +648,6 @@
             last = mixed[which, i, 2 * block : 3 * block, :]
             last = jnp.where(later == 0, wide(last[:, :HEAD_SIZE]), wide(last[:, HEAD_SIZE:]))
             rows_in[:, first + 2 * HEAD_SIZE : first + QW] = last.astype(BF16)
-        pl.when(r == 2)(gather.relay)
         resid[...] = wide(tok[here, :]) + jnp.dot(rows_in[...], wo[...], preferred_element_type=F32)
 
         @pl.when(r == lax.div(p * own_rows, block))
@@ -660,6 +659,7 @@
 
     for load in loads[3:]:
         load.wait()
+    gather.relay()
 
     @pl.loop(0, rows // block)
     def _(r):
@@ -697,13 +697,13 @@
         stores[-1].start()
 
     store(tok, grad_hidden)
-    scatter.relay_again()
     over_rows = lambda a, b: lax.dot_general(a, b, (((0,), (0,)), ((), ())), preferred_element_type=F32).astype(BF16)
 
     for first in range(0, hidden, 256):
         count = min(256, hidden - first)
         gd[first : first + count, :] = over_rows(act[:, first : first + count], dy[...])
     store(gd, g_down)
+    scatter.relay_again()
 
     @pl.loop(0, width // 256)
     def _(r):
@@ -773,6 +773,7 @@
 
 HOP = 2
 LAG = 3
+UNITS = 8
 ORDER = "both"
 
 
@@ -998,15 +999,15 @@
 
 
 def first_steps(dims):
-    at = dict(scatter1=3, scatter2=12, resid=18, relay=24, heads=31, own_wo=35)
+    at = dict(scatter1=3, scatter2=12, resid=18, relay=24, heads=30, own_wo=30 + UNITS)
     at["attention"] = at["own_wo"] + 1
-    at["keys"] = at["attention"] + 2 * GROUP * dims[2] + 2
+    at["keys"] = at["attention"] + 2 * GROUP * dims[2] + 1
     at["turn"] = at["keys"] + 1
-    at["normed"] = at["turn"] + 4
+    at["normed"] = at["turn"] + UNITS
     at["products"] = at["normed"] + 2
     at["again1"] = at["products"] + 3
     at["again2"] = at["again1"] + 6
-    at["tokens"] = at["again2"] + 7
+    at["tokens"] = at["again2"] + 6
     return at
 
 
@@ -1022,7 +1023,7 @@
         (hidden, depth, 32, 0, "stay"),
         (depth, early, 32, 0, "rows"),
         (QW, depth, 48, at["own_wo"] + 1, "stay"),
-        (depth, 2 * hidden - early + QW + 2 * HEAD_SIZE, 96, at["products"] + 3, "rows"),
+        (depth, 2 * hidden - early + QW + 2 * HEAD_SIZE, 192, at["products"] + 3, "rows"),
         (16 * dims[1], max(depth // dims[1], LANES), 16 * dims[1], at["tokens"] + 1, "gain"),
     ):
         place = max(place, ready)
@@ -1031,13 +1032,14 @@
     return kinds
 
 
-def back_kernel(dims, kinds, steps, grad_hidden, g_down, g_wide, g_last, resid, tokens, cotangent, gains, acc, qx, kv_all, spans,
-                heads, cosine, sine, wo, wqkv, normed,
+def back_kernel(dims, kinds, steps, grad_hidden, g_down, g_wide, g_last, resid, tokens, cotangent, gains, acc_in, qx_in,
+                kv_all, spans, heads_in, cosine_in, sine_in, wo, wqkv, normed,
                 out_down, out_wide, out_wo, out_last, out_gains, tokens_grad,
                 xs, own_down, own_wide, own_gwo, own_last, own_gains,
                 land_down, land_wide, land_wo, land_last, land_gains,
                 also_down, also_wide, also_wo, also_last, also_gains,
-                grad_resid, attn_own, big, dox, mixed, dq, dkv, kv_in, dkv_sum, turned, small, kx, vx, dk, dv, wq_in, own_wo, *rest):
+                grad_resid, attn_own, big, dox, mixed, dq, dkv, kv_in, dkv_sum, turned, small, kx, vx, dk, dv, wq_in, own_wo,
+                acc, qx, heads, cosine, sine, *rest):
     count = len(scatter_parts(resid.shape[-1], ORDER)) * 4 + 1
     scratch1, rest = rest[:count], rest[count:]
     send, recv, line_send, line_recv, red_recv, fin_recv, hand_wide, hand_last, bulk, local = rest
@@ -1048,14 +1050,15 @@
     own_rows, width = resid.shape
     rows = qx.shape[1]
     part = rows // 2
-    block = rows // 4
+    small_block = rows // UNITS
     depth = width // F
     sems = Sems(send, recv)
     loads = [
         pltpu.make_async_copy(src, dst, local.at[i])
         for i, (src, dst) in enumerate(
             [(grad_hidden, xs), (g_down, own_down), (g_wide, own_wide), (g_last, own_last), (wqkv, wq_in),
-             (wo.at[pl.ds(pl.multiple_of(team.y * QW, 16), QW)], own_wo)]
+             (wo.at[pl.ds(pl.multiple_of(team.y * QW, 16), QW)], own_wo), (acc_in, acc), (qx_in, qx),
+             (heads_in, heads), (cosine_in, cosine), (sine_in, sine)]
         )
     ]
     for load in loads:
@@ -1089,8 +1092,8 @@
     loads[1].wait()
     gain_attn, gain_ffn = gains[0:1, :], gains[1:2, :]
     gain_q, gain_k = gains[2:3, 0:HEAD_SIZE], gains[3:4, 0:HEAD_SIZE]
-    home = pltpu.make_async_copy(attn_own, big.at[pl.ds(pl.multiple_of(p * own_rows, 16), own_rows)], local.at[6])
-    fetch = pltpu.make_async_copy(normed, big, local.at[7])
+    home = pltpu.make_async_copy(attn_own, big.at[pl.ds(pl.multiple_of(p * own_rows, 16), own_rows)], local.at[11])
+    fetch = pltpu.make_async_copy(normed, big, local.at[12])
 
     def resid_phase():
         def store(columns, total):
@@ -1115,8 +1118,8 @@
         home.wait()
 
     def heads_unit(r):
-        lane = lane_ids(block)
-        here = pl.ds(pl.multiple_of(r * block, block), block)
+        lane = lane_ids(small_block)
+        here = pl.ds(pl.multiple_of(r * small_block, small_block), small_block)
         grad = dot_last(big[here, :], own_wo[...]).astype(BF16)
         for h in range(GROUP):
             sums_h = acc[h, here, :]
@@ -1165,7 +1168,7 @@
 
     def fetch_keys(source):
         slot = lax.rem(source, 2)
-        return pltpu.make_async_copy(kv_all.at[source], kv_in.at[slot], local.at[8 + slot])
+        return pltpu.make_async_copy(kv_all.at[source], kv_in.at[slot], local.at[13 + slot])
 
     fetch_keys(t * 0).start()
 
@@ -1225,7 +1228,7 @@
         small[2:4, :] = jnp.zeros((2, width), F32)
 
     def turn_unit(r):
-        here = pl.ds(pl.multiple_of(r * block, block), block)
+        here = pl.ds(pl.multiple_of(r * small_block, small_block), small_block)
         cos, sin = cosine[here, 0:HEAD_SIZE], sine[here, 0:HEAD_SIZE]
         q_term = jnp.zeros((1, HEAD_SIZE), F32)
         for h in range(GROUP + 1):
@@ -1306,7 +1309,7 @@
         ):
             pl.when(s == at[name])(body)
         for name, count, body in (
-            ("heads", 4, heads_unit), ("turn", 4, turn_unit), ("normed", 2, normed_unit),
+            ("heads", UNITS, heads_unit), ("turn", UNITS, turn_unit), ("normed", 2, normed_unit),
             ("products", 3, products_unit),
         ):
             i = s - at[name]
@@ -1356,7 +1359,7 @@
     return pl.pallas_call(
         functools.partial(back_kernel, dims, kinds, steps),
         out_shape=outs,
-        in_specs=[ANY] * 4 + [VMEM] * 6 + [ANY] + [VMEM] * 4 + [ANY] * 3,
+        in_specs=[ANY] * 4 + [VMEM] * 4 + [ANY] * 3 + [VMEM] + [ANY] * 6,
         out_specs=[ANY] * 5 + [VMEM],
         scratch_shapes=[pltpu.VMEM(eight, BF16)]
         + [pltpu.VMEM((kind[0], kind[1]), BF16) for kind in kinds] * 2
@@ -1379,6 +1382,11 @@
             pltpu.VMEM((part, LANES), F32),
             pltpu.VMEM(wqkv.shape, BF16),
             pltpu.VMEM((QW, width), BF16),
+            pltpu.VMEM(acc.shape, F32),
+            pltpu.VMEM(qx.shape, BF16),
+            pltpu.VMEM(heads.shape, F32),
+            pltpu.VMEM(cosine.shape, F32),
+            pltpu.VMEM(sine.shape, F32),
         ]
         + scatter_shapes(own_rows, width, ORDER)
         + [
@@ -1390,7 +1398,7 @@
             pltpu.SemaphoreType.DMA((positions,)),
             *hands,
             pltpu.SemaphoreType.DMA((7, len(kinds), 2)),
-            pltpu.SemaphoreType.DMA((11,)),
+            pltpu.SemaphoreType.DMA((15,)),
         ],
         compiler_params=pltpu.CompilerParams(
             collective_id=3, has_side_effects=True, vmem_limit_bytes=60 * 1024 * 1024

time: 467 us -> 462 us (0.989)
    pallas_call x1, Pallas kernels: 57.4 us -> 51.6 us  [feed(): pl.pallas_call(functools.partial(feed_kernel, dims), out_shape=(shape((ro...]
where the time goes in v5:
time: 462 us
  Pallas kernels  459 us (99%)
    pallas_call x1, Pallas kernels, backward(): pl.pallas_call(functools.partial(back_kernel, dims, kinds, steps), out_sh...  294 us
    pallas_call x1, Pallas kernels, front(): pl.pallas_call(functools.partial(front_kernel, dims), out_shape=(wide_sha...  91.9 us
    pallas_call x1, Pallas kernels, feed(): pl.pallas_call(functools.partial(feed_kernel, dims), out_shape=(shape((ro...  51.6 us
    pallas_call x1, Pallas kernels, place(): pl.pallas_call(functools.partial(place_kernel, n, hidden), grid=(count,),...  22 us

profile of v5, /device:TPU:0, one launch (start us, length us, event | category | flops | bytes accessed | tf_op | source)
XLA Modules:
  0.0 461.5 jit_solution(15429505841113425502)
XLA Ops:
  0.6 0.7 fusion.4
  1.4 0.6 pad.13.gains
  2.0 91.9 %front.1 = (f32[1024,128]{1,0:T(8,128)}, f32[1024,128]{1,0:T(8,128)}, s32[8,128]{1,0:T(8,128)}, bf16[1024,1536]{1,0:T(8,128)(2,1)}, bf16[1536,320]{1,0:T(8,128)(...) custom-call(bf16[128,1536]{1,0:T(8,128)(2,1)} %tokens.3, ...), custom_call_target="tpu_custom_call" | custom-call | tf_op jit(solution)/shard_map/front/pallas_call | solution.py:579
  94.0 51.6 %feed.1 = (bf16[1024,1536]{1,0:T(8,128)(2,1)}, bf16[864,1536]{1,0:T(8,128)(2,1)}, bf16[1536,1664]{1,0:T(8,128)(2,1)}, bf16[1536,384]{1,0:T(8,128)(2,1)}, f32[128,1536]{1,0:T(8,128)}, /*index=5*/f32[128,1536]{1,0:T(8,128)}) custom-call(bf16[1024,1536]{1,0:T(8,128)(2,1)} %get-tuple-element.52.tok_in, bf16[2,8,768,128]{3,2,1,0:T(8,128)(2,1)} %get-tuple-element.53.mixed_in, ...), custom_call_target="tpu_custom_call" | custom-call | tf_op jit(solution)/shard_map/feed/pallas_call | solution.py:735
  145.6 293.8 %backward.1 = (bf16[2,864,1536]{2,1,0:T(8,128)(2,1)}, bf16[8,384,1664]{2,1,0:T(8,128)(2,1)}, bf16[2,192,1536]{2,1,0:T(8,128)(2,1)}, bf16[8,384,384]{2,1,0:T(8,12...) custom-call(bf16[2,2,2,128,1536]{4,3,2,1,0:T(8,128)(2,1)} %bitcast.8, ...), custom_call_target="tpu_custom_call" | custom-call | tf_op jit(solution)/shard_map/backward/pallas_call | solution.py:1359
  439.3 22.0 %place.1 = (f32[384,6912]{1,0:T(8,128)}, f32[384,6912]{1,0:T(8,128)}, f32[384,1536]{1,0:T(8,128)}, f32[384,512]{1,0:T(8,128)}, f32[384,512]{1,0:T(8,128)}, /*ind...) custom-call(bf16[8,384,1664]{2,1,0:T(8,128)(2,1)} %get-tuple-element, ...), custom_call_target="tpu_custom_call" | custom-call | tf_op jit(solution)/shard_map/place/pallas_call | solution.py:1449
  (1 shorter events, 0.0 us)

commit v6 on v5

--- a/solution.py
+++ b/solution.py
@@ -773,7 +773,7 @@
 
 HOP = 2
 LAG = 3
-UNITS = 8
+UNITS = 4
 ORDER = "both"
 
 

time: 462 us -> 462 us (level)
  no operation moved by 1% of the time
where the time goes in v6:
time: 462 us
  Pallas kernels  459 us (99%)
    pallas_call x1, Pallas kernels, backward(): pl.pallas_call(functools.partial(back_kernel, dims, kinds, steps), out_sh...  294 us
    pallas_call x1, Pallas kernels, front(): pl.pallas_call(functools.partial(front_kernel, dims), out_shape=(wide_sha...  91.9 us
    pallas_call x1, Pallas kernels, feed(): pl.pallas_call(functools.partial(feed_kernel, dims), out_shape=(shape((ro...  51.6 us
    pallas_call x1, Pallas kernels, place(): pl.pallas_call(functools.partial(place_kernel, n, hidden), grid=(count,),...  22 us

profile of v6, /device:TPU:0, one launch (start us, length us, event | category | flops | bytes accessed | tf_op | source)
XLA Modules:
  0.0 461.6 jit_solution(6977497599210737904)
XLA Ops:
  0.6 0.7 fusion.4
  1.4 0.6 pad.13.gains
  2.0 91.9 %front.1 = (f32[1024,128]{1,0:T(8,128)}, f32[1024,128]{1,0:T(8,128)}, s32[8,128]{1,0:T(8,128)}, bf16[1024,1536]{1,0:T(8,128)(2,1)}, bf16[1536,320]{1,0:T(8,128)(...) custom-call(bf16[128,1536]{1,0:T(8,128)(2,1)} %tokens.3, ...), custom_call_target="tpu_custom_call" | custom-call | tf_op jit(solution)/shard_map/front/pallas_call | solution.py:579
  94.0 51.6 %feed.1 = (bf16[1024,1536]{1,0:T(8,128)(2,1)}, bf16[864,1536]{1,0:T(8,128)(2,1)}, bf16[1536,1664]{1,0:T(8,128)(2,1)}, bf16[1536,384]{1,0:T(8,128)(2,1)}, f32[128,1536]{1,0:T(8,128)}, /*index=5*/f32[128,1536]{1,0:T(8,128)}) custom-call(bf16[1024,1536]{1,0:T(8,128)(2,1)} %get-tuple-element.52.tok_in, bf16[2,8,768,128]{3,2,1,0:T(8,128)(2,1)} %get-tuple-element.53.mixed_in, ...), custom_call_target="tpu_custom_call" | custom-call | tf_op jit(solution)/shard_map/feed/pallas_call | solution.py:735
  145.6 293.9 %backward.1 = (bf16[2,864,1536]{2,1,0:T(8,128)(2,1)}, bf16[8,384,1664]{2,1,0:T(8,128)(2,1)}, bf16[2,192,1536]{2,1,0:T(8,128)(2,1)}, bf16[8,384,384]{2,1,0:T(8,12...) custom-call(bf16[2,2,2,128,1536]{4,3,2,1,0:T(8,128)(2,1)} %bitcast.8, ...), custom_call_target="tpu_custom_call" | custom-call | tf_op jit(solution)/shard_map/backward/pallas_call | solution.py:1359
  439.4 22.0 %place.1 = (f32[384,6912]{1,0:T(8,128)}, f32[384,6912]{1,0:T(8,128)}, f32[384,1536]{1,0:T(8,128)}, f32[384,512]{1,0:T(8,128)}, f32[384,512]{1,0:T(8,128)}, /*ind...) custom-call(bf16[8,384,1664]{2,1,0:T(8,128)(2,1)} %get-tuple-element, ...), custom_call_target="tpu_custom_call" | custom-call | tf_op jit(solution)/shard_map/place/pallas_call | solution.py:1449
  (1 shorter events, 0.0 us)

commit v7 on v6

--- a/solution.py
+++ b/solution.py
@@ -1056,16 +1056,19 @@
     loads = [
         pltpu.make_async_copy(src, dst, local.at[i])
         for i, (src, dst) in enumerate(
-            [(grad_hidden, xs), (g_down, own_down), (g_wide, own_wide), (g_last, own_last), (wqkv, wq_in),
+            [(g_down, own_down), (grad_hidden, xs), (g_wide, own_wide), (g_last, own_last), (wqkv, wq_in),
              (wo.at[pl.ds(pl.multiple_of(team.y * QW, 16), QW)], own_wo), (acc_in, acc), (qx_in, qx),
              (heads_in, heads), (cosine_in, cosine), (sine_in, sine)]
         )
     ]
-    for load in loads:
+    for load in loads[:2]:
         load.start()
     own_gains[...] = jnp.zeros_like(own_gains)
     greet(team_peers(team) + line_peers(team))
-    loads[0].wait()
+    for load in loads[:2]:
+        load.wait()
+    for load in loads[2:]:
+        load.start()
     scatter = Scatter(sems, team, xs, scratch1, ORDER)
     scatter.begin()
     again = Scatter(sems, team, xs, scratch1, ORDER)
@@ -1089,7 +1092,6 @@
         ],
         red_recv, fin_recv, [None, hand_wide, None, hand_last, None], bulk,
     )
-    loads[1].wait()
     gain_attn, gain_ffn = gains[0:1, :], gains[1:2, :]
     gain_q, gain_k = gains[2:3, 0:HEAD_SIZE], gains[3:4, 0:HEAD_SIZE]
     home = pltpu.make_async_copy(attn_own, big.at[pl.ds(pl.multiple_of(p * own_rows, 16), own_rows)], local.at[11])

time: 462 us -> 462 us (level)
  no operation moved by 1% of the time
where the time goes in v7:
time: 462 us
  Pallas kernels  459 us (99%)
    pallas_call x1, Pallas kernels, backward(): pl.pallas_call(functools.partial(back_kernel, dims, kinds, steps), out_sh...  294 us
    pallas_call x1, Pallas kernels, front(): pl.pallas_call(functools.partial(front_kernel, dims), out_shape=(wide_sha...  91.9 us
    pallas_call x1, Pallas kernels, feed(): pl.pallas_call(functools.partial(feed_kernel, dims), out_shape=(shape((ro...  51.6 us
    pallas_call x1, Pallas kernels, place(): pl.pallas_call(functools.partial(place_kernel, n, hidden), grid=(count,),...  22 us

profile of v7, /device:TPU:0, one launch (start us, length us, event | category | flops | bytes accessed | tf_op | source)
XLA Modules:
  0.0 461.6 jit_solution(17060623480923386506)
XLA Ops:
  0.6 0.7 fusion.4
  1.4 0.6 pad.13.gains
  2.0 91.9 %front.1 = (f32[1024,128]{1,0:T(8,128)}, f32[1024,128]{1,0:T(8,128)}, s32[8,128]{1,0:T(8,128)}, bf16[1024,1536]{1,0:T(8,128)(2,1)}, bf16[1536,320]{1,0:T(8,128)(...) custom-call(bf16[128,1536]{1,0:T(8,128)(2,1)} %tokens.3, ...), custom_call_target="tpu_custom_call" | custom-call | tf_op jit(solution)/shard_map/front/pallas_call | solution.py:579
  94.0 51.6 %feed.1 = (bf16[1024,1536]{1,0:T(8,128)(2,1)}, bf16[864,1536]{1,0:T(8,128)(2,1)}, bf16[1536,1664]{1,0:T(8,128)(2,1)}, bf16[1536,384]{1,0:T(8,128)(2,1)}, f32[128,1536]{1,0:T(8,128)}, /*index=5*/f32[128,1536]{1,0:T(8,128)}) custom-call(bf16[1024,1536]{1,0:T(8,128)(2,1)} %get-tuple-element.52.tok_in, bf16[2,8,768,128]{3,2,1,0:T(8,128)(2,1)} %get-tuple-element.53.mixed_in, ...), custom_call_target="tpu_custom_call" | custom-call | tf_op jit(solution)/shard_map/feed/pallas_call | solution.py:735
  145.6 293.8 %backward.1 = (bf16[2,864,1536]{2,1,0:T(8,128)(2,1)}, bf16[8,384,1664]{2,1,0:T(8,128)(2,1)}, bf16[2,192,1536]{2,1,0:T(8,128)(2,1)}, bf16[8,384,384]{2,1,0:T(8,12...) custom-call(bf16[2,2,2,128,1536]{4,3,2,1,0:T(8,128)(2,1)} %bitcast.8, ...), custom_call_target="tpu_custom_call" | custom-call | tf_op jit(solution)/shard_map/backward/pallas_call | solution.py:1361
  439.4 22.0 %place.1 = (f32[384,6912]{1,0:T(8,128)}, f32[384,6912]{1,0:T(8,128)}, f32[384,1536]{1,0:T(8,128)}, f32[384,512]{1,0:T(8,128)}, f32[384,512]{1,0:T(8,128)}, /*ind...) custom-call(bf16[8,384,1664]{2,1,0:T(8,128)(2,1)} %get-tuple-element, ...), custom_call_target="tpu_custom_call" | custom-call | tf_op jit(solution)/shard_map/place/pallas_call | solution.py:1451
  (1 shorter events, 0.0 us)
